TPU v7x, 32 devices: a whole 2x2x4 slice. The times are simulated.
32 devices in a mesh: dp: 16 (over z, y, core), seq: 2 (over x).
Axes of the slice: x: 2, y: 2, z: 4, core: 2. Of those that a mesh axis runs over, the one named last changes fastest.
Arguments:
- x_in: bfloat16 [2, 16, 1024, 768], P(None, 'dp', 'seq'), may hold values from -6 to 6
- grad_out: bfloat16 [2, 16, 1024, 768], P(None, 'dp', 'seq'), may hold values from -6 to 6
- norm_gain: bfloat16 [768], P(('dp', 'seq')), may hold values from 0.099609375 to 1.8984375
- in_weight: bfloat16 [768, 3352], P(('dp', 'seq')), may hold values from -0.21875 to 0.21875
- conv_weight: bfloat16 [4, 1792], P(None, ('dp', 'seq')), may hold values from -3 to 3
- conv_bias: bfloat16 [1792], P(('dp', 'seq')), may hold values from -3 to 3
- gate_gain: bfloat16 [1536], P(('dp', 'seq')), may hold values from 0.099609375 to 1.8984375
- out_weight: bfloat16 [1536, 768], P(('dp', 'seq')), may hold values from -0.15625 to 0.15625
- dt_bias: float32 [24], replicated, may hold values from -4.5 to -2
- a_log: float32 [24], replicated, may hold values from -7.5 to 0
- skip: float32 [24], replicated, may hold values from 0.5 to 2
Outputs:
- y_out: bfloat16 [2, 16, 1024, 768], P(None, 'dp', 'seq')
- dx_in: bfloat16 [2, 16, 1024, 768], P(None, 'dp', 'seq')
- grad_norm_gain: float32 [768], P(('dp', 'seq'))
- grad_in_weight: float32 [768, 3352], P(('dp', 'seq'))
- grad_conv_weight: float32 [4, 1792], P(None, ('dp', 'seq'))
- grad_conv_bias: float32 [1792], P(('dp', 'seq'))
- grad_gate_gain: float32 [1536], P(('dp', 'seq'))
- grad_out_weight: float32 [1536, 768], P(('dp', 'seq'))
- grad_dt_bias: float32 [24], replicated
- grad_a_log: float32 [24], replicated
- grad_skip: float32 [24], replicated
All inputs are finite; a program needn't handle non-finite values.
Results may differ from a plain program's by a relative error of at most 0.012.
The roundings to bfloat16 on the way count: a program that leaves them out, or rounds other values in their place, can miss the bound.
Values may be sent and summed in bfloat16 or wider, within the bound.
No kernel may reach another device: no remote copies, remote signals or barrier semaphores. Data moves between devices by JAX's collectives and lax.ppermute only.
A program may use at most 192 MiB of HBM per device.

v0:
```python
import jax
import jax.numpy as jnp
from jax import lax
from jax.sharding import PartitionSpec as P

HEADS = 24
HEADDIM = 64
STATE = 128
KCONV = 4
GROUP = 256
INNER = 1536
CONVW = 1792


EPS = 1e-05


def shifted(array, axis, by):
    devices = lax.axis_size(axis)
    pairs = [(i, i + by) for i in range(devices) if 0 <= i + by < devices]
    return lax.ppermute(array, axis, pairs)


def prefix(array, axis, join, neutral, backward):
    count = lax.axis_size(axis)
    place = lax.axis_index(axis)
    ahead = count - 1 - place if backward else place
    gathered = jax.tree.map(
        lambda a, kind: lax.all_gather(a.astype(kind), axis), array, (jnp.bfloat16, jnp.bfloat16)
    )
    state = jax.tree.map(lambda a, e: jnp.zeros_like(a) + jnp.asarray(e, a.dtype), array, neutral)

    def one(hop, state):
        source = count - 1 - hop if backward else hop
        return join(
            state,
            jax.tree.map(
                lambda a, own: lax.dynamic_index_in_dim(a, source, 0, False).astype(own.dtype),
                gathered,
                array,
            ),
        )

    return lax.fori_loop(0, ahead, one, state)


def tdot(left, right):
    return lax.dot_general(
        left, right, (((0,), (0,)), ((), ())), preferred_element_type=jnp.float32
    )


def ndot(left, right):
    return lax.dot_general(
        left, right, (((1,), (1,)), ((), ())), preferred_element_type=jnp.float32
    )


def dsilu(value):
    sig = jax.nn.sigmoid(value)
    return sig * (1.0 + value * (1.0 - sig))


def merge_states(earlier, later):
    return (earlier[0] * later[0], earlier[1] * later[0][:, None, None] + later[1])


def decay_table(cum_t):
    size = cum_t.shape[-1]
    rows = lax.broadcasted_iota(jnp.int32, (size, size), 0)
    cols = lax.broadcasted_iota(jnp.int32, (size, size), 1)
    lower = rows >= cols
    diff = cum_t[:, :, :, None] - cum_t[:, :, None, :]
    return jnp.exp(jnp.where(lower, diff, 0.0)) * lower.astype(jnp.float32)


def forward(xb, wts, dt_bias, rate, skip):
    gain_in, w_in, w_conv, b_conv, gain_gate, w_out = wts
    length = xb.shape[0]
    count = length // GROUP
    xf = xb.astype(jnp.float32)
    r_in = lax.rsqrt(jnp.mean(xf * xf, -1, keepdims=True) + EPS)
    normed = (xf * r_in * gain_in.astype(jnp.float32)).astype(jnp.bfloat16)
    proj = jnp.dot(normed, w_in, preferred_element_type=jnp.float32).astype(jnp.bfloat16)
    conv_in = proj[:, INNER : INNER + CONVW]
    rim = shifted(conv_in[length - KCONV + 1 :], "seq", 1)
    padded = jnp.concatenate([rim, conv_in], 0).astype(jnp.float32)
    taps = w_conv.astype(jnp.float32)
    conv_out = b_conv.astype(jnp.float32) + jnp.zeros((length, CONVW), jnp.float32)
    for tap in range(KCONV):
        conv_out = conv_out + taps[tap] * padded[tap : tap + length]
    mixed = jax.nn.silu(conv_out).astype(jnp.bfloat16)
    xh = mixed[:, :INNER].reshape(count, GROUP, HEADS, HEADDIM)
    bm = mixed[:, INNER : INNER + STATE].reshape(count, GROUP, STATE)
    cm = mixed[:, INNER + STATE :].reshape(count, GROUP, STATE)
    dt_raw = proj[:, INNER + CONVW :].astype(jnp.float32)
    step = jax.nn.softplus(dt_raw + dt_bias)
    step_t = step.reshape(count, GROUP, HEADS).transpose(0, 2, 1)
    cum_t = jnp.cumsum(step_t * rate[None, :, None], -1)
    decay = decay_table(cum_t)
    cbm = jnp.einsum("ctn,csn->cts", cm, bm, preferred_element_type=jnp.float32)
    weights = (cbm[:, None] * decay * step_t[:, :, None, :]).astype(jnp.bfloat16)
    inside = jnp.einsum("chts,cshp->cthp", weights, xh, preferred_element_type=jnp.float32)
    last = cum_t[:, :, -1]
    block_decay = jnp.exp(last)
    scale = (jnp.exp(last[:, :, None] - cum_t) * step_t).transpose(0, 2, 1)
    x_scaled = (xh.astype(jnp.float32) * scale[..., None]).astype(jnp.bfloat16)
    local = jnp.einsum("cshp,csn->chpn", x_scaled, bm, preferred_element_type=jnp.float32)
    total_decay = jnp.ones((HEADS,), jnp.float32)
    total_state = jnp.zeros((HEADS, HEADDIM, STATE), jnp.float32)
    for block in range(count):
        total_state = total_state * block_decay[block][:, None, None] + local[block]
        total_decay = total_decay * block_decay[block]
    identity = (jnp.ones((HEADS,), jnp.float32), jnp.zeros((HEADS, HEADDIM, STATE), jnp.float32))
    _, incoming = prefix((total_decay, total_state), "seq", merge_states, identity, False)
    entering = []
    running = incoming
    for block in range(count):
        entering.append(running)
        running = running * block_decay[block][:, None, None] + local[block]
    state_in = jnp.stack(entering)
    state_low = state_in.astype(jnp.bfloat16)
    exp_cum = jnp.exp(cum_t).transpose(0, 2, 1)
    carried = exp_cum[..., None] * jnp.einsum(
        "ctn,chpn->cthp", cm, state_low, preferred_element_type=jnp.float32
    )
    ssd = (inside + carried + skip[None, None, :, None] * xh.astype(jnp.float32)).reshape(
        length, INNER
    )
    zsig = jax.nn.silu(proj[:, :INNER].astype(jnp.float32))
    gated = ssd * zsig
    r_gate = lax.rsqrt(jnp.mean(gated * gated, -1, keepdims=True) + EPS)
    gnorm = (gated * r_gate * gain_gate.astype(jnp.float32)).astype(jnp.bfloat16)
    result = (xf + jnp.dot(gnorm, w_out, preferred_element_type=jnp.float32)).astype(jnp.bfloat16)
    saved = (
        xf,
        r_in,
        normed,
        proj,
        padded,
        conv_out,
        mixed,
        step_t,
        cum_t,
        state_in,
        state_low,
        carried,
        ssd,
        zsig,
        gated,
        r_gate,
        gnorm,
    )
    return (result, saved)


def backward(saved, cot, wts, dt_bias, rate, skip):
    gain_in, w_in, w_conv, b_conv, gain_gate, w_out = wts
    (
        xf,
        r_in,
        normed,
        proj,
        padded,
        conv_out,
        mixed,
        step_t,
        cum_t,
        state_in,
        state_low,
        carried,
        ssd,
        zsig,
        gated,
        r_gate,
        gnorm,
    ) = saved
    length = xf.shape[0]
    count = length // GROUP
    grad_wout = tdot(gnorm, cot)
    dgnorm = ndot(cot, w_out)
    scaled_g = gain_gate.astype(jnp.float32) * dgnorm
    grad_ggain = jnp.sum(dgnorm * gated * r_gate, 0)
    dgated = r_gate * scaled_g - gated * r_gate**3 * jnp.mean(scaled_g * gated, -1, keepdims=True)
    dssd = (dgated * zsig).astype(jnp.bfloat16)
    zpart = proj[:, :INNER].astype(jnp.float32)
    dzpart = dgated * ssd * dsilu(zpart)
    xh = mixed[:, :INNER].reshape(count, GROUP, HEADS, HEADDIM)
    bm = mixed[:, INNER : INNER + STATE].reshape(count, GROUP, STATE)
    cm = mixed[:, INNER + STATE :].reshape(count, GROUP, STATE)
    xhf = xh.astype(jnp.float32)
    dyr = dssd.reshape(count, GROUP, HEADS, HEADDIM)
    dyf = dyr.astype(jnp.float32)
    decay = decay_table(cum_t)
    cbm = jnp.einsum("ctn,csn->cts", cm, bm, preferred_element_type=jnp.float32)
    full = cbm[:, None] * decay * step_t[:, :, None, :]
    weights = full.astype(jnp.bfloat16)
    grad_skip = jnp.sum(dyf * xhf, (0, 1, 3))
    dxh = skip[None, None, :, None] * dyf
    dweights = jnp.einsum("cthp,cshp->chts", dyr, xh, preferred_element_type=jnp.float32)
    dxh = dxh + jnp.einsum("chts,cthp->cshp", weights, dyr, preferred_element_type=jnp.float32)
    dcbm = jnp.sum(dweights * decay * step_t[:, :, None, :], 1).astype(jnp.bfloat16)
    dstep = jnp.sum(dweights * cbm[:, None] * decay, 2)
    product = dweights * full
    dcum = jnp.sum(product, 3) - jnp.sum(product, 2)
    dcum = dcum + jnp.sum(dyf * carried, -1).transpose(0, 2, 1)
    exp_cum = jnp.exp(cum_t).transpose(0, 2, 1)
    dcarry = (dyf * exp_cum[..., None]).astype(jnp.bfloat16)
    dcm = jnp.einsum("cthp,chpn->ctn", dcarry, state_low, preferred_element_type=jnp.float32)
    dstate_low = jnp.einsum("cthp,ctn->chpn", dcarry, cm, preferred_element_type=jnp.float32)
    last = cum_t[:, :, -1]
    block_decay = jnp.exp(last)
    total_decay = jnp.ones((HEADS,), jnp.float32)
    running = jnp.zeros((HEADS, HEADDIM, STATE), jnp.float32)
    for block in reversed(range(count)):
        running = running * block_decay[block][:, None, None] + dstate_low[block]
        total_decay = total_decay * block_decay[block]
    identity = (jnp.ones((HEADS,), jnp.float32), jnp.zeros((HEADS, HEADDIM, STATE), jnp.float32))
    _, later = prefix((total_decay, running), "seq", merge_states, identity, True)
    leaving = [later] * count
    running = later
    for block in reversed(range(count)):
        leaving[block] = running
        running = running * block_decay[block][:, None, None] + dstate_low[block]
    grad_state = jnp.stack(leaving)
    dlast = block_decay * jnp.sum(grad_state * state_in, (2, 3))
    scale_t = jnp.exp(last[:, :, None] - cum_t) * step_t
    scale = scale_t.transpose(0, 2, 1)
    x_scaled = (xhf * scale[..., None]).astype(jnp.bfloat16)
    grad_low = grad_state.astype(jnp.bfloat16)
    dxs = jnp.einsum("csn,chpn->cshp", bm, grad_low, preferred_element_type=jnp.float32)
    dbm = jnp.einsum("cshp,chpn->csn", x_scaled, grad_low, preferred_element_type=jnp.float32)
    dxh = dxh + dxs * scale[..., None]
    dscale = jnp.sum(dxs * xhf, -1).transpose(0, 2, 1)
    dstep = dstep + dscale * jnp.exp(last[:, :, None] - cum_t)
    dlast = dlast + jnp.sum(dscale * scale_t, -1)
    dcum = dcum - dscale * scale_t
    final = (lax.broadcasted_iota(jnp.int32, (GROUP,), 0) == GROUP - 1).astype(jnp.float32)
    dcum = dcum + dlast[:, :, None] * final
    dlog = jnp.flip(jnp.cumsum(jnp.flip(dcum, -1), -1), -1)
    dstep = dstep + dlog * rate[None, :, None]
    grad_alog = jnp.sum(dlog * step_t, (0, 2)) * rate
    dcm = dcm + jnp.einsum("cts,csn->ctn", dcbm, bm, preferred_element_type=jnp.float32)
    dbm = dbm + jnp.einsum("cts,ctn->csn", dcbm, cm, preferred_element_type=jnp.float32)
    dmixed = jnp.concatenate(
        [dxh.reshape(length, INNER), dbm.reshape(length, STATE), dcm.reshape(length, STATE)], -1
    )
    dmixed = dmixed.astype(jnp.bfloat16).astype(jnp.float32)
    dconv = dmixed * dsilu(conv_out)
    grad_cbias = jnp.sum(dconv, 0)
    grad_cweight = jnp.stack(
        [jnp.sum(dconv * padded[tap : tap + length], 0) for tap in range(KCONV)]
    )
    rim_back = shifted(dconv[: KCONV - 1], "seq", -1)
    extended = jnp.concatenate([dconv, rim_back], 0)
    taps = w_conv.astype(jnp.float32)
    dconv_in = jnp.zeros((length, CONVW), jnp.float32)
    for tap in range(KCONV):
        dconv_in = dconv_in + taps[tap] * extended[KCONV - 1 - tap : KCONV - 1 - tap + length]
    dt_raw = proj[:, INNER + CONVW :].astype(jnp.float32)
    ddt_raw = dstep.transpose(0, 2, 1).reshape(length, HEADS) * jax.nn.sigmoid(dt_raw + dt_bias)
    grad_dtb = jnp.sum(ddt_raw, 0)
    dproj = jnp.concatenate([dzpart, dconv_in, ddt_raw], -1).astype(jnp.bfloat16)
    grad_win = tdot(normed, dproj)
    dnormed = ndot(dproj, w_in)
    scaled_in = gain_in.astype(jnp.float32) * dnormed
    grad_gin = jnp.sum(dnormed * xf * r_in, 0)
    dx_in = (
        r_in * scaled_in
        - xf * r_in**3 * jnp.mean(scaled_in * xf, -1, keepdims=True)
        + cot.astype(jnp.float32)
    )
    head_terms = jnp.stack([grad_dtb, grad_alog, grad_skip]).reshape(1, 3 * HEADS)
    return (
        dx_in.astype(jnp.bfloat16),
        (grad_gin, grad_win, grad_cweight, grad_cbias, grad_ggain, grad_wout, head_terms),
    )


def shards(
    x_in,
    grad_out,
    norm_gain,
    in_weight,
    conv_weight,
    conv_bias,
    gate_gain,
    out_weight,
    dt_bias,
    a_log,
    skip,
):
    micro = x_in.shape[0]
    rate = -jnp.exp(a_log)
    devices = lax.axis_size(("dp", "seq"))
    results = []
    saves = []
    for index in range(micro):
        wts = (
            lax.all_gather(norm_gain, ("dp", "seq"), axis=0, tiled=True),
            lax.all_gather(in_weight, ("dp", "seq"), axis=0, tiled=True),
            lax.all_gather(conv_weight, ("dp", "seq"), axis=1, tiled=True),
            lax.all_gather(conv_bias, ("dp", "seq"), axis=0, tiled=True),
            lax.all_gather(gate_gain, ("dp", "seq"), axis=0, tiled=True),
            lax.all_gather(out_weight, ("dp", "seq"), axis=0, tiled=True),
        )
        result, saved = forward(x_in[index, 0], wts, dt_bias, rate, skip)
        results.append(result)
        saves.append(saved)
    dx_list = [None] * micro
    summed = None
    for index in reversed(range(micro)):
        wts = (
            lax.all_gather(norm_gain, ("dp", "seq"), axis=0, tiled=True),
            lax.all_gather(in_weight, ("dp", "seq"), axis=0, tiled=True),
            lax.all_gather(conv_weight, ("dp", "seq"), axis=1, tiled=True),
            lax.all_gather(conv_bias, ("dp", "seq"), axis=0, tiled=True),
            lax.all_gather(gate_gain, ("dp", "seq"), axis=0, tiled=True),
            lax.all_gather(out_weight, ("dp", "seq"), axis=0, tiled=True),
        )
        dx_part, terms = backward(saves[index], grad_out[index, 0], wts, dt_bias, rate, skip)
        dx_list[index] = dx_part
        summed = terms if summed is None else jax.tree.map(lambda a, b: a + b, summed, terms)
    spread = summed[:6] + (jnp.broadcast_to(summed[6], (devices, 3 * HEADS)),)
    summed = (
        lax.psum_scatter(spread[0], ("dp", "seq"), scatter_dimension=0, tiled=True),
        lax.psum_scatter(spread[1], ("dp", "seq"), scatter_dimension=0, tiled=True),
        lax.psum_scatter(spread[2], ("dp", "seq"), scatter_dimension=1, tiled=True),
        lax.psum_scatter(spread[3], ("dp", "seq"), scatter_dimension=0, tiled=True),
        lax.psum_scatter(spread[4], ("dp", "seq"), scatter_dimension=0, tiled=True),
        lax.psum_scatter(spread[5], ("dp", "seq"), scatter_dimension=0, tiled=True),
        lax.psum_scatter(spread[6], ("dp", "seq"), scatter_dimension=0, tiled=True),
    )
    heads_sum = summed[6].reshape(3, HEADS)
    y_out = jnp.stack(results)[:, None]
    dx_in = jnp.stack(dx_list)[:, None]
    return (
        y_out,
        dx_in,
        summed[0],
        summed[1],
        summed[2],
        summed[3],
        summed[4],
        summed[5],
        heads_sum[0],
        heads_sum[1],
        heads_sum[2],
    )


def solution(mesh):
    return jax.shard_map(
        shards,
        mesh=mesh,
        in_specs=(
            P(None, "dp", "seq", None),
            P(None, "dp", "seq", None),
            P(("dp", "seq")),
            P(("dp", "seq"), None),
            P(None, ("dp", "seq")),
            P(("dp", "seq")),
            P(("dp", "seq")),
            P(("dp", "seq"), None),
            P(),
            P(),
            P(),
        ),
        out_specs=(
            P(None, "dp", "seq", None),
            P(None, "dp", "seq", None),
            P(("dp", "seq")),
            P(("dp", "seq"), None),
            P(None, ("dp", "seq")),
            P(("dp", "seq")),
            P(("dp", "seq")),
            P(("dp", "seq"), None),
            P(),
            P(),
            P(),
        ),
        check_vma=False,
    )
```

profile of v0, /device:TPU:8, one launch (start us, length us, event | category | flops | bytes accessed | tf_op | source)
XLA Modules:
  0.0 704.7 jit_solution(8700887190203744016)
XLA Ops:
  11.3 41.1 %all-reduce.10 = (bf16[768]{0:T(1024)(128)(2,1)S(1)}, bf16[1792]{0:T(1024)(128)(2,1)S(1)}, bf16[1536]{0:T(1024)(128)(2,1)S(1)}) all-reduce(bf16[768]{0:T(1024)(128)(2,1)S(1)} %dynamic-update-slice.1, bf16[1792]{0:T(1024)(128)(2,1)S(1)} %dynamic-update-slice, ...), channel_id=1, replica_groups=mesh['dp'=16,'seq'=2] {'dp','seq'}, use_global_device_ids=true, to_apply=%add.1 | all-reduce | flops 4096 | bytes 16384
  52.3 53.5 %all-gather = bf16[32,56,4]{1,2,0:T(4,128)(2,1)S(1)} all-gather(bf16[1,56,4]{1,2,0:T(4,128)(2,1)} %bitcast.505), channel_id=1, replica_groups=mesh['dp'=16,'seq'=2] {'dp','seq'}, dimensions={0}, use_global_device_ids=true | all-gather | bytes 14784 | tf_op jit(solution)/shard_map/all_gather | solution.py:302
  110.5 5.1 fusion.168
  115.6 21.9 %all-gather.6.cloned.1.call-done = bf16[768,3352]{1,0:T(8,128)(2,1)} async-done(((bf16[24,3352]{1,0:T(8,128)(2,1)}), bf16[768,3352]{1,0:T(8,128)(2,1)}) %all-gather.6.cloned.1.call-update) | async-done | bytes 5148688 | tf_op jit(solution)/shard_map/all_gather | solution.py:301
  137.5 7.2 %convolution_convert_fusion.1 = bf16[512,3352]{0,1:T(8,128)(2,1)S(1)} fusion(bf16[768,3352]{1,0:T(8,128)(2,1)} %all-gather.6.cloned.1.call-done, f32[768]{0:T(1024)S(1)} %convert_element_type.318, f32[512]{0:T(512)S(1)} %get-tuple-element.503, bf16[2,1,512,768]{3,2,1,0:T(8,128)(2,1)S(1)} %copy-done.33), kind=kOutput, calls=%fused_computation.30 | convolution fusion | flops 2639409152 | bytes 9373696 | tf_op jit(solution)/shard_map/dot_general | solution.py:84
  144.9 4.6 convolution_convert_fusion
  160.5 6.6 all-gather.1
  170.5 4.4 collective-permute-start.1
  174.9 9.3 %all-gather.2 = bf16[2,1,24]{2,1,0:T(2,128)(2,1)S(1)} all-gather(bf16[1,1,24]{2,1,0:T(2,128)(2,1)S(1)} %get-tuple-element.485), channel_id=1, replica_groups=mesh['dp'=16,'seq'=2] {'seq'}, dimensions={0}, use_global_device_ids=true | all-gather | bytes 144 | tf_op jit(solution)/shard_map/all_gather | solution.py:29
  187.5 8.8 %multiply_convert_fusion.1 = (bf16[512,1792]{0,1:T(8,128)(2,1)S(1)}, f32[512,1792]{0,1:T(8,128)}, bf16[512,1792]{0,1:T(8,128)(2,1)S(1)}, f32[512,1792]{0,1:T(8,128)}) fusion(f32[515,1792]{0,1:T(8,128)S(1)} %maximum_convert_fusion, f32[1792]{0:T(1024)S(1)} %get-tuple-element.372, f32[1792]{0:T(1024)S(1)} %get-tuple-element.373, ...), kind=kLoop, calls=%fused_computation.91 | loop fusion | flops 23855104 | bytes 40406016 | tf_op jit(solution)/shard_map/convert_element_type | solution.py:92
  205.1 10.9 %all_gather.33 = bf16[2,24,64,128]{3,2,1,0:T(8,128)(2,1)S(1)} all-gather(bf16[1,24,64,128]{3,2,1,0:T(8,128)(2,1)S(1)} %fusion.159), channel_id=1, replica_groups=mesh['dp'=16,'seq'=2] {'seq'}, dimensions={0}, use_global_device_ids=true | all-gather | bytes 1179648 | tf_op jit(solution)/shard_map/all_gather | solution.py:29
  221.8 4.2 fusion.45
  245.0 9.6 %all_gather.29 = bf16[2,24,64,128]{3,2,1,0:T(8,128)(2,1)} all-gather(bf16[1,24,64,128]{3,2,1,0:T(8,128)(2,1)S(1)} %fusion.160), channel_id=1, replica_groups=mesh['dp'=16,'seq'=2] {'seq'}, dimensions={0}, use_global_device_ids=true | all-gather | bytes 1179648 | tf_op jit(solution)/shard_map/all_gather | solution.py:29
  255.6 7.9 %while.52 = (s32[]{:T(128)}, f32[24,64,128]{2,1,0:T(8,128)}, s32[]{:T(128)}, bf16[2,24]{1,0:T(2,128)(2,1)S(1)}, bf16[2,24,64,128]{3,2,1,0:T(8,128)(2,1)}, /*index=5*/s32[]{:T(128)}, s32[]{:T(128)}, s32[]{:T(128)}) while((s32[]{:T(128)}, f32[24,64,128]{2,1,0:T(8,128)}, s32[]{:T(128)}, bf16[2,24]{1,0:T(2,128)(2,1)S(1)}, ...), condition=%wide.region_4.5_spmd, body=%wide.region_3.4_spmd.sunk | while | flops 589853 | bytes 1966455 | solution.py:44
  269.1 4.2 fusion.35
  285.9 7.7 %multiply_reduce_fusion.13 = (f32[1536]{0:T(1024)}, bf16[512,1536]{0,1:T(8,128)(2,1)}, bf16[512,1536]{0,1:T(8,128)(2,1)}, bf16[512,1536]{0,1:T(8,128)(2,1)}, f32[1536]{0:T(1024)}, /*index=5*/bf16[512,1536]{0,1:T(8,128)(2,1)}) fusion(bf16[512,1792]{0,1:T(8,128)(2,1)S(1)} %copy-done.19, bf16[512,3352]{0,1:T(8,128)(2,1)S(1)} %copy-done.42, ...), kind=kLoop, calls=%fused_computation.141 | loop fusion | flops 36172800 | bytes 31488000 | tf_op jit(solution)/shard_map/reduce_sum | solution.py:198
  297.1 3.9 fusion.58
  303.0 10.6 %all_gather.34 = bf16[2,24,64,128]{3,2,1,0:T(8,128)(2,1)} all-gather(bf16[1,24,64,128]{3,2,1,0:T(8,128)(2,1)S(1)} %fusion.158), channel_id=1, replica_groups=mesh['dp'=16,'seq'=2] {'seq'}, dimensions={0}, use_global_device_ids=true | all-gather | bytes 1179648 | tf_op jit(solution)/shard_map/all_gather | solution.py:29
  326.7 8.4 %fusion.138 = f32[2,24,256,256]{3,2,1,0:T(8,128)} fusion(bf16[2,256,24,64]{1,0,3,2:T(2,128)(2,1)} %reshape.380, bf16[2,256,24,64]{1,0,3,2:T(2,128)(2,1)} %copy-done.22), kind=kOutput, calls=%fused_computation.218 | convolution fusion | flops 402653184 | bytes 15728640 | tf_op jit(solution)/shard_map/cthp,cshp->chts/dot_general | solution.py:200
  337.0 8.6 %all_gather.35 = bf16[2,24,64,128]{3,2,1,0:T(8,128)(2,1)} all-gather(bf16[1,24,64,128]{3,2,1,0:T(8,128)(2,1)S(1)} %fusion.157), channel_id=1, replica_groups=mesh['dp'=16,'seq'=2] {'seq'}, dimensions={0}, use_global_device_ids=true | all-gather | bytes 1179648 | tf_op jit(solution)/shard_map/all_gather | solution.py:29
  368.7 17.0 %fusion.4 = (f32[2,24,256]{2,1,0:T(8,128)S(1)}, f32[2,24,256]{2,1,0:T(8,128)S(1)}, f32[2,24,256]{2,1,0:T(8,128)}, bf16[2,256,256]{2,1,0:T(8,128)(2,1)}, bf16[2,2...) fusion(f32[2,24,256]{2,1,0:T(8,128)S(1)} %bitcast.496, ...), kind=kOutput, calls=%fused_computation.20 | convolution fusion | flops 490397696 | bytes 18120704 | tf_op jit(solution)/shard_map/cthp,cshp->chts/dot_general | solution.py:200
  412.2 6.6 fusion.56
  420.9 7.3 %multiply_reduce_fusion.7 = (f32[1792]{0:T(1024)}, f32[1792]{0:T(1024)}, f32[1792]{0:T(1024)}, f32[1792]{0:T(1024)}, f32[1792]{0:T(1024)}, /*index=5*/f32[512,1792]{0,1:T(8,128)S(1)}) fusion(f32[515,1792]{0,1:T(8,128)S(1)} %bitcast.439, f32[512,1792]{0,1:T(8,128)S(1)} %copy-done.21, bf16[512,128]{0,1:T(8,128)(2,1)S(1)} %copy.428, ...), kind=kLoop, calls=%fused_computation.81 | loop fusion | flops 21093632 | bytes 23890944 | tf_op jit(solution)/shard_map/reduce_sum | solution.py:252
  434.9 7.2 %convolution_add_fusion.1 = f32[1536,768]{1,0:T(8,128)} fusion(f32[1536,768]{1,0:T(8,128)} %fusion.162, bf16[2,1,512,768]{3,2,1,0:T(8,128)(2,1)} %param.20, f32[512,1536]{0,1:T(8,128)} %copy-done.10, f32[1536]{0:T(1024)S(1)} %convert_element_type.332, f32[512]{0:T(512)S(1)} %get-tuple-element.473), kind=kOutput, calls=%fused_computation.57 | convolution fusion | flops 1211498496 | bytes 13377536 | tf_op jit(solution)/shard_map/dot_general | solution.py:48
  449.0 6.7 fusion.61
  457.8 7.3 %multiply_reduce_fusion.11 = (f32[1792]{0:T(1024)}, f32[1792]{0:T(1024)}, f32[1792]{0:T(1024)}, f32[1792]{0:T(1024)}, f32[1792]{0:T(1024)}, /*index=5*/f32[512,1792]{0,1:T(8,128)S(1)}) fusion(f32[515,1792]{0,1:T(8,128)S(1)} %bitcast.437, f32[512,1792]{0,1:T(8,128)S(1)} %copy-done.20, bf16[512,128]{0,1:T(8,128)(2,1)S(1)} %copy.434, ...), kind=kLoop, calls=%fused_computation.85 | loop fusion | flops 21093632 | bytes 23890944 | tf_op jit(solution)/shard_map/reduce_sum | solution.py:252
  477.1 21.0 %fusion.29 = (bf16[512,1792]{0,1:T(8,128)(2,1)S(1)}, bf16[512,1792]{0,1:T(8,128)(2,1)S(1)}) fusion(f32[512,1792]{0,1:T(8,128)} %copy-done.14, f32[3,1792]{0,1:T(8,128)} %copy.373, f32[1792]{0:T(1024)S(1)} %copy-done.113, f32[1792]{0:T(1024)S(1)} %copy-done.115, f32[1792]{0:T(1024)S(1)} %copy-done.117, f32[1792]{0:T(1024)S(1)} %copy-done.111, ...), kind=kLoop, calls=%fused_computation.71 | loop fusion | flops 20185088 | bytes 11081728 | tf_op jit(solution)/shard_map/convert.20
  501.5 8.9 %convolution_add_fusion = f32[768,3352]{1,0:T(8,128)} fusion(f32[768,3352]{1,0:T(8,128)S(1)} %fusion.94, bf16[512,24]{0,1:T(8,128)(2,1)S(1)} %get-tuple-element.424, bf16[512,1792]{0,1:T(8,128)(2,1)S(1)} %get-tuple-element.459, bf16[512,1536]{0,1:T(8,128)(2,1)} %get-tuple-element.461, f32[768]{0:T(1024)S(1)} %copy-done.91, f32[512]{0:T(512)S(1)} %copy-done.122, ...), kind=kOutput, calls=%fused_computation.24 | convolution fusion | flops 2650564608 | bytes 25139200 | tf_op jit(solution)/shard_map/dot_general | solution.py:48
  511.8 3.6 fusion.113
  523.3 4.8 fusion.93
  528.1 39.1 %all-reduce.9 = (f32[768]{0:T(1024)S(1)}, f32[4,1792]{1,0:T(4,128)S(1)}, f32[1792]{0:T(1024)S(1)}, f32[1536]{0:T(1024)S(1)}, f32[32,72]{1,0:T(8,128)S(1)}) all-reduce(f32[768]{0:T(1024)S(1)} %add.472, f32[4,1792]{1,0:T(4,128)S(1)} %maximum_add_fusion, f32[1792]{0:T(1024)S(1)} %add.475, ...), channel_id=2, replica_groups=mesh['dp'=16,'seq'=2] {'dp','seq'}, use_global_device_ids=true, to_apply=%region_42.43.clone | all-reduce | flops 13568 | bytes 108544
  574.2 123.7 %reduce-scatter.8.cloned.1.call-done = f32[24,3352]{1,0:T(8,128)} async-done(((f32[768,3352]{1,0:T(8,128)}), f32[24,3352]{1,0:T(8,128)}) %reduce-scatter.8.cloned.1.call-update) | async-done | bytes 321808
  (584 shorter events, 201.9 us)
Async XLA Ops:
  7.2 103.4 %all-gather.8.cloned.1.call-start = ((), (), s32[]{:S(2)}) async-start(), calls=%async_computation.3 | async-start | bytes 2433024 | tf_op jit(solution)/shard_map/all_gather | solution.py:305
  7.9 129.6 %all-gather.6.cloned.1.call-start = ((), (), s32[]{:S(2)}) async-start(), calls=%async_computation.2 | async-start | bytes 5474304 | tf_op jit(solution)/shard_map/all_gather | solution.py:301
  8.7 565.5 %reduce-scatter.6.cloned.1.call-start = ((), (), s32[]{:S(2)}) async-start(), calls=%async_computation.4 | async-start | bytes 4866048 | tf_op jit(solution)/shard_map/reduce_scatter | solution.py:331
  52.3 92.5 %copy-start.90 = (f32[768]{0:T(1024)}, f32[768]{0:T(1024)S(1)}, u32[]{:S(2)}) copy-start(f32[768]{0:T(1024)S(1)} %convert_element_type.318) | copy-start | bytes 9220
  106.7 80.1 %copy-start.110 = (f32[1792]{0:T(1024)}, f32[1792]{0:T(1024)S(1)}, u32[]{:S(2)}) copy-start(f32[1792]{0:T(1024)S(1)} %get-tuple-element.371) | copy-start | bytes 21508
  106.7 80.1 %copy-start.112 = (f32[1792]{0:T(1024)}, f32[1792]{0:T(1024)S(1)}, u32[]{:S(2)}) copy-start(f32[1792]{0:T(1024)S(1)} %get-tuple-element.372) | copy-start | bytes 21508
  106.7 80.1 %copy-start.114 = (f32[1792]{0:T(1024)}, f32[1792]{0:T(1024)S(1)}, u32[]{:S(2)}) copy-start(f32[1792]{0:T(1024)S(1)} %get-tuple-element.373) | copy-start | bytes 21508
  106.7 80.1 %copy-start.116 = (f32[1792]{0:T(1024)}, f32[1792]{0:T(1024)S(1)}, u32[]{:S(2)}) copy-start(f32[1792]{0:T(1024)S(1)} %get-tuple-element.374) | copy-start | bytes 21508
  109.9 41.4 %copy-start.150 = (f32[24]{0:T(128)}, f32[24]{0:T(128)S(1)}, u32[]{:S(2)}) copy-start(f32[24]{0:T(128)S(1)} %exponential_negate_fusion) | copy-start | bytes 292
  110.5 27.0 %copy-start.121 = (f32[512]{0:T(512)}, f32[512]{0:T(512)S(1)}, u32[]{:S(2)}) copy-start(f32[512]{0:T(512)S(1)} %get-tuple-element.503) | copy-start | bytes 6148
  110.5 34.4 %copy-start.147 = (f32[512]{0:T(512)}, f32[512]{0:T(512)S(1)}, u32[]{:S(2)}) copy-start(f32[512]{0:T(512)S(1)} %get-tuple-element.469) | copy-start | bytes 6148
  110.5 27.0 %copy-start.33 = (bf16[2,1,512,768]{3,2,1,0:T(8,128)(2,1)S(1)}, bf16[2,1,512,768]{3,2,1,0:T(8,128)(2,1)}, u32[]{:S(2)}) copy-start(bf16[2,1,512,768]{3,2,1,0:T(8,128)(2,1)} %param.19) | copy-start | bytes 4718596
  153.0 51.9 %copy-start.151 = (f32[24]{0:T(128)}, f32[24]{0:T(128)S(1)}, u32[]{:S(2)}) copy-start(f32[24]{0:T(128)S(1)} %get-tuple-element.484) | copy-start | bytes 292
  153.0 63.1 %copy-start.152 = (f32[24]{0:T(128)}, f32[24]{0:T(128)S(1)}, u32[]{:S(2)}) copy-start(f32[24]{0:T(128)S(1)} %get-tuple-element.483) | copy-start | bytes 292
  153.6 30.7 %collective-permute-start = (bf16[3,1792]{0,1:T(8,128)(2,1)S(1)}, bf16[3,1792]{0,1:T(8,128)(2,1)S(1)}, u32[]{:S(2)}, u32[]{:S(2)}) collective-permute-start(bf16[3,1792]{0,1:T(8,128)(2,1)S(1)} %slice.310), channel_id=1, source_target_pairs={{0,1},{2,3},{4,5},{6,7},{8,9},{10,11},{12,13},{14,15},{16,17},{18,... | collective-permute-start | bytes 32264 | tf_op jit(solution)/shard_map/ppermute | solution.py:21
  157.6 46.7 %copy-start.84 = (f32[2,24,256]{2,1,0:T(8,128)}, f32[2,24,256]{2,1,0:T(8,128)S(1)}, u32[]{:S(2)}) copy-start(f32[2,24,256]{2,1,0:T(8,128)S(1)} %get-tuple-element.456) | copy-start | bytes 147460
  159.3 84.4 %copy-start.154 = (f32[24]{0:T(128)}, f32[24]{0:T(128)S(1)}, u32[]{:S(2)}) copy-start(f32[24]{0:T(128)S(1)} %get-tuple-element.481) | copy-start | bytes 292
  159.3 104.3 %copy-start.156 = (f32[24]{0:T(128)}, f32[24]{0:T(128)S(1)}, u32[]{:S(2)}) copy-start(f32[24]{0:T(128)S(1)} %get-tuple-element.480) | copy-start | bytes 292
  160.0 81.7 %copy-start.87 = (f32[2,24,256]{2,1,0:T(8,128)}, f32[2,24,256]{2,1,0:T(8,128)S(1)}, u32[]{:S(2)}) copy-start(f32[2,24,256]{2,1,0:T(8,128)S(1)} %get-tuple-element.454) | copy-start | bytes 147460
  170.5 14.8 %collective-permute-start.1 = (bf16[3,1792]{0,1:T(8,128)(2,1)S(1)}, bf16[3,1792]{0,1:T(8,128)(2,1)S(1)}, u32[]{:S(2)}, u32[]{:S(2)}) collective-permute-start(bf16[3,1792]{0,1:T(8,128)(2,1)S(1)} %slice.329), channel_id=1, source_target_pairs={{0,1},{2,3},{4,5},{6,7},{8,9},{10,11},{12,13},{14,15},{16,17},{18,... | collective-permute-start | bytes 32264 | tf_op jit(solution)/shard_map/ppermute | solution.py:21
  355.0 31.0 %copy-start.73 = (f32[2,256,24]{1,2,0:T(8,128)}, f32[2,256,24]{1,2,0:T(8,128)S(1)}, u32[]{:S(2)}) copy-start(f32[2,256,24]{1,2,0:T(8,128)S(1)} %get-tuple-element.500) | copy-start | bytes 147460
  433.2 38.6 %collective-permute-start.2 = (f32[3,1792]{1,0:T(4,128)}, f32[3,1792]{1,0:T(4,128)}, u32[]{:S(2)}, u32[]{:S(2)}) collective-permute-start(f32[3,1792]{1,0:T(4,128)} %copy.372), channel_id=1, source_target_pairs={{1,0},{3,2},{5,4},{7,6},{9,8},{11,10},{13,12},{15,14},{17,16},{19,... | collective-permute-start | bytes 64520 | tf_op jit(solution)/shard_map/ppermute | solution.py:21
  442.1 255.8 %reduce-scatter.8.cloned.1.call-start = ((), (), s32[]{:S(2)}) async-start(), calls=%async_computation.5 | async-start | bytes 10948608
  469.4 6.4 collective-permute-start.3
  477.1 21.0 %copy-start.34 = (bf16[2,1,512,768]{3,2,1,0:T(8,128)(2,1)S(1)}, bf16[2,1,512,768]{3,2,1,0:T(8,128)(2,1)}, u32[]{:S(2)}) copy-start(bf16[2,1,512,768]{3,2,1,0:T(8,128)(2,1)} %param.19) | copy-start | bytes 4718596
  477.1 21.0 %copy-start.66 = (bf16[512,1536]{0,1:T(8,128)(2,1)S(1)}, bf16[512,1536]{0,1:T(8,128)(2,1)}, u32[]{:S(2)}) copy-start(bf16[512,1536]{0,1:T(8,128)(2,1)} %get-tuple-element.442) | copy-start | bytes 4718596
  477.1 21.0 %copy-start.91 = (f32[768]{0:T(1024)S(1)}, f32[768]{0:T(1024)}, u32[]{:S(2)}) copy-start(f32[768]{0:T(1024)} %copy-done.90) | copy-start | bytes 9220
  477.1 21.0 %copy-start.148 = (f32[512]{0:T(512)S(1)}, f32[512]{0:T(512)}, u32[]{:S(2)}) copy-start(f32[512]{0:T(512)} %copy-done.147) | copy-start | bytes 6148
  523.3 46.4 %copy-start.32 = (bf16[2,1,512,768]{3,2,1,0:T(8,128)(2,1)S(1)}, bf16[2,1,512,768]{3,2,1,0:T(8,128)(2,1)}, u32[]{:S(2)}) copy-start(bf16[2,1,512,768]{3,2,1,0:T(8,128)(2,1)} %param.20) | copy-start | bytes 4718596
  523.3 46.4 %copy-start.36 = (bf16[2,1,512,768]{3,2,1,0:T(8,128)(2,1)S(1)}, bf16[2,1,512,768]{3,2,1,0:T(8,128)(2,1)}, u32[]{:S(2)}) copy-start(bf16[2,1,512,768]{3,2,1,0:T(8,128)(2,1)} %param.19) | copy-start | bytes 4718596
  523.3 46.4 %copy-start.146 = (f32[512]{0:T(512)S(1)}, f32[512]{0:T(512)}, u32[]{:S(2)}) copy-start(f32[512]{0:T(512)} %get-tuple-element.468) | copy-start | bytes 6148
  523.3 46.4 %copy-start.149 = (f32[512]{0:T(512)S(1)}, f32[512]{0:T(512)}, u32[]{:S(2)}) copy-start(f32[512]{0:T(512)} %get-tuple-element.504) | copy-start | bytes 6148
  (159 other events, 754.9 us)
Sparse Core Ops, SparseCore 0:
  10.9 57.6 all-gather.7
  71.5 65.8 all-gather.5
  442.3 107.1 reduce-scatter.5
  557.0 140.8 reduce-scatter.7
where the time goes:
time: 712 us; the launch traced here: 705 us
  blocking collectives  189 us (27%)
  waiting for transfers between devices  149 us (21%)
  matrix products  132 us (19%)
  other arithmetic  102 us (14%)
  local copies, waits for them, and re-layouts  97.5 us (14%)
  between operations  16.3 us (2%)
  starting transfers between devices  10.9 us (2%)
  loops' own time  7.96 us (1%)
    unnamed x5, waiting for transfers between devices  125 us
    unnamed x2, blocking collectives  80.2 us
    all_gather x6, blocking collectives, prefix(): lax.all_gather(a.astype(kind), axis)  55.5 us
    all_gather x1, blocking collectives, shards(): lax.all_gather(conv_weight, ('dp', 'seq'), axis=1, tiled=True)  53.5 us
    unnamed x381, local copies, waits for them, and re-layouts  37.1 us
    another operation x13, other arithmetic  30.8 us
    dot_general x2, matrix products, backward(): jnp.einsum('cthp,cshp->chts', dyr, xh, preferred_element_type=jnp.float32)  25.5 us
    dot_general x4, matrix products, tdot(): lax.dot_general(left, right, (((0,), (0,)), ((), ())), preferred_element_...  23 us
  transfers between devices with their start and end apart: 8, of which 3 were waited for; matrix products, arithmetic and copies ran while one was open for 16% of the time, Pallas kernels for 0%

commit v1 on v0

--- a/solution.py
+++ b/solution.py
@@ -1,6 +1,8 @@
 import jax
 import jax.numpy as jnp
 from jax import lax
+from jax.experimental import pallas as pl
+from jax.experimental.pallas import tpu as pltpu
 from jax.sharding import PartitionSpec as P
 
 HEADS = 24
@@ -277,7 +279,574 @@
     )
 
 
+PAIR = 2 * HEADDIM
+WIDE = 768
+TAIL = 384
+LOW = -1e30
+
+
+def silu_parts(value):
+    sig = 0.5 * jnp.tanh(0.5 * value) + 0.5
+    return (sig, value * sig)
+
+
+def split_dot(value, right):
+    top = value.astype(jnp.bfloat16)
+    rest = (value - top.astype(jnp.float32)).astype(jnp.bfloat16)
+    return jnp.dot(top, right, preferred_element_type=jnp.float32) + jnp.dot(
+        rest, right, preferred_element_type=jnp.float32
+    )
+
+
+def exact_dot(left, value):
+    total = None
+    for _ in range(3):
+        part = value.astype(jnp.bfloat16)
+        value = value - part.astype(jnp.float32)
+        term = jnp.dot(left, part, preferred_element_type=jnp.float32)
+        total = term if total is None else total + term
+    return total
+
+
+def lower_ones(size, flipped):
+    rows = lax.broadcasted_iota(jnp.int32, (size, size), 0)
+    cols = lax.broadcasted_iota(jnp.int32, (size, size), 1)
+    return rows <= cols if flipped else rows >= cols
+
+
+def step_sizes(raw, heads_ref):
+    shifted_raw = raw.astype(jnp.float32) + heads_ref[0:1, :]
+    dt = jnp.maximum(shifted_raw, 0.0) + jnp.log1p(jnp.exp(-jnp.abs(shifted_raw)))
+    ones = lower_ones(GROUP, False).astype(jnp.float32).astype(jnp.bfloat16)
+    cum = exact_dot(ones, dt * heads_ref[1:2, :])
+    return (shifted_raw, dt, cum, cum - jnp.log(dt))
+
+
+def spread_lanes(table, head, rows):
+    return jnp.broadcast_to(table[:, head : head + 1], (rows, PAIR))
+
+
+def forward_kernel(
+    z_ref, xr_ref, bcd_ref, x_ref, go_ref, wout_ref, taps_ref, heads_ref, lanes_ref, seg_ref,
+    y_ref, gn_ref, dz_ref, dssd_ref, mixed_ref, slope_ref, state_ref, delta_ref, ggain_ref,
+    run_ref, cin_ref, cb_ref, ssd_ref, dgn_ref, high_ref, rest_ref,
+):
+    half = GROUP // 2
+
+    @pl.when(pl.program_id(0) == 0)
+    def _():
+        run_ref[...] = jnp.zeros_like(run_ref)
+        cin_ref[0:8, :] = jnp.zeros((8, CONVW), jnp.float32)
+        ggain_ref[...] = jnp.zeros_like(ggain_ref)
+
+    cin_ref[8 : 8 + GROUP, 0:INNER] = xr_ref[...].astype(jnp.float32)
+    cin_ref[8 : 8 + GROUP, INNER:CONVW] = bcd_ref[:, 0 : 2 * STATE].astype(jnp.float32)
+
+    def conv_chunk(chunk, carry):
+        at = pl.ds(pl.multiple_of(chunk * PAIR, PAIR), PAIR)
+        total = taps_ref[KCONV : KCONV + 1, at] + taps_ref[0:1, at] * cin_ref[5 : 5 + GROUP, at]
+        for tap in range(1, KCONV):
+            total = total + taps_ref[tap : tap + 1, at] * cin_ref[5 + tap : 5 + tap + GROUP, at]
+        sig, value = silu_parts(total)
+        mixed_ref[:, at] = value.astype(jnp.bfloat16)
+        slope_ref[:, at] = sig + value * (1.0 - sig)
+        return carry
+
+    lax.fori_loop(0, CONVW // PAIR, conv_chunk, 0)
+    cin_ref[0:8, :] = cin_ref[GROUP : GROUP + 8, :]
+
+    bm = mixed_ref[:, INNER : INNER + STATE]
+    cm = mixed_ref[:, INNER + STATE : CONVW]
+    bm_t = bm.astype(jnp.float32).T.astype(jnp.bfloat16)
+    cb_ref[...] = ndot(cm, bm)
+    _, _, cum, late = step_sizes(bcd_ref[:, 2 * STATE :], heads_ref)
+    late_t = late.T
+    dgn_ref[...] = ndot(go_ref[...], wout_ref[...])
+    lower = lower_ones(half, False)
+    first = lax.broadcasted_iota(jnp.int32, (1, PAIR), 1) < HEADDIM
+    for pair in range(HEADS // 2):
+        at = slice(pair * PAIR, (pair + 1) * PAIR)
+        xp = mixed_ref[:, at]
+        spread = []
+        inside = []
+        for head in (2 * pair, 2 * pair + 1):
+            here = spread_lanes(cum, head, GROUP)
+            row = late_t[head : head + 1, :]
+            near = jnp.exp(jnp.where(lower, here[:half] - row[:, :half], LOW))
+            far = jnp.exp(here[half:] - row[:, :half])
+            last = jnp.exp(jnp.where(lower, here[half:] - row[:, half:], LOW))
+            near = (cb_ref[:half, :half] * near).astype(jnp.bfloat16)
+            far = (cb_ref[half:, :half] * far).astype(jnp.bfloat16)
+            last = (cb_ref[half:, half:] * last).astype(jnp.bfloat16)
+            above = jnp.dot(near, xp[:half], preferred_element_type=jnp.float32)
+            below = jnp.dot(
+                jnp.concatenate([far, last], 1), xp, preferred_element_type=jnp.float32
+            )
+            inside.append(jnp.concatenate([above, below], 0))
+            spread.append(here)
+        both = jnp.where(first, spread[0], spread[1])
+        end = both[GROUP - 1 : GROUP, :]
+        state = run_ref[:, at]
+        carried = jnp.exp(both) * jnp.dot(
+            cm, state.astype(jnp.bfloat16), preferred_element_type=jnp.float32
+        )
+        xf = xp.astype(jnp.float32)
+        ssd_ref[:, at] = (
+            jnp.where(first, inside[0], inside[1]) + carried + lanes_ref[1:2, at] * xf
+        )
+        both_late = jnp.where(
+            first, spread_lanes(late, 2 * pair, GROUP), spread_lanes(late, 2 * pair + 1, GROUP)
+        )
+        xw = (xf * jnp.exp(end - both_late)).astype(jnp.bfloat16)
+        state_ref[:, at] = state
+        run_ref[:, at] = jnp.exp(end) * state + jnp.dot(
+            bm_t, xw, preferred_element_type=jnp.float32
+        )
+
+    def gate_rows(index, total):
+        rows = pl.ds(pl.multiple_of(index * 16, 16), 16)
+        ssd = ssd_ref[rows, :]
+        z = z_ref[rows, :].astype(jnp.float32)
+        sig, value = silu_parts(z)
+        gated = ssd * value
+        scale = lax.rsqrt(jnp.mean(gated * gated, -1, keepdims=True) + EPS)
+        unit = gated * scale
+        gain = lanes_ref[0:1, :]
+        gn_ref[rows, :] = (unit * gain).astype(jnp.bfloat16)
+        dgn = dgn_ref[rows, :]
+        total = total + dgn * unit
+        scaled = gain * dgn
+        mean = jnp.mean(scaled * unit, -1, keepdims=True)
+        dgated = scale * (scaled - unit * mean)
+        dssd = (dgated * value).astype(jnp.bfloat16)
+        dssd_ref[rows, :] = dssd
+        dz_ref[rows, :] = (dgated * ssd * (sig + value * (1.0 - sig))).astype(jnp.bfloat16)
+        xh = mixed_ref[rows, 0:INNER].astype(jnp.float32)
+        product = dssd.astype(jnp.float32) * (ssd - lanes_ref[1:2, :] * xh)
+        top = product.astype(jnp.bfloat16)
+        high_ref[rows, :] = top
+        rest_ref[rows, :] = (product - top.astype(jnp.float32)).astype(jnp.bfloat16)
+        return total
+
+    total = lax.fori_loop(0, GROUP // 16, gate_rows, jnp.zeros((16, INNER), jnp.float32))
+    ggain_ref[...] = ggain_ref[...] + total[0:8] + total[8:16]
+    seg = seg_ref[...]
+    delta_ref[...] = jnp.dot(
+        high_ref[...], seg, preferred_element_type=jnp.float32
+    ) + jnp.dot(rest_ref[...], seg, preferred_element_type=jnp.float32)
+    y_ref[...] = (
+        x_ref[...].astype(jnp.float32)
+        + jnp.dot(gn_ref[...], wout_ref[...], preferred_element_type=jnp.float32)
+    ).astype(jnp.bfloat16)
+
+
+def backward_kernel(
+    xr_ref, bcd_ref, mixed_ref, slope_ref, dssd_ref, state_ref, delta_ref,
+    taps_ref, heads_ref, lanes_ref, seg_ref,
+    dxr_ref, dbcd_ref, gconv_ref, ghead_ref, gskip_ref,
+    run_ref, dext_ref, cb_ref, dcb_ref, xw_ref, dcarry_ref, high_ref, rest_ref, lane_ref, low_ref,
+):
+    half = GROUP // 2
+
+    @pl.when(pl.program_id(0) == 0)
+    def _():
+        run_ref[...] = jnp.zeros_like(run_ref)
+        dext_ref[GROUP:, :] = jnp.zeros((8, CONVW), jnp.float32)
+        gconv_ref[...] = jnp.zeros_like(gconv_ref)
+        ghead_ref[...] = jnp.zeros_like(ghead_ref)
+        gskip_ref[...] = jnp.zeros_like(gskip_ref)
+        lane_ref[...] = jnp.zeros_like(lane_ref)
+
+    bm = mixed_ref[:, INNER : INNER + STATE]
+    cm = mixed_ref[:, INNER + STATE : CONVW]
+    cm_t = cm.astype(jnp.float32).T.astype(jnp.bfloat16)
+    cb_ref[...] = ndot(bm, cm)
+    dcb_ref[...] = jnp.zeros_like(dcb_ref)
+    raw, dt, cum, late = step_sizes(bcd_ref[:, 2 * STATE :], heads_ref)
+    cum_t = cum.T
+    upper = lower_ones(half, True)
+    first = lax.broadcasted_iota(jnp.int32, (1, PAIR), 1) < HEADDIM
+    masks = (first.astype(jnp.float32), 1.0 - first.astype(jnp.float32))
+    for pair in range(HEADS // 2):
+        at = slice(pair * PAIR, (pair + 1) * PAIR)
+        xp = mixed_ref[:, at]
+        dp = dssd_ref[:, at]
+        xf = xp.astype(jnp.float32)
+        df = dp.astype(jnp.float32)
+        spread = []
+        inside = []
+        for place, head in enumerate((2 * pair, 2 * pair + 1)):
+            here = spread_lanes(late, head, GROUP)
+            row = cum_t[head : head + 1, :]
+            own = (xf * masks[place]).astype(jnp.bfloat16)
+            dw_top = ndot(own[:half], dp)
+            dw_low = ndot(own[half:], dp[half:])
+            near = jnp.exp(jnp.where(upper, row[:, :half] - here[:half], LOW))
+            dcb_ref[:half, :half] += dw_top[:, :half] * near
+            near = (cb_ref[:half, :half] * near).astype(jnp.bfloat16)
+            far = jnp.exp(row[:, half:] - here[:half])
+            dcb_ref[:half, half:] += dw_top[:, half:] * far
+            far = (cb_ref[:half, half:] * far).astype(jnp.bfloat16)
+            last = jnp.exp(jnp.where(upper, row[:, half:] - here[half:], LOW))
+            dcb_ref[half:, half:] += dw_low * last
+            last = (cb_ref[half:, half:] * last).astype(jnp.bfloat16)
+            above = jnp.dot(
+                jnp.concatenate([near, far], 1), dp, preferred_element_type=jnp.float32
+            )
+            below = jnp.dot(last, dp[half:], preferred_element_type=jnp.float32)
+            inside.append(jnp.concatenate([above, below], 0))
+            spread.append(here)
+        both = jnp.where(
+            first, spread_lanes(cum, 2 * pair, GROUP), spread_lanes(cum, 2 * pair + 1, GROUP)
+        )
+        end = both[GROUP - 1 : GROUP, :]
+        scale = jnp.exp(end - jnp.where(first, spread[0], spread[1]))
+        xw_ref[:, at] = (xf * scale).astype(jnp.bfloat16)
+        dcarry = (df * jnp.exp(both)).astype(jnp.bfloat16)
+        dcarry_ref[:, at] = dcarry
+        grad = run_ref[:, at]
+        grad_low = grad.astype(jnp.bfloat16)
+        low_ref[:, at] = grad_low
+        dxs = jnp.dot(bm, grad_low, preferred_element_type=jnp.float32) * scale
+        inner = jnp.where(first, inside[0], inside[1]) + dxs
+        gskip_ref[0:1, at] += jnp.sum(df * xf, 0, keepdims=True)
+        product = xf * inner
+        top = product.astype(jnp.bfloat16)
+        high_ref[:, at] = top
+        rest_ref[:, at] = (product - top.astype(jnp.float32)).astype(jnp.bfloat16)
+        dmixed = (inner + lanes_ref[1:2, at] * df).astype(jnp.bfloat16).astype(jnp.float32)
+        dext_ref[0:GROUP, at] = dmixed * slope_ref[:, at]
+        decay = jnp.exp(end)
+        lane_ref[0:1, at] = jnp.sum(xf * dxs, 0, keepdims=True) + decay * jnp.sum(
+            grad * state_ref[:, at], 0, keepdims=True
+        )
+        run_ref[:, at] = decay * grad + jnp.dot(cm_t, dcarry, preferred_element_type=jnp.float32)
+
+    dcb_t = dcb_ref[...]
+    dcb = dcb_t.T.astype(jnp.bfloat16)
+    dbm = ndot(xw_ref[...], low_ref[...]) + jnp.dot(
+        dcb_t.astype(jnp.bfloat16), cm, preferred_element_type=jnp.float32
+    )
+    dcm = ndot(dcarry_ref[...], state_ref[...].astype(jnp.bfloat16)) + jnp.dot(
+        dcb, bm, preferred_element_type=jnp.float32
+    )
+    for place, part in enumerate((dbm, dcm)):
+        at = slice(INNER + place * STATE, INNER + (place + 1) * STATE)
+        dext_ref[0:GROUP, at] = part.astype(jnp.bfloat16).astype(jnp.float32) * slope_ref[:, at]
+    seg = seg_ref[...]
+    sums = jnp.dot(high_ref[...], seg, preferred_element_type=jnp.float32) + jnp.dot(
+        rest_ref[...], seg, preferred_element_type=jnp.float32
+    )
+    dlast = split_dot(lane_ref[...], seg)[0:1, :]
+    final = lax.broadcasted_iota(jnp.int32, (GROUP, 1), 0) == GROUP - 1
+    dcum = delta_ref[...] - sums + jnp.where(final, dlast, 0.0)
+    ones = lower_ones(GROUP, True).astype(jnp.float32).astype(jnp.bfloat16)
+    dlog = exact_dot(ones, dcum)
+    rate = heads_ref[1:2, :]
+    ddt = jnp.where(dt > 0.0, sums / dt, 0.0) + dlog * rate
+    ddt = ddt / (1.0 + jnp.exp(-raw))
+    dbcd_ref[:, 2 * STATE :] = ddt.astype(jnp.bfloat16)
+    ghead_ref[0:1, :] += jnp.sum(ddt, 0, keepdims=True)
+    ghead_ref[1:2, :] += jnp.sum(dlog * dt, 0, keepdims=True) * rate
+
+    def conv_piece(at, source):
+        given = source.astype(jnp.float32)
+        total = None
+        for tap in range(KCONV):
+            moved = dext_ref[KCONV - 1 - tap : KCONV - 1 - tap + GROUP, at]
+            term = taps_ref[tap : tap + 1, at] * moved
+            total = term if total is None else total + term
+            gconv_ref[tap : tap + 1, at] += jnp.sum(given * moved, 0, keepdims=True)
+            if tap == KCONV - 1:
+                gconv_ref[KCONV : KCONV + 1, at] += jnp.sum(moved, 0, keepdims=True)
+        return total.astype(jnp.bfloat16)
+
+    def conv_chunk(chunk, carry):
+        at = pl.ds(pl.multiple_of(chunk * PAIR, PAIR), PAIR)
+        dxr_ref[:, at] = conv_piece(at, xr_ref[:, at])
+        return carry
+
+    lax.fori_loop(0, INNER // PAIR, conv_chunk, 0)
+    for place in range(2):
+        at = slice(INNER + place * STATE, INNER + (place + 1) * STATE)
+        inner = slice(place * STATE, (place + 1) * STATE)
+        dbcd_ref[:, inner] = conv_piece(at, bcd_ref[:, inner])
+    dext_ref[GROUP:, :] = dext_ref[0:8, :]
+
+
+def run_forward(proj, x, go, wout, taps, heads, lanes, seg):
+    length = x.shape[0]
+    count = length // GROUP
+    tall = lambda width: pl.BlockSpec((GROUP, width), lambda i: (i, 0))
+    fixed = lambda a: pl.BlockSpec(a.shape, lambda i: (0, 0))
+    f32, b16 = jnp.float32, jnp.bfloat16
+    return pl.pallas_call(
+        forward_kernel,
+        grid=(count,),
+        in_specs=[
+            pl.BlockSpec((GROUP, INNER), lambda i: (i, 0)),
+            pl.BlockSpec((GROUP, INNER), lambda i: (i, 1)),
+            pl.BlockSpec((GROUP, TAIL), lambda i: (i, 2 * INNER // TAIL)),
+            tall(WIDE), tall(WIDE), fixed(wout), fixed(taps), fixed(heads), fixed(lanes), fixed(seg),
+        ],
+        out_specs=[
+            tall(WIDE), tall(INNER), tall(INNER), tall(INNER), tall(CONVW), tall(CONVW),
+            pl.BlockSpec((STATE, INNER), lambda i: (i, 0)), tall(PAIR),
+            pl.BlockSpec((8, INNER), lambda i: (0, 0)),
+        ],
+        out_shape=[
+            jax.ShapeDtypeStruct((length, WIDE), b16),
+            jax.ShapeDtypeStruct((length, INNER), b16),
+            jax.ShapeDtypeStruct((length, INNER), b16),
+            jax.ShapeDtypeStruct((length, INNER), b16),
+            jax.ShapeDtypeStruct((length, CONVW), b16),
+            jax.ShapeDtypeStruct((length, CONVW), f32),
+            jax.ShapeDtypeStruct((count * STATE, INNER), f32),
+            jax.ShapeDtypeStruct((length, PAIR), f32),
+            jax.ShapeDtypeStruct((8, INNER), f32),
+        ],
+        scratch_shapes=[
+            pltpu.VMEM((STATE, INNER), f32), pltpu.VMEM((GROUP + 8, CONVW), f32),
+            pltpu.VMEM((GROUP, GROUP), f32), pltpu.VMEM((GROUP, INNER), f32),
+            pltpu.VMEM((GROUP, INNER), f32), pltpu.VMEM((GROUP, INNER), b16),
+            pltpu.VMEM((GROUP, INNER), b16),
+        ],
+        compiler_params=pltpu.CompilerParams(
+            dimension_semantics=("arbitrary",), vmem_limit_bytes=48 * 1024 * 1024
+        ),
+        cost_estimate=pl.CostEstimate(flops=12 * 10**9, bytes_accessed=40 * 10**6, transcendentals=10**7),
+        name="scan_forward",
+    )(proj, proj, proj, x, go, wout, taps, heads, lanes, seg)
+
+
+def run_backward(proj, mixed, slope, dssd, states, delta, taps, heads, lanes, seg):
+    length = proj.shape[0]
+    count = length // GROUP
+    tall = lambda width: pl.BlockSpec((GROUP, width), lambda i: (count - 1 - i, 0))
+    fixed = lambda a: pl.BlockSpec(a.shape, lambda i: (0, 0))
+    f32, b16 = jnp.float32, jnp.bfloat16
+    return pl.pallas_call(
+        backward_kernel,
+        grid=(count,),
+        in_specs=[
+            pl.BlockSpec((GROUP, INNER), lambda i: (count - 1 - i, 1)),
+            pl.BlockSpec((GROUP, TAIL), lambda i: (count - 1 - i, 2 * INNER // TAIL)),
+            tall(CONVW), tall(CONVW), tall(INNER),
+            pl.BlockSpec((STATE, INNER), lambda i: (count - 1 - i, 0)), tall(PAIR),
+            fixed(taps), fixed(heads), fixed(lanes), fixed(seg),
+        ],
+        out_specs=[
+            tall(INNER), tall(TAIL),
+            pl.BlockSpec((8, CONVW), lambda i: (0, 0)),
+            pl.BlockSpec((8, PAIR), lambda i: (0, 0)),
+            pl.BlockSpec((8, INNER), lambda i: (0, 0)),
+        ],
+        out_shape=[
+            jax.ShapeDtypeStruct((length, INNER), b16),
+            jax.ShapeDtypeStruct((length, TAIL), b16),
+            jax.ShapeDtypeStruct((8, CONVW), f32),
+            jax.ShapeDtypeStruct((8, PAIR), f32),
+            jax.ShapeDtypeStruct((8, INNER), f32),
+        ],
+        scratch_shapes=[
+            pltpu.VMEM((STATE, INNER), f32), pltpu.VMEM((GROUP + 8, CONVW), f32),
+            pltpu.VMEM((GROUP, GROUP), f32), pltpu.VMEM((GROUP, GROUP), f32),
+            pltpu.VMEM((GROUP, INNER), b16), pltpu.VMEM((GROUP, INNER), b16),
+            pltpu.VMEM((GROUP, INNER), b16), pltpu.VMEM((GROUP, INNER), b16),
+            pltpu.VMEM((8, INNER), f32), pltpu.VMEM((STATE, INNER), b16),
+        ],
+        compiler_params=pltpu.CompilerParams(
+            dimension_semantics=("arbitrary",), vmem_limit_bytes=48 * 1024 * 1024
+        ),
+        cost_estimate=pl.CostEstimate(flops=12 * 10**9, bytes_accessed=40 * 10**6, transcendentals=10**7),
+        name="scan_backward",
+    )(proj, proj, mixed, slope, dssd, states, delta, taps, heads, lanes, seg)
+
+
+def head_segments():
+    rows = lax.broadcasted_iota(jnp.int32, (INNER, PAIR), 0) // HEADDIM
+    cols = lax.broadcasted_iota(jnp.int32, (INNER, PAIR), 1)
+    return (rows == cols).astype(jnp.bfloat16)
+
+
+def head_tables(dt_bias, rate, skip):
+    pad = lambda v: jnp.pad(v.astype(jnp.float32), (0, PAIR - HEADS))
+    zero = jnp.zeros((PAIR,), jnp.float32)
+    heads = jnp.stack([pad(dt_bias), pad(rate)] + [zero] * 6)
+    return (heads, jnp.repeat(skip, HEADDIM))
+
+
+def whole_sequence(xb, cot, wts, dt_bias, rate, skip):
+    gain_in, w_in, taps_bias, gain_gate, w_out = wts
+    xf = xb.astype(jnp.float32)
+    r_in = lax.rsqrt(jnp.mean(xf * xf, -1, keepdims=True) + EPS)
+    gain = gain_in.astype(jnp.float32)
+    normed = (xf * r_in * gain).astype(jnp.bfloat16)
+    proj = jnp.dot(normed, w_in, preferred_element_type=jnp.float32).astype(jnp.bfloat16)
+    heads, skip_lanes = head_tables(dt_bias, rate, skip)
+    lanes = jnp.stack([gain_gate.astype(jnp.float32), skip_lanes] + [jnp.zeros_like(skip_lanes)] * 6)
+    seg = head_segments()
+    y, gnorm, dz, dssd, mixed, slope, states, delta, ggain = run_forward(
+        proj, xb, cot, w_out, taps_bias, heads, lanes, seg
+    )
+    grad_wout = tdot(gnorm, cot)
+    grad_wz = tdot(normed, dz)
+    dxr, dbcd, gconv, ghead, gskip = run_backward(
+        proj, mixed, slope, dssd, states, delta, taps_bias, heads, lanes, seg
+    )
+    dnormed = (
+        ndot(dz, w_in[:, :INNER]) + ndot(dxr, w_in[:, INNER : 2 * INNER]) + ndot(dbcd, w_in[:, 2 * INNER :])
+    )
+    scaled = gain * dnormed
+    dx = (
+        r_in * scaled
+        - xf * r_in**3 * jnp.mean(scaled * xf, -1, keepdims=True)
+        + cot.astype(jnp.float32)
+    ).astype(jnp.bfloat16)
+    grad_gin = jnp.sum(dnormed * xf * r_in, 0)
+    grad_wx = tdot(normed, dxr)
+    grad_wtail = tdot(normed, dbcd)
+    head_terms = jnp.concatenate(
+        [ghead[0, :HEADS], ghead[1, :HEADS], jnp.sum(gskip[0].reshape(HEADS, HEADDIM), -1)]
+    )
+    return (
+        y, dx,
+        (grad_gin, grad_wz, grad_wx, grad_wtail, gconv, jnp.sum(ggain, 0), grad_wout, head_terms),
+    )
+
+
+SMALL = 280
+
+
+def swap_halves(parts):
+    place = lax.axis_index("seq")
+    count = lax.axis_size("seq")
+    size = parts.shape[1]
+    whole = jnp.zeros((count * size,) + parts.shape[2:], parts.dtype)
+    own = lax.dynamic_index_in_dim(parts, place, 0, False)
+    whole = lax.dynamic_update_slice_in_dim(whole, own, place * size, 0)
+    for hop in range(1, count):
+        there = lax.rem(place + hop, count)
+        source = lax.rem(place + count - hop, count)
+        sent = lax.dynamic_index_in_dim(parts, there, 0, False)
+        got = lax.ppermute(sent, "seq", [(i, (i + hop) % count) for i in range(count)])
+        whole = lax.dynamic_update_slice_in_dim(whole, got, source * size, 0)
+    return whole
+
+
+def gather_weights(norm_gain, in_weight, conv_weight, conv_bias, gate_gain, out_weight):
+    devices = lax.axis_size(("dp", "seq"))
+    rows = in_weight.shape[0]
+    small = jnp.concatenate([norm_gain, conv_weight.reshape(-1), conv_bias, gate_gain])
+    sizes = (norm_gain.size, conv_weight.size, conv_bias.size, gate_gain.size)
+    line = jnp.pad(small[None], ((0, rows - 1), (0, WIDE - SMALL - small.size)))
+    pieces = [in_weight[:, k * WIDE : (k + 1) * WIDE] for k in range(4)]
+    pieces.append(jnp.concatenate([in_weight[:, 4 * WIDE :], line], 1))
+    pieces.append(out_weight)
+    packed = jnp.concatenate(pieces, 0)
+    full = lax.all_gather(packed, ("dp", "seq"), axis=0)
+    columns = [
+        full[:, k * rows : (k + 1) * rows].reshape(devices * rows, WIDE) for k in range(4)
+    ]
+    last = full[:, 4 * rows : 5 * rows].reshape(devices * rows, WIDE)[:, :SMALL]
+    columns.append(jnp.pad(last, ((0, 0), (0, TAIL - SMALL))))
+    w_in = jnp.concatenate(columns, 1)
+    w_out = full[:, 5 * rows :].reshape(devices * out_weight.shape[0], WIDE)
+    table = full[:, 4 * rows, SMALL : SMALL + small.size]
+    a, b, c = sizes[0], sizes[0] + sizes[1], sizes[0] + sizes[1] + sizes[2]
+    gain_in = table[:, :a].reshape(-1)
+    taps = table[:, a:b].reshape(devices, KCONV, -1).transpose(1, 0, 2).reshape(KCONV, -1)
+    bias = table[:, b:c].reshape(1, -1)
+    gain_gate = table[:, c:].reshape(-1)
+    taps_bias = jnp.pad(
+        jnp.concatenate([taps, bias], 0).astype(jnp.float32), ((0, 7 - KCONV), (0, 0))
+    )
+    return (gain_in, w_in, taps_bias, gain_gate, w_out)
+
+
+def by_owner(grad, devices):
+    return grad.astype(jnp.bfloat16).reshape(devices, -1, grad.shape[-1])
+
+
 def shards(
+    x_in, grad_out, norm_gain, in_weight, conv_weight, conv_bias, gate_gain, out_weight, dt_bias, a_log, skip
+):
+    if x_in.shape[0] != lax.axis_size("seq"):
+        return shards_general(
+            x_in, grad_out, norm_gain, in_weight, conv_weight, conv_bias, gate_gain, out_weight,
+            dt_bias, a_log, skip,
+        )
+    rate = -jnp.exp(a_log)
+    devices = lax.axis_size(("dp", "seq"))
+    micro, _, length, _ = x_in.shape
+    rows = in_weight.shape[0]
+    wts = gather_weights(norm_gain, in_weight, conv_weight, conv_bias, gate_gain, out_weight)
+    xb = swap_halves(x_in[:, 0])
+    cot = swap_halves(grad_out[:, 0])
+    y, dx, terms = whole_sequence(xb, cot, wts, dt_bias, rate, skip)
+    y_out = swap_halves(y.reshape(micro, length, WIDE)).reshape(x_in.shape)
+    dx_in = swap_halves(dx.reshape(micro, length, WIDE)).reshape(x_in.shape)
+    grad_gin, grad_wz, grad_wx, grad_wtail, gconv, ggain, grad_wout, head_terms = terms
+    early = jnp.concatenate(
+        [
+            by_owner(grad_wz[:, :WIDE], devices),
+            by_owner(grad_wz[:, WIDE:], devices),
+            by_owner(grad_wout, devices),
+        ],
+        1,
+    )
+    small = jnp.concatenate(
+        [
+            grad_gin.reshape(devices, -1),
+            gconv[:KCONV].reshape(KCONV, devices, -1).transpose(1, 0, 2).reshape(devices, -1),
+            gconv[KCONV].reshape(devices, -1),
+            ggain.reshape(devices, -1),
+            jnp.broadcast_to(head_terms, (devices, 3 * HEADS)),
+        ],
+        1,
+    ).astype(jnp.bfloat16)
+    line = jnp.pad(small[:, None], ((0, 0), (0, rows - 1), (0, WIDE - SMALL - small.shape[1])))
+    late = jnp.concatenate(
+        [
+            by_owner(grad_wx[:, :WIDE], devices),
+            by_owner(grad_wx[:, WIDE:], devices),
+            jnp.concatenate([by_owner(grad_wtail[:, :SMALL], devices), line], 2),
+        ],
+        1,
+    )
+    early = reduce_owned(early).astype(jnp.float32)
+    late = reduce_owned(late).astype(jnp.float32)
+    own_in = jnp.concatenate(
+        [early[:rows], early[rows : 2 * rows], late[:rows], late[rows : 2 * rows], late[2 * rows :, :SMALL]],
+        1,
+    )
+    own = late[2 * rows, SMALL : SMALL + small.shape[1]]
+    cuts = [norm_gain.size, conv_weight.size, conv_bias.size, gate_gain.size, HEADS, HEADS, HEADS]
+    found = []
+    at = 0
+    for size in cuts:
+        found.append(own[at : at + size])
+        at += size
+    return (
+        y_out,
+        dx_in,
+        found[0],
+        own_in,
+        found[1].reshape(conv_weight.shape),
+        found[2],
+        found[3],
+        early[2 * rows :],
+        found[4],
+        found[5],
+        found[6],
+    )
+
+
+def reduce_owned(parts):
+    return lax.psum_scatter(parts, ("dp", "seq"), scatter_dimension=0, tiled=False)
+
+
+def shards_general(
     x_in,
     grad_out,
     norm_gain,

time: 712 us -> 485 us (0.68)
  blocking collectives: 189 us -> 0 us
  waiting for transfers between devices: 149 us -> 261 us
  matrix products: 132 us -> 32.9 us
  other arithmetic: 102 us -> 14.8 us
  Pallas kernels: 0 us -> 86.1 us
  local copies, waits for them, and re-layouts: 97.5 us -> 68.3 us
  loops' own time: 7.96 us -> 0 us
    reduce_scatter x1 -> x2, waiting for transfers between devices: 0.01 us -> 154 us  [reduce_owned(): lax.psum_scatter(parts, ('dp', 'seq'), scatter_dimension=0, tiled=False)]
    unnamed x5 -> x3, waiting for transfers between devices: 125 us -> 0.05 us
    all_gather x7 -> x0, blocking collectives: 109 us -> none  [the longest x6 55.5 us: prefix(): lax.all_gather(a.astype(kind), axis)]
    pallas_call x0 -> x2, Pallas kernels: none -> 86.1 us  [the longest x1 48.4 us: run_forward(): pl.pallas_call(forward_kernel, grid=(count,), in_specs=[pl.BlockSpec((GRO...]
    dot_general x28 -> x1, matrix products: 92.9 us -> 10.7 us  [whole_sequence(): jnp.dot(normed, w_in, preferred_element_type=jnp.float32)]
    unnamed x2 -> x0, blocking collectives: 80.2 us -> none
    ppermute x4, waiting for transfers between devices: 2.05 us -> 69.4 us  [swap_halves(): lax.ppermute(sent, 'seq', [(i, (i + hop) % count) for i in range(count)])]
    another operation x21 -> x4, other arithmetic: 40.5 us -> 0.23 us
  transfers between devices with their start and end apart: 8 -> 7, of which waited for: 3 -> 7; matrix products, arithmetic and copies ran while one was open for 16% -> 7% of each run, Pallas kernels for 0% -> 0%
where the time goes in v1:
time: 485 us; the launch traced here: 482 us
  waiting for transfers between devices  261 us (54%)
  Pallas kernels  86.1 us (18%)
  local copies, waits for them, and re-layouts  68.3 us (14%)
  matrix products  32.9 us (7%)
  other arithmetic  14.8 us (3%)
  between operations  14.4 us (3%)
    reduce_scatter x2, waiting for transfers between devices, reduce_owned(): lax.psum_scatter(parts, ('dp', 'seq'), scatter_dimension=0, tiled=False)  154 us
    ppermute x4, waiting for transfers between devices, swap_halves(): lax.ppermute(sent, 'seq', [(i, (i + hop) % count) for i in range(count)])  69.4 us
    pallas_call x1, Pallas kernels, run_forward(): pl.pallas_call(forward_kernel, grid=(count,), in_specs=[pl.BlockSpec((GRO...  48.4 us
    pallas_call x1, Pallas kernels, run_backward(): pl.pallas_call(backward_kernel, grid=(count,), in_specs=[pl.BlockSpec((GR...  37.7 us
    all_gather x1, waiting for transfers between devices, gather_weights(): full = lax.all_gather(packed, ('dp', 'seq'), axis=0)  37.3 us
    unnamed x83, local copies, waits for them, and re-layouts  16.2 us
    dot_general x4, matrix products, tdot(): lax.dot_general(left, right, (((0,), (0,)), ((), ())), preferred_element_...  13.7 us
    dot_general x1, matrix products, whole_sequence(): jnp.dot(normed, w_in, preferred_element_type=jnp.float32)  10.7 us
  transfers between devices with their start and end apart: 7, of which 7 were waited for; matrix products, arithmetic and copies ran while one was open for 7% of the time, Pallas kernels for 0%

profile of v1, /device:TPU:8, one launch (start us, length us, event | category | flops | bytes accessed | tf_op | source)
XLA Modules:
  0.0 481.9 jit_solution(16028985956311747962)
XLA Ops:
  14.5 2.1 dynamic-slice_bitcast_fusion.3
  16.5 1.5 collective-permute-start
  18.0 2.1 dynamic-slice_bitcast_fusion.2
  24.5 14.6 %collective-permute-done = bf16[512,768]{1,0:T(8,128)(2,1)} collective-permute-done((bf16[512,768]{1,0:T(8,128)(2,1)}, bf16[512,768]{1,0:T(8,128)(2,1)}, u32[]{:S(2)}, u32[]{:S(2)}) %collective-permute-start) | collective-permute-done | bytes 786464 | tf_op jit(solution)/shard_map/ppermute | solution.py:732
  40.3 21.9 %collective-permute-done.1 = bf16[512,768]{1,0:T(8,128)(2,1)} collective-permute-done((bf16[512,768]{1,0:T(8,128)(2,1)}, bf16[512,768]{1,0:T(8,128)(2,1)}, u32[]{:S(2)}, u32[]{:S(2)}) %collective-permute-start.1) | collective-permute-done | bytes 786464 | tf_op jit(solution)/shard_map/ppermute | solution.py:732
  64.4 37.3 %all-gather.3.cloned.1.call-done = bf16[5376,768]{1,0:T(8,128)(2,1)} async-done(((bf16[168,768]{1,0:T(8,128)(2,1)}), bf16[5376,768]{1,0:T(8,128)(2,1)}) %all-gather.3.cloned.1.call-update) | async-done | bytes 8257552 | tf_op jit(solution)/shard_map/all_gather | solution.py:747
  101.6 5.0 %fusion.51 = (bf16[32,24,768]{2,1,0:T(8,128)(2,1)}, bf16[32,24,768]{2,1,0:T(8,128)(2,1)}, bf16[32,24,768]{2,1,0:T(8,128)(2,1)}, bf16[32,24,768]{2,1,0:T(8,128)(2,1)}, bf16[32,24,768]{2,1,0:T(8,128)(2,1)S(1)}) fusion(bf16[32,168,768]{2,1,0:T(8,128)(2,1)} %bitcast.97), kind=kLoop, calls=%fused_computation.121 | loop fusion | bytes 11796480 | tf_op jit(solution)/shard_map/slice | solution.py:751
  107.8 3.2 slice.233
  121.5 2.6 constant_dynamic-update-slice_fusion.3
  127.5 10.7 %convolution_convert_fusion.z_ref.xr_ref.bcd_ref = bf16[1024,3456]{1,0:T(8,128)(2,1)} fusion(bf16[768,3456]{1,0:T(8,128)(2,1)} %fusion.27, bf16[1024,768]{1,0:T(8,128)(2,1)S(1)} %constant_dynamic-update-slice_fusion.7.x_ref, f32[768]{0:T(1024)S(1)} %copy-done.22, f32[1024]{0:T(1024)S(1)} %copy-done.20), kind=kOutput, calls=%fused_computation | convolution fusion | flops 5442502656 | bytes 13966336 | tf_op jit(solution)/shard_map/dot_general | solution.py:685
  138.2 48.4 %scan_forward.1 = (bf16[1024,768]{1,0:T(8,128)(2,1)S(1)}, bf16[1024,1536]{1,0:T(8,128)(2,1)}, bf16[1024,1536]{1,0:T(8,128)(2,1)}, bf16[1024,1536]{1,0:T(8,128)(2...) custom-call(bf16[1024,3456]{1,0:T(8,128)(2,1)} %convolution_convert_, ...), custom_call_target="tpu_custom_call" | custom-call | flops 12000000000 | bytes 40000000 | tf_op jit(solution)/shard_map/scan_forward/pallas_call | solution.py:583
  188.4 37.7 %scan_backward.1 = (bf16[1024,1536]{1,0:T(8,128)(2,1)S(1)}, bf16[1024,384]{1,0:T(8,128)(2,1)S(1)}, f32[8,1792]{1,0:T(8,128)S(1)}, f32[8,128]{1,0:T(8,128)S(1)}, f32[8,1536]{1,0:T(8,128)S(1)}) custom-call(bf16[1024,3456]{1,0:T(8,128)(2,1)} %convolution_convert_fusion.z_ref.xr_ref.bcd_ref, bf16[1024,3456]{1,0:T(8,128)(2,1)} %convolution_convert_fusion.z_ref.xr_ref.bcd_ref, ...), custom_call_target="tpu_custom_call" | custom-call | flops 12000000000 | bytes 40000000 | tf_op jit(solution)/shard_map/scan_backward/pallas_call | solution.py:628
  227.2 1.8 fusion.47
  229.0 2.6 fusion.19
  231.6 4.0 convolution_convert_fusion.3
  235.7 4.9 %fusion.14 = (bf16[768]{0:T(1024)(128)(2,1)S(1)}, f32[1024]{0:T(1024)S(1)}, f32[1024,768]{1,0:T(8,128)}) fusion(bf16[1024,768]{1,0:T(8,128)(2,1)S(1)} %constant_dynamic-update-slice_fusion.7.x_ref, f32[1024]{0:T(1024)S(1)} %copy-done.20, f32[768]{0:T(1024)S(1)} %copy-done.22, f32[1024,768]{1,0:T(8,128)S(1)} %fusion.26, f32[1024,768]{1,0:T(8,128)S(1)} %fusion.19, ...), kind=kOutput, calls=%fused_computation.26 | convolution fusion | flops 2427713792 | bytes 16527872 | tf_op jit(solution)/shard_map/dot_general | solution.py:56
  242.2 1.8 slice.293
  244.0 2.1 copy.41
  246.1 1.9 copy.43
  248.0 1.8 fusion.53
  252.5 2.1 fusion.4
  254.7 3.8 copy.46
  259.1 4.9 %convolution_convert_fusion.2 = bf16[768,1536]{1,0:T(8,128)(2,1)S(1)} fusion(bf16[1024,1536]{1,0:T(8,128)(2,1)} %get-tuple-element.26, bf16[1024,768]{1,0:T(8,128)(2,1)S(1)} %constant_dynamic-update-slice_fusion.7.x_ref, f32[768]{0:T(1024)S(1)} %copy-done.23, f32[1024]{0:T(1024)S(1)} %copy-done.21), kind=kOutput, calls=%fused_computation.15 | convolution fusion | flops 2420244480 | bytes 7085056 | tf_op jit(solution)/shard_map/dot_general | solution.py:50
  264.2 1.8 copy-done.34
  266.0 2.9 convolution_convert_fusion.1
  268.9 2.5 pad_maximum_fusion
  272.7 1.5 collective-permute-start.2
  274.1 2.5 fusion.11
  278.4 14.7 %collective-permute-done.2 = bf16[512,768]{1,0:T(8,128)(2,1)S(1)} collective-permute-done((bf16[512,768]{1,0:T(8,128)(2,1)S(1)}, bf16[512,768]{1,0:T(8,128)(2,1)S(1)}, u32[]{:S(2)}, u32[]{:S(2)}) %collective-permute-start.2) | collective-permute-done | bytes 786464 | tf_op jit(solution)/shard_map/ppermute | solution.py:732
  293.2 18.2 %collective-permute-done.3 = bf16[512,768]{1,0:T(8,128)(2,1)S(1)} collective-permute-done((bf16[512,768]{1,0:T(8,128)(2,1)S(1)}, bf16[512,768]{1,0:T(8,128)(2,1)S(1)}, u32[]{:S(2)}, u32[]{:S(2)}) %collective-permute-start.3) | collective-permute-done | bytes 786464 | tf_op jit(solution)/shard_map/ppermute | solution.py:732
  311.4 49.3 %reduce-scatter.3.cloned.1.call-done = bf16[1,72,768]{2,1,0:T(8,128)(2,1)} async-done(((bf16[32,72,768]{2,1,0:T(8,128)(2,1)}), bf16[1,72,768]{2,1,0:T(8,128)(2,1)}) %reduce-scatter.3.cloned.1.call-update) | async-done | bytes 110608 | tf_op jit(solution)/shard_map/reduce_scatter | solution.py:846
  367.0 105.2 %reduce-scatter.5.cloned.1.call-done = bf16[1,96,768]{2,1,0:T(8,128)(2,1)} async-done(((bf16[32,96,768]{2,1,0:T(8,128)(2,1)}), bf16[1,96,768]{2,1,0:T(8,128)(2,1)}) %reduce-scatter.5.cloned.1.call-update) | async-done | bytes 147472 | tf_op jit(solution)/shard_map/reduce_scatter | solution.py:846
  (169 shorter events, 50.2 us)
Async XLA Ops:
  7.2 14.5 %copy-start.13 = (bf16[2,1,512,768]{3,2,1,0:T(8,128)(2,1)S(1)}, bf16[2,1,512,768]{3,2,1,0:T(8,128)(2,1)}, u32[]{:S(2)}) copy-start(bf16[2,1,512,768]{3,2,1,0:T(8,128)(2,1)} %param.11) | copy-start | bytes 4718596
  7.2 13.6 %copy-start.30 = (f32[24]{0:T(128)S(1)}, f32[24]{0:T(128)}, u32[]{:S(2)}) copy-start(f32[24]{0:T(128)} %param.21) | copy-start | bytes 292
  7.2 94.4 %all-gather.3.cloned.1.call-start = ((), (), s32[]{:S(2)}) async-start(), calls=%async_computation.4 | async-start | bytes 8515584 | tf_op jit(solution)/shard_map/all_gather | solution.py:747
  14.4 346.3 %reduce-scatter.3.cloned.1.call-start = ((), (), s32[]{:S(2)}) async-start(), calls=%async_computation.2 | async-start | bytes 3649536 | tf_op jit(solution)/shard_map/reduce_scatter | solution.py:846
  16.5 22.6 %collective-permute-start = (bf16[512,768]{1,0:T(8,128)(2,1)}, bf16[512,768]{1,0:T(8,128)(2,1)}, u32[]{:S(2)}, u32[]{:S(2)}) collective-permute-start(bf16[512,768]{1,0:T(8,128)(2,1)} %dynamic-slice_bitcast_fusion.3), channel_id=1, source_target_pairs={{0,1},{1,0},{2,3},{3,2},{4,5},{5,4},{6,7},{7,6},{8,9},{9,8},{10,11... | collective-permute-start | bytes 2359304 | tf_op jit(solution)/shard_map/ppermute | solution.py:732
  20.1 42.1 %collective-permute-start.1 = (bf16[512,768]{1,0:T(8,128)(2,1)}, bf16[512,768]{1,0:T(8,128)(2,1)}, u32[]{:S(2)}, u32[]{:S(2)}) collective-permute-start(bf16[512,768]{1,0:T(8,128)(2,1)} %dynamic-slice_bitcast_fusion.2), channel_id=1, source_target_pairs={{0,1},{1,0},{2,3},{3,2},{4,5},{5,4},{6,7},{7,6},{8,9},{9,8},{10,11... | collective-permute-start | bytes 2359304 | tf_op jit(solution)/shard_map/ppermute | solution.py:732
  20.7 2.4 copy-start.26
  20.8 2.4 copy-start.28
  106.6 6.5 %copy-start.7 = (bf16[32,24,768]{2,1,0:T(8,128)(2,1)}, bf16[32,24,768]{2,1,0:T(8,128)(2,1)S(1)}, u32[]{:S(2)}) copy-start(bf16[32,24,768]{2,1,0:T(8,128)(2,1)S(1)} %get-tuple-element.78) | copy-start | bytes 3538948
  121.4 2.7 copy-start.10
  121.5 3.8 copy-start.9
  121.5 4.9 %copy-start.17 = (bf16[4,1792]{1,0:T(4,128)(2,1)S(1)}, bf16[4,1792]{1,0:T(4,128)(2,1)}, u32[]{:S(2)}) copy-start(bf16[4,1792]{1,0:T(4,128)(2,1)} %reshape.240) | copy-start | bytes 43012
  121.5 4.9 %copy-start.18 = (bf16[1,1792]{1,0:T(2,128)(2,1)S(1)}, bf16[1,1792]{1,0:T(2,128)(2,1)}, u32[]{:S(2)}) copy-start(bf16[1,1792]{1,0:T(2,128)(2,1)} %reshape.241) | copy-start | bytes 10756
  121.5 4.9 %copy-start.19 = (f32[1,1536]{1,0:T(1,128)S(1)}, f32[1,1536]{1,0:T(1,128)}, u32[]{:S(2)}) copy-start(f32[1,1536]{1,0:T(1,128)} %stack_reshape.3) | copy-start | bytes 18436
  121.5 4.9 %copy-start.27 = (f32[8]{0:T(128)S(1)}, f32[8]{0:T(128)}, u32[]{:S(2)}) copy-start(f32[8]{0:T(128)} %copy-done.26) | copy-start | bytes 100
  121.5 4.9 %copy-start.29 = (f32[8]{0:T(128)S(1)}, f32[8]{0:T(128)}, u32[]{:S(2)}) copy-start(f32[8]{0:T(128)} %copy-done.28) | copy-start | bytes 100
  121.5 5.0 %copy-start.5 = (bf16[32,24,768]{2,1,0:T(8,128)(2,1)S(1)}, bf16[32,24,768]{2,1,0:T(8,128)(2,1)}, u32[]{:S(2)}) copy-start(bf16[32,24,768]{2,1,0:T(8,128)(2,1)} %get-tuple-element.74) | copy-start | bytes 3538948
  121.5 5.0 %copy-start.25 = (pred[384]{0:T(512)(128)(4,1)S(1)}, pred[384]{0:T(512)(128)(4,1)}, u32[]{:S(2)}) copy-start(pred[384]{0:T(512)(128)(4,1)} %constant.75.clone.1) | copy-start | bytes 1156
  124.1 3.4 copy-start.20
  124.1 3.4 copy-start.22
  226.1 2.9 copy-start.4
  226.1 2.9 copy-start.16
  231.6 4.1 copy-start.6
  231.6 4.1 copy-start.8
  231.6 4.1 copy-start.33
  235.7 5.0 %slice-start = ((bf16[8,1792]{1,0:T(8,128)(2,1)}), bf16[4,1792]{1,0:T(4,128)(2,1)S(1)}, s32[]{:S(2)}) async-start(bf16[8,1792]{1,0:T(8,128)(2,1)} %copy-done.16), calls=%async_computation.5 | async-start | bytes 28672 | tf_op jit(solution)/shard_map/slice | solution.py:801
  235.7 5.3 %copy-start.3 = (f32[8,1536]{1,0:T(8,128)S(1)}, f32[8,1536]{1,0:T(8,128)}, u32[]{:S(2)}) copy-start(f32[8,1536]{1,0:T(8,128)} %copy-done.2) | copy-start | bytes 147460
  258.5 213.7 %reduce-scatter.5.cloned.1.call-start = ((), (), s32[]{:S(2)}) async-start(), calls=%async_computation.3 | async-start | bytes 4866048 | tf_op jit(solution)/shard_map/reduce_scatter | solution.py:846
  272.7 20.4 %collective-permute-start.2 = (bf16[512,768]{1,0:T(8,128)(2,1)S(1)}, bf16[512,768]{1,0:T(8,128)(2,1)S(1)}, u32[]{:S(2)}, u32[]{:S(2)}) collective-permute-start(bf16[512,768]{1,0:T(8,128)(2,1)S(1)} %dynamic-slice_bitcast_fusion.1), channel_id=1, source_target_pairs={{0,1},{1,0},{2,3},{3,2},{4,5},{5,4},{6,7},{7,6},{8,9},{9,8},{10,11... | collective-permute-start | bytes 2359304 | tf_op jit(solution)/shard_map/ppermute | solution.py:732
  276.8 34.6 %collective-permute-start.3 = (bf16[512,768]{1,0:T(8,128)(2,1)S(1)}, bf16[512,768]{1,0:T(8,128)(2,1)S(1)}, u32[]{:S(2)}, u32[]{:S(2)}) collective-permute-start(bf16[512,768]{1,0:T(8,128)(2,1)S(1)} %dynamic-slice_bitcast_fusion), channel_id=1, source_target_pairs={{0,1},{1,0},{2,3},{3,2},{4,5},{5,4},{6,7},{7,6},{8,9},{9,8},{10,11... | collective-permute-start | bytes 2359304 | tf_op jit(solution)/shard_map/ppermute | solution.py:732
  293.2 181.5 %copy-start.12 = (bf16[1024,768]{1,0:T(8,128)(2,1)}, bf16[1024,768]{1,0:T(8,128)(2,1)S(1)}, u32[]{:S(2)}) copy-start(bf16[1024,768]{1,0:T(8,128)(2,1)S(1)} %constant_dynamic-update-slice_fusion.5) | copy-start | bytes 4718596
  311.4 163.2 %copy-start.11 = (bf16[1024,768]{1,0:T(8,128)(2,1)}, bf16[1024,768]{1,0:T(8,128)(2,1)S(1)}, u32[]{:S(2)}) copy-start(bf16[1024,768]{1,0:T(8,128)(2,1)S(1)} %constant_dynamic-update-slice_fusion.8) | copy-start | bytes 4718596
  (11 other events, 11.7 us)
Sparse Core Ops, SparseCore 0:
  14.5 87.0 all-gather.2
  258.6 102.0 reduce-scatter.2
  366.2 105.9 reduce-scatter.4

commit v2 on v1

--- a/solution.py
+++ b/solution.py
@@ -281,7 +281,7 @@
 
 PAIR = 2 * HEADDIM
 WIDE = 768
-TAIL = 384
+XTAIL = 1920
 LOW = -1e30
 
 
@@ -326,10 +326,10 @@
     return jnp.broadcast_to(table[:, head : head + 1], (rows, PAIR))
 
 
-def forward_kernel(
-    z_ref, xr_ref, bcd_ref, x_ref, go_ref, wout_ref, taps_ref, heads_ref, lanes_ref, seg_ref,
-    y_ref, gn_ref, dz_ref, dssd_ref, mixed_ref, slope_ref, state_ref, delta_ref, ggain_ref,
-    run_ref, cin_ref, cb_ref, ssd_ref, dgn_ref, high_ref, rest_ref,
+def scan_kernel(
+    xt_ref, taps_ref, heads_ref, lanes_ref,
+    mixed_ref, slope_ref, state_ref, ssd_ref,
+    run_ref, cin_ref, cb_ref,
 ):
     half = GROUP // 2
 
@@ -337,10 +337,8 @@
     def _():
         run_ref[...] = jnp.zeros_like(run_ref)
         cin_ref[0:8, :] = jnp.zeros((8, CONVW), jnp.float32)
-        ggain_ref[...] = jnp.zeros_like(ggain_ref)
-
-    cin_ref[8 : 8 + GROUP, 0:INNER] = xr_ref[...].astype(jnp.float32)
-    cin_ref[8 : 8 + GROUP, INNER:CONVW] = bcd_ref[:, 0 : 2 * STATE].astype(jnp.float32)
+
+    cin_ref[8 : 8 + GROUP, :] = xt_ref[:, 0:CONVW].astype(jnp.float32)
 
     def conv_chunk(chunk, carry):
         at = pl.ds(pl.multiple_of(chunk * PAIR, PAIR), PAIR)
@@ -359,9 +357,8 @@
     cm = mixed_ref[:, INNER + STATE : CONVW]
     bm_t = bm.astype(jnp.float32).T.astype(jnp.bfloat16)
     cb_ref[...] = ndot(cm, bm)
-    _, _, cum, late = step_sizes(bcd_ref[:, 2 * STATE :], heads_ref)
+    _, _, cum, late = step_sizes(xt_ref[:, CONVW:], heads_ref)
     late_t = late.T
-    dgn_ref[...] = ndot(go_ref[...], wout_ref[...])
     lower = lower_ones(half, False)
     first = lax.broadcasted_iota(jnp.int32, (1, PAIR), 1) < HEADDIM
     for pair in range(HEADS // 2):
@@ -403,6 +400,18 @@
             bm_t, xw, preferred_element_type=jnp.float32
         )
 
+
+def gate_kernel(
+    z_ref, ssd_ref, xh_ref, x_ref, go_ref, wout_ref, lanes_ref, seg_ref,
+    y_ref, gn_ref, dz_ref, dssd_ref, delta_ref, ggain_ref,
+    dgn_ref, high_ref, rest_ref,
+):
+    @pl.when(pl.program_id(0) == 0)
+    def _():
+        ggain_ref[...] = jnp.zeros_like(ggain_ref)
+
+    dgn_ref[...] = ndot(go_ref[...], wout_ref[...])
+
     def gate_rows(index, total):
         rows = pl.ds(pl.multiple_of(index * 16, 16), 16)
         ssd = ssd_ref[rows, :]
@@ -421,7 +430,7 @@
         dssd = (dgated * value).astype(jnp.bfloat16)
         dssd_ref[rows, :] = dssd
         dz_ref[rows, :] = (dgated * ssd * (sig + value * (1.0 - sig))).astype(jnp.bfloat16)
-        xh = mixed_ref[rows, 0:INNER].astype(jnp.float32)
+        xh = xh_ref[rows, :].astype(jnp.float32)
         product = dssd.astype(jnp.float32) * (ssd - lanes_ref[1:2, :] * xh)
         top = product.astype(jnp.bfloat16)
         high_ref[rows, :] = top
@@ -441,9 +450,9 @@
 
 
 def backward_kernel(
-    xr_ref, bcd_ref, mixed_ref, slope_ref, dssd_ref, state_ref, delta_ref,
+    xt_ref, mixed_ref, slope_ref, dssd_ref, state_ref, delta_ref,
     taps_ref, heads_ref, lanes_ref, seg_ref,
-    dxr_ref, dbcd_ref, gconv_ref, ghead_ref, gskip_ref,
+    dxt_ref, gconv_ref, ghead_ref, gskip_ref,
     run_ref, dext_ref, cb_ref, dcb_ref, xw_ref, dcarry_ref, high_ref, rest_ref, lane_ref, low_ref,
 ):
     half = GROUP // 2
@@ -462,7 +471,7 @@
     cm_t = cm.astype(jnp.float32).T.astype(jnp.bfloat16)
     cb_ref[...] = ndot(bm, cm)
     dcb_ref[...] = jnp.zeros_like(dcb_ref)
-    raw, dt, cum, late = step_sizes(bcd_ref[:, 2 * STATE :], heads_ref)
+    raw, dt, cum, late = step_sizes(xt_ref[:, CONVW:], heads_ref)
     cum_t = cum.T
     upper = lower_ones(half, True)
     first = lax.broadcasted_iota(jnp.int32, (1, PAIR), 1) < HEADDIM
@@ -545,12 +554,13 @@
     rate = heads_ref[1:2, :]
     ddt = jnp.where(dt > 0.0, sums / dt, 0.0) + dlog * rate
     ddt = ddt / (1.0 + jnp.exp(-raw))
-    dbcd_ref[:, 2 * STATE :] = ddt.astype(jnp.bfloat16)
+    dxt_ref[:, CONVW:] = ddt.astype(jnp.bfloat16)
     ghead_ref[0:1, :] += jnp.sum(ddt, 0, keepdims=True)
     ghead_ref[1:2, :] += jnp.sum(dlog * dt, 0, keepdims=True) * rate
 
-    def conv_piece(at, source):
-        given = source.astype(jnp.float32)
+    def conv_chunk(chunk, carry):
+        at = pl.ds(pl.multiple_of(chunk * PAIR, PAIR), PAIR)
+        given = xt_ref[:, at].astype(jnp.float32)
         total = None
         for tap in range(KCONV):
             moved = dext_ref[KCONV - 1 - tap : KCONV - 1 - tap + GROUP, at]
@@ -559,94 +569,109 @@
             gconv_ref[tap : tap + 1, at] += jnp.sum(given * moved, 0, keepdims=True)
             if tap == KCONV - 1:
                 gconv_ref[KCONV : KCONV + 1, at] += jnp.sum(moved, 0, keepdims=True)
-        return total.astype(jnp.bfloat16)
-
-    def conv_chunk(chunk, carry):
-        at = pl.ds(pl.multiple_of(chunk * PAIR, PAIR), PAIR)
-        dxr_ref[:, at] = conv_piece(at, xr_ref[:, at])
+        dxt_ref[:, at] = total.astype(jnp.bfloat16)
         return carry
 
-    lax.fori_loop(0, INNER // PAIR, conv_chunk, 0)
-    for place in range(2):
-        at = slice(INNER + place * STATE, INNER + (place + 1) * STATE)
-        inner = slice(place * STATE, (place + 1) * STATE)
-        dbcd_ref[:, inner] = conv_piece(at, bcd_ref[:, inner])
+    lax.fori_loop(0, CONVW // PAIR, conv_chunk, 0)
     dext_ref[GROUP:, :] = dext_ref[0:8, :]
 
 
-def run_forward(proj, x, go, wout, taps, heads, lanes, seg):
-    length = x.shape[0]
+def tall_block(width, count=None):
+    if count is None:
+        return pl.BlockSpec((GROUP, width), lambda i: (i, 0))
+    return pl.BlockSpec((GROUP, width), lambda i: (count - 1 - i, 0))
+
+
+def fixed_block(shape):
+    return pl.BlockSpec(shape, lambda i: (0, 0))
+
+
+def kernel_options():
+    return pltpu.CompilerParams(
+        dimension_semantics=("arbitrary",), vmem_limit_bytes=48 * 1024 * 1024
+    )
+
+
+def shape_of(rows, width, kind):
+    return jax.ShapeDtypeStruct((rows, width), kind)
+
+
+def run_scan(xt, taps, heads, lanes):
+    length = xt.shape[0]
     count = length // GROUP
-    tall = lambda width: pl.BlockSpec((GROUP, width), lambda i: (i, 0))
-    fixed = lambda a: pl.BlockSpec(a.shape, lambda i: (0, 0))
     f32, b16 = jnp.float32, jnp.bfloat16
     return pl.pallas_call(
-        forward_kernel,
+        scan_kernel,
         grid=(count,),
         in_specs=[
-            pl.BlockSpec((GROUP, INNER), lambda i: (i, 0)),
-            pl.BlockSpec((GROUP, INNER), lambda i: (i, 1)),
-            pl.BlockSpec((GROUP, TAIL), lambda i: (i, 2 * INNER // TAIL)),
-            tall(WIDE), tall(WIDE), fixed(wout), fixed(taps), fixed(heads), fixed(lanes), fixed(seg),
+            tall_block(XTAIL), fixed_block(taps.shape), fixed_block(heads.shape), fixed_block(lanes.shape),
         ],
         out_specs=[
-            tall(WIDE), tall(INNER), tall(INNER), tall(INNER), tall(CONVW), tall(CONVW),
-            pl.BlockSpec((STATE, INNER), lambda i: (i, 0)), tall(PAIR),
-            pl.BlockSpec((8, INNER), lambda i: (0, 0)),
+            tall_block(CONVW), tall_block(CONVW), pl.BlockSpec((STATE, INNER), lambda i: (i, 0)),
+            tall_block(INNER),
         ],
         out_shape=[
-            jax.ShapeDtypeStruct((length, WIDE), b16),
-            jax.ShapeDtypeStruct((length, INNER), b16),
-            jax.ShapeDtypeStruct((length, INNER), b16),
-            jax.ShapeDtypeStruct((length, INNER), b16),
-            jax.ShapeDtypeStruct((length, CONVW), b16),
-            jax.ShapeDtypeStruct((length, CONVW), f32),
-            jax.ShapeDtypeStruct((count * STATE, INNER), f32),
-            jax.ShapeDtypeStruct((length, PAIR), f32),
-            jax.ShapeDtypeStruct((8, INNER), f32),
+            shape_of(length, CONVW, b16), shape_of(length, CONVW, f32),
+            shape_of(count * STATE, INNER, f32), shape_of(length, INNER, f32),
         ],
         scratch_shapes=[
             pltpu.VMEM((STATE, INNER), f32), pltpu.VMEM((GROUP + 8, CONVW), f32),
-            pltpu.VMEM((GROUP, GROUP), f32), pltpu.VMEM((GROUP, INNER), f32),
+            pltpu.VMEM((GROUP, GROUP), f32),
+        ],
+        compiler_params=kernel_options(),
+        cost_estimate=pl.CostEstimate(flops=25 * 10**9, bytes_accessed=30 * 10**6, transcendentals=10**7),
+        name="scan_forward",
+    )(xt, taps, heads, lanes)
+
+
+def run_gate(z, ssd, mixed, x, go, wout, lanes, seg):
+    length = x.shape[0]
+    f32, b16 = jnp.float32, jnp.bfloat16
+    return pl.pallas_call(
+        gate_kernel,
+        grid=(length // GROUP,),
+        in_specs=[
+            tall_block(INNER), tall_block(INNER), tall_block(INNER), tall_block(WIDE), tall_block(WIDE),
+            fixed_block(wout.shape), fixed_block(lanes.shape), fixed_block(seg.shape),
+        ],
+        out_specs=[
+            tall_block(WIDE), tall_block(INNER), tall_block(INNER), tall_block(INNER), tall_block(PAIR),
+            fixed_block((8, INNER)),
+        ],
+        out_shape=[
+            shape_of(length, WIDE, b16), shape_of(length, INNER, b16), shape_of(length, INNER, b16),
+            shape_of(length, INNER, b16), shape_of(length, PAIR, f32), shape_of(8, INNER, f32),
+        ],
+        scratch_shapes=[
             pltpu.VMEM((GROUP, INNER), f32), pltpu.VMEM((GROUP, INNER), b16),
             pltpu.VMEM((GROUP, INNER), b16),
         ],
-        compiler_params=pltpu.CompilerParams(
-            dimension_semantics=("arbitrary",), vmem_limit_bytes=48 * 1024 * 1024
-        ),
-        cost_estimate=pl.CostEstimate(flops=12 * 10**9, bytes_accessed=40 * 10**6, transcendentals=10**7),
-        name="scan_forward",
-    )(proj, proj, proj, x, go, wout, taps, heads, lanes, seg)
-
-
-def run_backward(proj, mixed, slope, dssd, states, delta, taps, heads, lanes, seg):
-    length = proj.shape[0]
+        compiler_params=kernel_options(),
+        cost_estimate=pl.CostEstimate(flops=20 * 10**9, bytes_accessed=30 * 10**6, transcendentals=10**7),
+        name="gate_both_ways",
+    )(z, ssd, mixed, x, go, wout, lanes, seg)
+
+
+def run_backward(xt, mixed, slope, dssd, states, delta, taps, heads, lanes, seg):
+    length = xt.shape[0]
     count = length // GROUP
-    tall = lambda width: pl.BlockSpec((GROUP, width), lambda i: (count - 1 - i, 0))
-    fixed = lambda a: pl.BlockSpec(a.shape, lambda i: (0, 0))
     f32, b16 = jnp.float32, jnp.bfloat16
     return pl.pallas_call(
         backward_kernel,
         grid=(count,),
         in_specs=[
-            pl.BlockSpec((GROUP, INNER), lambda i: (count - 1 - i, 1)),
-            pl.BlockSpec((GROUP, TAIL), lambda i: (count - 1 - i, 2 * INNER // TAIL)),
-            tall(CONVW), tall(CONVW), tall(INNER),
-            pl.BlockSpec((STATE, INNER), lambda i: (count - 1 - i, 0)), tall(PAIR),
-            fixed(taps), fixed(heads), fixed(lanes), fixed(seg),
+            tall_block(XTAIL, count), tall_block(CONVW, count), tall_block(CONVW, count),
+            tall_block(INNER, count), pl.BlockSpec((STATE, INNER), lambda i: (count - 1 - i, 0)),
+            tall_block(PAIR, count), fixed_block(taps.shape), fixed_block(heads.shape),
+            fixed_block(lanes.shape), fixed_block(seg.shape),
         ],
         out_specs=[
-            tall(INNER), tall(TAIL),
-            pl.BlockSpec((8, CONVW), lambda i: (0, 0)),
-            pl.BlockSpec((8, PAIR), lambda i: (0, 0)),
-            pl.BlockSpec((8, INNER), lambda i: (0, 0)),
+            tall_block(XTAIL, count), fixed_block((8, CONVW)), fixed_block((8, PAIR)),
+            fixed_block((8, INNER)),
         ],
         out_shape=[
-            jax.ShapeDtypeStruct((length, INNER), b16),
-            jax.ShapeDtypeStruct((length, TAIL), b16),
-            jax.ShapeDtypeStruct((8, CONVW), f32),
-            jax.ShapeDtypeStruct((8, PAIR), f32),
-            jax.ShapeDtypeStruct((8, INNER), f32),
+            shape_of(length, XTAIL, b16), shape_of(8, CONVW, f32), shape_of(8, PAIR, f32),
+            shape_of(8, INNER, f32),
         ],
         scratch_shapes=[
             pltpu.VMEM((STATE, INNER), f32), pltpu.VMEM((GROUP + 8, CONVW), f32),
@@ -655,12 +680,10 @@
             pltpu.VMEM((GROUP, INNER), b16), pltpu.VMEM((GROUP, INNER), b16),
             pltpu.VMEM((8, INNER), f32), pltpu.VMEM((STATE, INNER), b16),
         ],
-        compiler_params=pltpu.CompilerParams(
-            dimension_semantics=("arbitrary",), vmem_limit_bytes=48 * 1024 * 1024
-        ),
-        cost_estimate=pl.CostEstimate(flops=12 * 10**9, bytes_accessed=40 * 10**6, transcendentals=10**7),
+        compiler_params=kernel_options(),
+        cost_estimate=pl.CostEstimate(flops=30 * 10**9, bytes_accessed=30 * 10**6, transcendentals=10**7),
         name="scan_backward",
-    )(proj, proj, mixed, slope, dssd, states, delta, taps, heads, lanes, seg)
+    )(xt, mixed, slope, dssd, states, delta, taps, heads, lanes, seg)
 
 
 def head_segments():
@@ -676,174 +699,276 @@
     return (heads, jnp.repeat(skip, HEADDIM))
 
 
-def whole_sequence(xb, cot, wts, dt_bias, rate, skip):
-    gain_in, w_in, taps_bias, gain_gate, w_out = wts
+def input_norm(xb, gain_in):
     xf = xb.astype(jnp.float32)
     r_in = lax.rsqrt(jnp.mean(xf * xf, -1, keepdims=True) + EPS)
-    gain = gain_in.astype(jnp.float32)
-    normed = (xf * r_in * gain).astype(jnp.bfloat16)
-    proj = jnp.dot(normed, w_in, preferred_element_type=jnp.float32).astype(jnp.bfloat16)
-    heads, skip_lanes = head_tables(dt_bias, rate, skip)
-    lanes = jnp.stack([gain_gate.astype(jnp.float32), skip_lanes] + [jnp.zeros_like(skip_lanes)] * 6)
-    seg = head_segments()
-    y, gnorm, dz, dssd, mixed, slope, states, delta, ggain = run_forward(
-        proj, xb, cot, w_out, taps_bias, heads, lanes, seg
-    )
-    grad_wout = tdot(gnorm, cot)
-    grad_wz = tdot(normed, dz)
-    dxr, dbcd, gconv, ghead, gskip = run_backward(
-        proj, mixed, slope, dssd, states, delta, taps_bias, heads, lanes, seg
-    )
-    dnormed = (
-        ndot(dz, w_in[:, :INNER]) + ndot(dxr, w_in[:, INNER : 2 * INNER]) + ndot(dbcd, w_in[:, 2 * INNER :])
-    )
-    scaled = gain * dnormed
+    return (xf, r_in, (xf * r_in * gain_in.astype(jnp.float32)).astype(jnp.bfloat16))
+
+
+def input_grad(xf, r_in, gain_in, dnormed, cot):
+    scaled = gain_in.astype(jnp.float32) * dnormed
     dx = (
         r_in * scaled
         - xf * r_in**3 * jnp.mean(scaled * xf, -1, keepdims=True)
         + cot.astype(jnp.float32)
     ).astype(jnp.bfloat16)
-    grad_gin = jnp.sum(dnormed * xf * r_in, 0)
-    grad_wx = tdot(normed, dxr)
-    grad_wtail = tdot(normed, dbcd)
-    head_terms = jnp.concatenate(
-        [ghead[0, :HEADS], ghead[1, :HEADS], jnp.sum(gskip[0].reshape(HEADS, HEADDIM), -1)]
-    )
-    return (
-        y, dx,
-        (grad_gin, grad_wz, grad_wx, grad_wtail, gconv, jnp.sum(ggain, 0), grad_wout, head_terms),
-    )
-
-
-SMALL = 280
-
-
-def swap_halves(parts):
+    return (dx, jnp.sum(dnormed * xf * r_in, 0))
+
+
+def low_dot(left, right):
+    return jnp.dot(left, right, preferred_element_type=jnp.float32).astype(jnp.bfloat16)
+
+
+SPARE = 1816
+
+
+def grid_place():
+    dp = lax.axis_index("dp")
+    return (dp // 4, lax.rem(dp // 2, 2), lax.rem(dp, 2), lax.axis_index("seq"))
+
+
+def grid_moves(step):
+    high = lax.axis_size("dp") // 4
+    pairs = []
+    for z in range(high):
+        for y in range(2):
+            for c in range(2):
+                for x in range(2):
+                    to = ((z + step[0]) % high, y ^ step[1], c ^ step[2], x ^ step[3])
+                    pairs.append((((z * 2 + y) * 2 + c) * 2 + x, ((to[0] * 2 + to[1]) * 2 + to[2]) * 2 + to[3]))
+    return pairs
+
+
+def grid_send(array, step):
+    return lax.ppermute(array, ("dp", "seq"), grid_moves(step))
+
+
+def pick(array, axes, places):
+    start = [0] * array.ndim
+    size = list(array.shape)
+    for axis, place in zip(axes, places):
+        start[axis] = place
+        size[axis] = 1
+    out = lax.dynamic_slice(array, start, size)
+    return out.reshape([n for axis, n in enumerate(array.shape) if axis not in axes])
+
+
+def add_up(parts):
+    total = parts[0].astype(jnp.float32)
+    for part in parts[1:]:
+        total = total + part.astype(jnp.float32)
+    return total
+
+
+FLIPS = ((0, 1), (1, 0), (1, 1))
+
+
+def reduce_core(parts, kind=jnp.bfloat16):
+    high = lax.axis_size("dp") // 4
+    _, _, c, _ = grid_place()
+    parts = parts.reshape((high, 2, 2, 2, -1) + parts.shape[1:])
+    got = grid_send(pick(parts, (2,), (1 - c,)), (0, 0, 1, 0))
+    return add_up([pick(parts, (2,), (c,)), got]).astype(kind)
+
+
+def plane_parts(parts):
+    _, y, _, x = grid_place()
+    found = [pick(parts, (1, 2), (y, x))]
+    for fy, fx in FLIPS:
+        piece = pick(parts, (1, 2), (y ^ fy, x ^ fx))
+        found.append(grid_send(piece, (0, fy, 0, fx)))
+    return found
+
+
+def reduce_plane(parts, kind=jnp.bfloat16):
+    return add_up(plane_parts(parts)).astype(kind)
+
+
+def reduce_line(parts):
+    high = lax.axis_size("dp") // 4
+    z, _, _, _ = grid_place()
+    found = [pick(parts, (0,), (z,))]
+    for hop in range(1, high):
+        piece = pick(parts, (0,), (lax.rem(z + hop, high),))
+        found.append(grid_send(piece, (hop, 0, 0, 0)))
+    return add_up(found)
+
+
+def place_in(array, axis, places, pieces):
+    for place, piece in zip(places, pieces):
+        array = lax.dynamic_update_slice_in_dim(array, jnp.expand_dims(piece, axis), place, axis)
+    return array
+
+
+def gather_line(own):
+    high = lax.axis_size("dp") // 4
+    z, _, _, _ = grid_place()
+    places = [z] + [lax.rem(z + high - hop, high) for hop in range(1, high)]
+    pieces = [own] + [grid_send(own, (hop, 0, 0, 0)) for hop in range(1, high)]
+    return place_in(jnp.zeros((high,) + own.shape, own.dtype), 0, places, pieces)
+
+
+def gather_plane(tall):
+    return [tall] + [grid_send(tall, (0, fy, 0, fx)) for fy, fx in FLIPS]
+
+
+def gather_core(pieces, cuts):
+    _, y, c, x = grid_place()
+    high, rows, _ = pieces[0].shape
+    found = []
+    for cut in cuts:
+        shape = (high, 2, 2, 2, len(cut) * rows, cut[0].stop - cut[0].start)
+        found.append(jnp.zeros(shape, pieces[0].dtype))
+    for (fy, fx), piece in zip(((0, 0),) + FLIPS, pieces):
+        other = grid_send(piece, (0, 0, 1, 0))
+        for core, value in ((c, piece), (1 - c, other)):
+            for k, cut in enumerate(cuts):
+                for j, columns in enumerate(cut):
+                    part = value[:, :, columns].reshape(high, 1, 1, 1, rows, -1)
+                    start = (0, y ^ fy, core, x ^ fx, j * rows, 0)
+                    found[k] = lax.dynamic_update_slice(found[k], part, start)
+    return [full.reshape((-1, full.shape[-1])) for full in found]
+
+
+def gather_small(own):
+    high = lax.axis_size("dp") // 4
+    z, y, c, x = grid_place()
+    flat = own.reshape(1, -1)
+    held = jnp.concatenate([flat] + [grid_send(flat, (hop, 0, 0, 0)) for hop in range(1, high)], 0)
+    held = jnp.concatenate([held] + [grid_send(held, (0, fy, 0, fx)) for fy, fx in FLIPS], 0)
+    held = jnp.concatenate([held, grid_send(held, (0, 0, 1, 0))], 0)
+    owner = lax.broadcasted_iota(jnp.int32, (high * 8, high * 8), 0)
+    slot = lax.broadcasted_iota(jnp.int32, (high * 8, high * 8), 1)
+    hop, flip, core = slot % high, slot // high % 4, slot // (4 * high)
+    source = ((z + high - hop) % high * 2 + (y ^ (flip // 2))) * 2 + (c ^ core)
+    match = owner == source * 2 + (x ^ (flip % 2))
+    order = match.astype(own.dtype)
+    return jnp.dot(order, held, preferred_element_type=jnp.float32).reshape((-1,) + own.shape)
+
+
+def reduce_all(parts, kind=jnp.bfloat16):
+    return reduce_line(reduce_plane(reduce_core(parts, kind), kind))
+
+
+def after(value, *others):
+    return lax.optimization_barrier((value,) + others)[0]
+
+
+def swap_send(parts):
     place = lax.axis_index("seq")
-    count = lax.axis_size("seq")
-    size = parts.shape[1]
-    whole = jnp.zeros((count * size,) + parts.shape[2:], parts.dtype)
+    return grid_send(lax.dynamic_index_in_dim(parts, 1 - place, 0, False), (0, 0, 0, 1))
+
+
+def swap_join(parts, got):
+    place = lax.axis_index("seq")
     own = lax.dynamic_index_in_dim(parts, place, 0, False)
-    whole = lax.dynamic_update_slice_in_dim(whole, own, place * size, 0)
-    for hop in range(1, count):
-        there = lax.rem(place + hop, count)
-        source = lax.rem(place + count - hop, count)
-        sent = lax.dynamic_index_in_dim(parts, there, 0, False)
-        got = lax.ppermute(sent, "seq", [(i, (i + hop) % count) for i in range(count)])
-        whole = lax.dynamic_update_slice_in_dim(whole, got, source * size, 0)
-    return whole
-
-
-def gather_weights(norm_gain, in_weight, conv_weight, conv_bias, gate_gain, out_weight):
-    devices = lax.axis_size(("dp", "seq"))
-    rows = in_weight.shape[0]
-    small = jnp.concatenate([norm_gain, conv_weight.reshape(-1), conv_bias, gate_gain])
-    sizes = (norm_gain.size, conv_weight.size, conv_bias.size, gate_gain.size)
-    line = jnp.pad(small[None], ((0, rows - 1), (0, WIDE - SMALL - small.size)))
-    pieces = [in_weight[:, k * WIDE : (k + 1) * WIDE] for k in range(4)]
-    pieces.append(jnp.concatenate([in_weight[:, 4 * WIDE :], line], 1))
-    pieces.append(out_weight)
-    packed = jnp.concatenate(pieces, 0)
-    full = lax.all_gather(packed, ("dp", "seq"), axis=0)
-    columns = [
-        full[:, k * rows : (k + 1) * rows].reshape(devices * rows, WIDE) for k in range(4)
-    ]
-    last = full[:, 4 * rows : 5 * rows].reshape(devices * rows, WIDE)[:, :SMALL]
-    columns.append(jnp.pad(last, ((0, 0), (0, TAIL - SMALL))))
-    w_in = jnp.concatenate(columns, 1)
-    w_out = full[:, 5 * rows :].reshape(devices * out_weight.shape[0], WIDE)
-    table = full[:, 4 * rows, SMALL : SMALL + small.size]
-    a, b, c = sizes[0], sizes[0] + sizes[1], sizes[0] + sizes[1] + sizes[2]
-    gain_in = table[:, :a].reshape(-1)
-    taps = table[:, a:b].reshape(devices, KCONV, -1).transpose(1, 0, 2).reshape(KCONV, -1)
-    bias = table[:, b:c].reshape(1, -1)
-    gain_gate = table[:, c:].reshape(-1)
-    taps_bias = jnp.pad(
-        jnp.concatenate([taps, bias], 0).astype(jnp.float32), ((0, 7 - KCONV), (0, 0))
-    )
-    return (gain_in, w_in, taps_bias, gain_gate, w_out)
-
-
-def by_owner(grad, devices):
-    return grad.astype(jnp.bfloat16).reshape(devices, -1, grad.shape[-1])
-
-
-def shards(
+    return jnp.concatenate([jnp.where(place == 0, own, got), jnp.where(place == 0, got, own)], 0)
+
+
+def swap_halves(parts, *guards):
+    return swap_join(parts, after(swap_send(parts), *guards))
+
+
+def pack_small(gain, taps, bias, gate, heads):
+    lines = [taps, bias[None], gate[None], gain[None], heads[None]]
+    lines = [jnp.pad(line, ((0, 0), (0, PAIR - line.shape[1]))) for line in lines]
+    return jnp.concatenate(lines, 0)
+
+
+def unpack_small(block, sizes):
+    taps = block[..., :KCONV, : sizes[0]]
+    return [taps] + [block[..., KCONV + k, :size] for k, size in enumerate(sizes[1:])]
+
+
+def fast_shards(
     x_in, grad_out, norm_gain, in_weight, conv_weight, conv_bias, gate_gain, out_weight, dt_bias, a_log, skip
 ):
-    if x_in.shape[0] != lax.axis_size("seq"):
-        return shards_general(
-            x_in, grad_out, norm_gain, in_weight, conv_weight, conv_bias, gate_gain, out_weight,
-            dt_bias, a_log, skip,
-        )
     rate = -jnp.exp(a_log)
     devices = lax.axis_size(("dp", "seq"))
     micro, _, length, _ = x_in.shape
     rows = in_weight.shape[0]
-    wts = gather_weights(norm_gain, in_weight, conv_weight, conv_bias, gate_gain, out_weight)
+    sizes = (conv_weight.shape[1], conv_bias.size, gate_gain.size, norm_gain.size)
+    first = jnp.pad(in_weight[:, INNER:], ((0, 0), (0, XTAIL - SPARE)))
+    second = jnp.concatenate([in_weight[:, :INNER], out_weight[:rows], out_weight[rows:]], 1)
+    small = pack_small(norm_gain, conv_weight, conv_bias, gate_gain, jnp.zeros((8,), norm_gain.dtype))
+
+    line_first = gather_line(first)
     xb = swap_halves(x_in[:, 0])
-    cot = swap_halves(grad_out[:, 0])
-    y, dx, terms = whole_sequence(xb, cot, wts, dt_bias, rate, skip)
-    y_out = swap_halves(y.reshape(micro, length, WIDE)).reshape(x_in.shape)
-    dx_in = swap_halves(dx.reshape(micro, length, WIDE)).reshape(x_in.shape)
-    grad_gin, grad_wz, grad_wx, grad_wtail, gconv, ggain, grad_wout, head_terms = terms
-    early = jnp.concatenate(
-        [
-            by_owner(grad_wz[:, :WIDE], devices),
-            by_owner(grad_wz[:, WIDE:], devices),
-            by_owner(grad_wout, devices),
-        ],
-        1,
-    )
-    small = jnp.concatenate(
-        [
-            grad_gin.reshape(devices, -1),
-            gconv[:KCONV].reshape(KCONV, devices, -1).transpose(1, 0, 2).reshape(devices, -1),
-            gconv[KCONV].reshape(devices, -1),
-            ggain.reshape(devices, -1),
-            jnp.broadcast_to(head_terms, (devices, 3 * HEADS)),
-        ],
-        1,
-    ).astype(jnp.bfloat16)
-    line = jnp.pad(small[:, None], ((0, 0), (0, rows - 1), (0, WIDE - SMALL - small.shape[1])))
-    late = jnp.concatenate(
-        [
-            by_owner(grad_wx[:, :WIDE], devices),
-            by_owner(grad_wx[:, WIDE:], devices),
-            jnp.concatenate([by_owner(grad_wtail[:, :SMALL], devices), line], 2),
-        ],
-        1,
-    )
-    early = reduce_owned(early).astype(jnp.float32)
-    late = reduce_owned(late).astype(jnp.float32)
-    own_in = jnp.concatenate(
-        [early[:rows], early[rows : 2 * rows], late[:rows], late[rows : 2 * rows], late[2 * rows :, :SMALL]],
-        1,
-    )
-    own = late[2 * rows, SMALL : SMALL + small.shape[1]]
-    cuts = [norm_gain.size, conv_weight.size, conv_bias.size, gate_gain.size, HEADS, HEADS, HEADS]
-    found = []
-    at = 0
-    for size in cuts:
-        found.append(own[at : at + size])
-        at += size
+    small = gather_small(small)
+    plane_first = gather_plane(line_first)
+    line_second = gather_line(after(second, xb))
+    (w_xt,) = gather_core(plane_first, [[slice(0, XTAIL)]])
+    plane_second = gather_plane(after(line_second, *plane_first))
+
+    taps, bias, gate, gain_in = unpack_small(small, sizes)
+    gain_in = gain_in.reshape(-1)
+    gate = gate.reshape(-1).astype(jnp.float32)
+    taps = taps.transpose(1, 0, 2).reshape(KCONV, -1)
+    taps_bias = jnp.concatenate([taps, bias.reshape(1, -1)], 0).astype(jnp.float32)
+    taps_bias = jnp.pad(taps_bias, ((0, 7 - KCONV), (0, 0)))
+    xf, r_in, normed = input_norm(xb, gain_in)
+    heads, skip_lanes = head_tables(dt_bias, rate, skip)
+    lanes = jnp.stack([gate, skip_lanes] + [jnp.zeros_like(skip_lanes)] * 6)
+    seg = head_segments()
+    xt = low_dot(normed, w_xt)
+    mixed, slope, states, ssd = run_scan(xt, taps_bias, heads, lanes)
+    cot = swap_halves(after(grad_out[:, 0], *plane_first), ssd)
+
+    w_z, w_out = gather_core(
+        plane_second,
+        [[slice(0, INNER)], [slice(INNER, INNER + WIDE), slice(INNER + WIDE, 2 * INNER)]],
+    )
+    z = low_dot(normed, w_z)
+    y, gnorm, dz, dssd, delta, ggain = run_gate(z, ssd, mixed, xb, cot, w_out, lanes, seg)
+    grad_wout = tdot(gnorm, cot).astype(jnp.bfloat16).reshape(devices, 2, rows, WIDE)
+    grad_wz = tdot(normed, dz).astype(jnp.bfloat16)
+    early = [grad_wz] + [grad_wout[:, k].reshape(WIDE, WIDE) for k in range(2)]
+    early = reduce_core(jnp.concatenate(early, 1))
+    dssd = after(dssd, early)
+    y_got = swap_send(y.reshape(micro, length, WIDE))
+    early = plane_parts(early)
+    dxt, gconv, ghead, gskip = run_backward(
+        xt, mixed, slope, dssd, states, delta, taps_bias, heads, lanes, seg
+    )
+    dxt, y_got = lax.optimization_barrier((dxt, y_got) + tuple(early))[:2]
+    y_out = swap_join(y.reshape(micro, length, WIDE), y_got).reshape(x_in.shape)
+    grad_wxt = tdot(normed, dxt).astype(jnp.bfloat16)
+    late = reduce_core(grad_wxt)
+    dnormed = ndot(after(dz, late), w_z) + ndot(after(dxt, late), w_xt)
+    late = plane_parts(late)
+    dx, grad_gin = input_grad(xf, r_in, gain_in, dnormed, cot)
+    dx_in = swap_halves(after(dx.reshape(micro, length, WIDE), *late)).reshape(x_in.shape)
+    late_pieces = late
+    both = [add_up(parts).astype(jnp.bfloat16) for parts in (early, late)]
+    both = reduce_line(jnp.concatenate(both, -1))
+    early, late = both[:, : 2 * INNER], both[:, 2 * INNER :]
+    head_terms = jnp.concatenate(
+        [ghead[0, :HEADS], ghead[1, :HEADS], jnp.sum(gskip[0].reshape(HEADS, HEADDIM), -1)]
+    )
+    grad_gin = after(grad_gin, *late_pieces)
+    tiny = jax.vmap(pack_small)(
+        grad_gin.reshape(devices, -1),
+        gconv[:KCONV].reshape(KCONV, devices, -1).transpose(1, 0, 2),
+        gconv[KCONV].reshape(devices, -1),
+        jnp.sum(ggain, 0).reshape(devices, -1),
+        jnp.broadcast_to(head_terms, (devices, 3 * HEADS)),
+    )
+    own = reduce_all(tiny.reshape(devices * (KCONV + 4), PAIR), jnp.float32)
+    own_in = jnp.concatenate([early[:, :INNER], late[:, :SPARE]], 1)
+    own_out = jnp.concatenate([early[:, INNER : INNER + WIDE], early[:, INNER + WIDE :]], 0)
+    found = unpack_small(own, sizes)
+    heads_sum = own[KCONV + 3]
     return (
-        y_out,
-        dx_in,
-        found[0],
-        own_in,
-        found[1].reshape(conv_weight.shape),
-        found[2],
-        found[3],
-        early[2 * rows :],
-        found[4],
-        found[5],
-        found[6],
-    )
-
-
-def reduce_owned(parts):
-    return lax.psum_scatter(parts, ("dp", "seq"), scatter_dimension=0, tiled=False)
+        y_out, dx_in, found[3], own_in, found[0], found[1], found[2], own_out,
+        heads_sum[:HEADS], heads_sum[HEADS : 2 * HEADS], heads_sum[2 * HEADS : 3 * HEADS],
+    )
+
+
+def shards(x_in, *rest):
+    dp, seq = lax.axis_size("dp"), lax.axis_size("seq")
+    if x_in.shape[0] == seq == 2 and dp % 4 == 0 and rest[1].size * dp * seq == WIDE:
+        return fast_shards(x_in, *rest)
+    return shards_general(x_in, *rest)
 
 
 def shards_general(

time: 485 us -> 329 us (0.68)
  waiting for transfers between devices: 261 us -> 98.7 us
  starting transfers between devices: 4.3 us -> 47.6 us
  local copies, waits for them, and re-layouts: 68.3 us -> 29 us
  between operations: 14.4 us -> 2.29 us
  Pallas kernels: 86.1 us -> 91.9 us
    reduce_scatter x2 -> x0, waiting for transfers between devices: 154 us -> none  [reduce_owned(): lax.psum_scatter(parts, ('dp', 'seq'), scatter_dimension=0, tiled=False)]
    ppermute x4 -> x49, starting transfers between devices: 4.18 us -> 47.6 us  [grid_send(): return lax.ppermute(array, ('dp', 'seq'), grid_moves(step))]
    all_gather x1 -> x0, waiting for transfers between devices: 37.3 us -> none  [gather_weights(): full = lax.all_gather(packed, ('dp', 'seq'), axis=0)]
    ppermute x4 -> x49, waiting for transfers between devices: 69.4 us -> 98.7 us  [grid_send(): return lax.ppermute(array, ('dp', 'seq'), grid_moves(step))]
    slice x19 -> x17, local copies, waits for them, and re-layouts: 22.3 us -> 3.18 us  [the longest x1 0.9 us: fast_shards(): first = jnp.pad(in_weight[:, INNER:], ((0, 0), (0, XTAIL - SPARE)))]
    unnamed x83 -> x49, local copies, waits for them, and re-layouts: 16.2 us -> 7.48 us
    reshape x11 -> x10, local copies, waits for them, and re-layouts: 11 us -> 2.8 us  [the longest x7 2.56 us: pick(): out.reshape([n for axis, n in enumerate(array.shape) if axis not in axes])]
    pad x0 -> x11, local copies, waits for them, and re-layouts: none -> 6.58 us  [the longest x10 6.57 us: pack_small(): jnp.pad(line, ((0, 0), (0, PAIR - line.shape[1])))]
  transfers between devices with their start and end apart: 7 -> 49, of which waited for: 7 -> 15; matrix products, arithmetic and copies ran while one was open for 7% -> 11% of each run, Pallas kernels for 0% -> 19%
where the time goes in v2:
time: 329 us; the launch traced here: 323 us
  waiting for transfers between devices  98.7 us (30%)
  Pallas kernels  91.9 us (28%)
  starting transfers between devices  47.6 us (14%)
  matrix products  35.4 us (11%)
  local copies, waits for them, and re-layouts  29 us (9%)
  other arithmetic  18.5 us (6%)
    ppermute x49, waiting for transfers between devices, grid_send(): return lax.ppermute(array, ('dp', 'seq'), grid_moves(step))  98.7 us
    ppermute x49, starting transfers between devices, grid_send(): return lax.ppermute(array, ('dp', 'seq'), grid_moves(step))  47.6 us
    pallas_call x1, Pallas kernels, run_backward(): pl.pallas_call(backward_kernel, grid=(count,), in_specs=[tall_block(XTAIL...  38.5 us
    pallas_call x1, Pallas kernels, run_gate(): pl.pallas_call(gate_kernel, grid=(length // GROUP,), in_specs=[tall_block...  30.1 us
    pallas_call x1, Pallas kernels, run_scan(): pl.pallas_call(scan_kernel, grid=(count,), in_specs=[tall_block(XTAIL), f...  23.3 us
    dot_general x3, matrix products, tdot(): lax.dot_general(left, right, (((0,), (0,)), ((), ())), preferred_element_...  13.9 us
    dot_general x2, matrix products, low_dot(): jnp.dot(left, right, preferred_element_type=jnp.float32)  10.9 us
    dot_general x2, matrix products, ndot(): lax.dot_general(left, right, (((1,), (1,)), ((), ())), preferred_element_...  10.4 us
  transfers between devices with their start and end apart: 49, of which 15 were waited for; matrix products, arithmetic and copies ran while one was open for 11% of the time, Pallas kernels for 19%

profile of v2, /device:TPU:8, one launch (start us, length us, event | category | flops | bytes accessed | tf_op | source)
XLA Modules:
  0.0 323.4 jit_solution(13155788303955501486)
XLA Ops:
  3.5 3.0 collective-permute-start.2
  6.5 2.5 collective-permute-start.1
  13.4 2.1 dynamic-slice_bitcast_fusion.5
  16.9 2.5 collective-permute-start.6
  21.5 1.9 collective-permute-start.13
  31.2 21.8 %collective-permute-done.16 = bf16[4,24,1920]{2,1,0:T(8,128)(2,1)S(1)} collective-permute-done((bf16[4,24,1920]{2,1,0:T(8,128)(2,1)S(1)}, bf16[4,24,1920]{2,1,0:T(8,128)(2,1)S(1)}, u32[]{:S(2)}, u32[]{:S(2)}) %collective-permute-start.16) | collective-permute-done | bytes 368672 | tf_op jit(solution)/shard_map/ppermute | solution.py:743
  53.0 4.0 %collective-permute-done.14 = bf16[4,24,1920]{2,1,0:T(8,128)(2,1)S(1)} collective-permute-done((bf16[4,24,1920]{2,1,0:T(8,128)(2,1)S(1)}, bf16[4,24,1920]{2,1,0:T(8,128)(2,1)S(1)}, u32[]{:S(2)}, u32[]{:S(2)}) %collective-permute-start.14) | collective-permute-done | bytes 368672 | tf_op jit(solution)/shard_map/ppermute | solution.py:743
  60.6 2.4 collective-permute-start.10
  63.9 2.6 collective-permute-start.8
  68.2 5.9 %convolution_convert_fusion.xt_ref = bf16[1024,1920]{1,0:T(8,128)(2,1)} fusion(bf16[768,1920]{1,0:T(8,128)(2,1)S(1)} %bitcast.359, f32[768]{0:T(1024)S(1)} %mul.76, f32[1024]{0:T(1024)S(1)} %get-tuple-element.136, bf16[512,768]{1,0:T(8,128)(2,1)S(1)} %get-tuple-element.112, bf16[512,768]{1,0:T(8,128)(2,1)S(1)} %get-tuple-element.111), kind=kOutput, calls=%fused_computation.8 | convolution fusion | flops 3027369984 | bytes 8461312 | tf_op jit(solution)/shard_map/dot_general | solution.py:719
  74.1 23.3 %scan_forward.1 = (bf16[1024,1792]{1,0:T(8,128)(2,1)}, f32[1024,1792]{1,0:T(8,128)}, f32[512,1536]{1,0:T(8,128)S(1)}, f32[1024,1536]{1,0:T(8,128)}) custom-call(bf16[1024,1920]{1,0:T(8,128)(2,1)} %convolution_convert_fusion.xt_ref, f32[8,1792]{1,0:T(8,128)S(1)} %select_maximum_fusion.taps_ref, f32[8,128]{1,0:T(8,128)S(1)} %maximum_maximum_fusion.1.heads_ref, ...), custom_call_target="tpu_custom_call" | custom-call | flops 24999999488 | bytes 30000000 | tf_op jit(solution)/shard_map/scan_forward/pallas_call | solution.py:603
  101.9 12.8 %collective-permute-done.22 = bf16[4,24,3072]{2,1,0:T(8,128)(2,1)S(1)} collective-permute-done((bf16[4,24,3072]{2,1,0:T(8,128)(2,1)S(1)}, bf16[4,24,3072]{2,1,0:T(8,128)(2,1)S(1)}, u32[]{:S(2)}, u32[]{:S(2)}) %collective-permute-start.22) | collective-permute-done | bytes 589856 | tf_op jit(solution)/shard_map/ppermute | solution.py:743
  114.8 11.3 %collective-permute-done.20 = bf16[4,24,3072]{2,1,0:T(8,128)(2,1)S(1)} collective-permute-done((bf16[4,24,3072]{2,1,0:T(8,128)(2,1)S(1)}, bf16[4,24,3072]{2,1,0:T(8,128)(2,1)S(1)}, u32[]{:S(2)}, u32[]{:S(2)}) %collective-permute-start.20) | collective-permute-done | bytes 589856 | tf_op jit(solution)/shard_map/ppermute | solution.py:743
  126.7 2.1 collective-permute-done.19
  129.1 5.0 %convolution_convert_fusion.1.z_ref = bf16[1024,1536]{1,0:T(8,128)(2,1)} fusion(bf16[768,1536]{1,0:T(8,128)(2,1)S(1)} %bitcast.361, f32[768]{0:T(1024)S(1)} %mul.76, f32[1024]{0:T(1024)S(1)} %get-tuple-element.136, bf16[512,768]{1,0:T(8,128)(2,1)S(1)} %get-tuple-element.112, bf16[512,768]{1,0:T(8,128)(2,1)S(1)} %get-tuple-element.111), kind=kOutput, calls=%fused_computation.9 | convolution fusion | flops 2422996992 | bytes 7085056 | tf_op jit(solution)/shard_map/dot_general | solution.py:719
  135.7 30.1 %gate_both_ways.1 = (bf16[1024,768]{1,0:T(8,128)(2,1)S(1)}, bf16[1024,1536]{1,0:T(8,128)(2,1)}, bf16[1024,1536]{1,0:T(8,128)(2,1)}, bf16[1024,1536]{1,0:T(8,128)...) custom-call(bf16[1024,1536]{1,0:T(8,128)(2,1)} %convolution_convert_fusion.1.z_ref, ...), custom_call_target="tpu_custom_call" | custom-call | flops 20000000000 | bytes 30000000 | tf_op jit(solution)/shard_map/gate_both_ways/pallas_call | solution.py:630
  165.8 4.6 %convolution_convert_fusion.2 = bf16[1536,768]{1,0:T(8,128)(2,1)S(1)} fusion(bf16[1024,1536]{1,0:T(8,128)(2,1)} %get-tuple-element.46, bf16[512,768]{1,0:T(8,128)(2,1)S(1)} %get-tuple-element.110, bf16[512,768]{1,0:T(8,128)(2,1)S(1)} %get-tuple-element.109), kind=kOutput, calls=%fused_computation.10 | convolution fusion | flops 2420244480 | bytes 7077888 | tf_op jit(solution)/shard_map/dot_general | solution.py:50
  172.3 3.1 convolution_convert_fusion.3
  177.5 3.3 %collective-permute-done.29 = bf16[4,2,2,24,3072]{4,3,2,1,0:T(8,128)(2,1)S(1)} collective-permute-done((bf16[4,2,2,24,3072]{4,3,2,1,0:T(8,128)(2,1)S(1)}, bf16[4,2,2,24,3072]{4,3,2,1,0:T(8,128)(2,1)S(1)}, u32[]{:S(2)}, u32[]{:S(2)}) %collective-permute-start.29) | collective-permute-done | bytes 2359328 | tf_op jit(solution)/shard_map/ppermute | solution.py:743
  182.9 1.7 collective-permute-start.33
  185.4 38.5 %scan_backward.1 = (bf16[1024,1920]{1,0:T(8,128)(2,1)}, f32[8,1792]{1,0:T(8,128)S(1)}, f32[8,128]{1,0:T(8,128)S(1)}, f32[8,1536]{1,0:T(8,128)S(1)}) custom-call(bf16[1024,1920]{1,0:T(8,128)(2,1)} %convolution_convert_fusion.xt_ref, bf16[1024,1792]{1,0:T(8,128)(2,1)} %get-tuple-element.39.xh_ref.mixed_ref, f32[1024,1792]{1,0:T(8,128)} %get-tuple-element.43.slope_ref, ...), custom_call_target="tpu_custom_call" | custom-call | flops 30000001024 | bytes 30000000 | tf_op jit(solution)/shard_map/scan_backward/pallas_call | solution.py:659
  225.2 6.3 %convolution_convert_fusion.4 = bf16[768,1920]{1,0:T(8,128)(2,1)S(1)} fusion(bf16[1024,1920]{1,0:T(8,128)(2,1)} %get-tuple-element.54, f32[768]{0:T(1024)S(1)} %mul.76, f32[1024]{0:T(1024)S(1)} %get-tuple-element.136, bf16[512,768]{1,0:T(8,128)(2,1)S(1)} %get-tuple-element.112, bf16[512,768]{1,0:T(8,128)(2,1)S(1)} %get-tuple-element.111), kind=kOutput, calls=%fused_computation.12 | convolution fusion | flops 3026878464 | bytes 8461312 | tf_op jit(solution)/shard_map/dot_general | solution.py:50
  242.3 5.7 %fusion.115 = f32[1024,768]{1,0:T(8,128)S(1)} fusion(bf16[1024,1920]{1,0:T(8,128)(2,1)} %get-tuple-element.54, bf16[768,1920]{1,0:T(8,128)(2,1)S(1)} %bitcast.360), kind=kOutput, calls=%fused_computation.273 | convolution fusion | flops 3019898880 | bytes 10027008 | tf_op jit(solution)/shard_map/dot_general | solution.py:56
  249.0 1.7 collective-permute-start.37
  251.6 4.7 %fusion.10 = (f32[768]{0:T(1024)S(1)}, f32[1024]{0:T(1024)S(1)}, f32[1024,768]{1,0:T(8,128)}) fusion(f32[1024]{0:T(1024)S(1)} %get-tuple-element.136, bf16[512,768]{1,0:T(8,128)(2,1)S(1)} %copy-done.3, bf16[512,768]{1,0:T(8,128)(2,1)S(1)} %get-tuple-element.111, f32[768]{0:T(1024)S(1)} %mul.76, f32[1024,768]{1,0:T(8,128)S(1)} %fusion.115, ...), kind=kOutput, calls=%fused_computation.22 | convolution fusion | flops 2424568064 | bytes 13383680 | tf_op jit(solution)/shard_map/dot_general | solution.py:56
  256.3 3.2 collective-permute-done.35
  259.5 8.3 %collective-permute-done.37 = bf16[4,24,1920]{2,1,0:T(8,128)(2,1)S(1)} collective-permute-done((bf16[4,24,1920]{2,1,0:T(8,128)(2,1)S(1)}, bf16[4,24,1920]{2,1,0:T(8,128)(2,1)S(1)}, u32[]{:S(2)}, u32[]{:S(2)}) %collective-permute-start.37) | collective-permute-done | bytes 368672 | tf_op jit(solution)/shard_map/ppermute | solution.py:743
  275.1 3.5 %fusion.7 = bf16[1024,768]{1,0:T(8,128)(2,1)S(1)} fusion(f32[1024,768]{1,0:T(8,128)} %get-tuple-element.137, f32[1024]{0:T(1024)S(1)} %broadcast_multiply_fusion, f32[1024]{0:T(1024)S(1)} %get-tuple-element.135, f32[768]{0:T(1024)S(1)} %mul.76, f32[1024]{0:T(1024)S(1)} %get-tuple-element.136, bf16[512,768]{1,0:T(8,128)(2,1)S(1)} %copy-done.7, ...), kind=kLoop, calls=%fused_computation.19 | loop fusion | flops 11796480 | bytes 7879680 | tf_op jit(solution)/shard_map/convert_element_type | solution.py:714
  282.9 1.9 collective-permute-start.47
  288.2 15.3 %collective-permute-done.43 = f32[8,128]{1,0:T(8,128)S(1)} collective-permute-done((f32[8,128]{1,0:T(8,128)S(1)}, f32[8,128]{1,0:T(8,128)S(1)}, u32[]{:S(2)}, u32[]{:S(2)}) %collective-permute-start.43) | collective-permute-done | bytes 4128 | tf_op jit(solution)/shard_map/ppermute | solution.py:743
  307.0 3.4 %collective-permute-done.48 = bf16[24,4992]{1,0:T(8,128)(2,1)S(1)} collective-permute-done((bf16[24,4992]{1,0:T(8,128)(2,1)S(1)}, bf16[24,4992]{1,0:T(8,128)(2,1)S(1)}, u32[]{:S(2)}, u32[]{:S(2)}) %collective-permute-start.48) | collective-permute-done | bytes 239648 | tf_op jit(solution)/shard_map/ppermute | solution.py:743
  311.9 9.7 %collective-permute-done.38 = bf16[512,768]{1,0:T(8,128)(2,1)S(1)} collective-permute-done((bf16[512,768]{1,0:T(8,128)(2,1)S(1)}, bf16[512,768]{1,0:T(8,128)(2,1)S(1)}, u32[]{:S(2)}, u32[]{:S(2)}) %collective-permute-start.38) | collective-permute-done | bytes 786464 | tf_op jit(solution)/shard_map/ppermute | solution.py:743
  (276 shorter events, 73.0 us)
Async XLA Ops:
  3.4 13.4 %collective-permute-start.3 = (bf16[1,1024]{1,0:T(2,128)(2,1)S(1)}, bf16[1,1024]{1,0:T(2,128)(2,1)S(1)}, u32[]{:S(2)}, u32[]{:S(2)}) collective-permute-start(bf16[1,1024]{1,0:T(2,128)(2,1)S(1)} %bitcast.380), channel_id=1, source_target_pairs={{0,24},{1,25},{2,26},{3,27},{4,28},{5,29},{6,30},{7,31},{8,0},{9,1... | collective-permute-start | bytes 6152 | tf_op jit(solution)/shard_map/ppermute | solution.py:743
  3.5 13.3 %collective-permute-start.2 = (bf16[1,1024]{1,0:T(2,128)(2,1)S(1)}, bf16[1,1024]{1,0:T(2,128)(2,1)S(1)}, u32[]{:S(2)}, u32[]{:S(2)}) collective-permute-start(bf16[1,1024]{1,0:T(2,128)(2,1)S(1)} %bitcast.381), channel_id=1, source_target_pairs={{0,16},{1,17},{2,18},{3,19},{4,20},{5,21},{6,22},{7,23},{8,24},{9,... | collective-permute-start | bytes 6152 | tf_op jit(solution)/shard_map/ppermute | solution.py:743
  6.5 10.3 %collective-permute-start.1 = (bf16[1,1024]{1,0:T(2,128)(2,1)S(1)}, bf16[1,1024]{1,0:T(2,128)(2,1)S(1)}, u32[]{:S(2)}, u32[]{:S(2)}) collective-permute-start(bf16[1,1024]{1,0:T(2,128)(2,1)S(1)} %bitcast.382), channel_id=1, source_target_pairs={{0,8},{1,9},{2,10},{3,11},{4,12},{5,13},{6,14},{7,15},{8,16},{9,17... | collective-permute-start | bytes 6152 | tf_op jit(solution)/shard_map/ppermute | solution.py:743
  9.9 17.2 %collective-permute-start.12 = (bf16[24,1920]{1,0:T(8,128)(2,1)S(1)}, bf16[24,1920]{1,0:T(8,128)(2,1)S(1)}, u32[]{:S(2)}, u32[]{:S(2)}) collective-permute-start(bf16[24,1920]{1,0:T(8,128)(2,1)S(1)} %pad.65), channel_id=1, source_target_pairs={{0,16},{1,17},{2,18},{3,19},{4,20},{5,21},{6,22},{7,23},{8,24},{9,... | collective-permute-start | bytes 276488 | tf_op jit(solution)/shard_map/ppermute | solution.py:743
  10.9 16.2 %collective-permute-start.11 = (bf16[24,1920]{1,0:T(8,128)(2,1)S(1)}, bf16[24,1920]{1,0:T(8,128)(2,1)S(1)}, u32[]{:S(2)}, u32[]{:S(2)}) collective-permute-start(bf16[24,1920]{1,0:T(8,128)(2,1)S(1)} %pad.65), channel_id=1, source_target_pairs={{0,8},{1,9},{2,10},{3,11},{4,12},{5,13},{6,14},{7,15},{8,16},{9,17... | collective-permute-start | bytes 276488 | tf_op jit(solution)/shard_map/ppermute | solution.py:743
  23.4 35.8 %collective-permute-start = (bf16[512,768]{1,0:T(8,128)(2,1)}, bf16[512,768]{1,0:T(8,128)(2,1)}, u32[]{:S(2)}, u32[]{:S(2)}) collective-permute-start(bf16[512,768]{1,0:T(8,128)(2,1)} %dynamic-slice_bitcast_fusion.5), channel_id=1, source_target_pairs={{0,1},{1,0},{2,3},{3,2},{4,5},{5,4},{6,7},{7,6},{8,9},{9,8},{10,11... | collective-permute-start | bytes 2359304 | tf_op jit(solution)/shard_map/ppermute | solution.py:743
  27.2 31.9 %collective-permute-start.24 = (bf16[4,24,1920]{2,1,0:T(8,128)(2,1)S(1)}, bf16[4,24,1920]{2,1,0:T(8,128)(2,1)S(1)}, u32[]{:S(2)}, u32[]{:S(2)}) collective-permute-start(bf16[4,24,1920]{2,1,0:T(8,128)(2,1)S(1)} %bitcast_dynamic-update-slice_fusion.15), channel_id=1, source_target_pairs={{0,2},{1,3},{2,0},{3,1},{4,6},{5,7},{6,4},{7,5},{8,10},{9,11},{10,... | collective-permute-start | bytes 1105928 | tf_op jit(solution)/shard_map/ppermute | solution.py:743
  27.4 25.5 %collective-permute-start.16 = (bf16[4,24,1920]{2,1,0:T(8,128)(2,1)S(1)}, bf16[4,24,1920]{2,1,0:T(8,128)(2,1)S(1)}, u32[]{:S(2)}, u32[]{:S(2)}) collective-permute-start(bf16[4,24,1920]{2,1,0:T(8,128)(2,1)S(1)} %bitcast_dynamic-update-slice_fusion.15), channel_id=1, source_target_pairs={{0,5},{1,4},{2,7},{3,6},{4,1},{5,0},{6,3},{7,2},{8,13},{9,12},{10,... | collective-permute-start | bytes 1105928 | tf_op jit(solution)/shard_map/ppermute | solution.py:743
  29.1 23.9 %collective-permute-start.15 = (bf16[4,24,1920]{2,1,0:T(8,128)(2,1)S(1)}, bf16[4,24,1920]{2,1,0:T(8,128)(2,1)S(1)}, u32[]{:S(2)}, u32[]{:S(2)}) collective-permute-start(bf16[4,24,1920]{2,1,0:T(8,128)(2,1)S(1)} %bitcast_dynamic-update-slice_fusion.15), channel_id=1, source_target_pairs={{0,4},{1,5},{2,6},{3,7},{4,0},{5,1},{6,2},{7,3},{8,12},{9,13},{10,... | collective-permute-start | bytes 1105928 | tf_op jit(solution)/shard_map/ppermute | solution.py:743
  29.6 27.4 %collective-permute-start.14 = (bf16[4,24,1920]{2,1,0:T(8,128)(2,1)S(1)}, bf16[4,24,1920]{2,1,0:T(8,128)(2,1)S(1)}, u32[]{:S(2)}, u32[]{:S(2)}) collective-permute-start(bf16[4,24,1920]{2,1,0:T(8,128)(2,1)S(1)} %bitcast_dynamic-update-slice_fusion.15), channel_id=1, source_target_pairs={{0,1},{1,0},{2,3},{3,2},{4,5},{5,4},{6,7},{7,6},{8,9},{9,8},{10,11... | collective-permute-start | bytes 1105928 | tf_op jit(solution)/shard_map/ppermute | solution.py:743
  57.1 44.6 %collective-permute-start.28 = (bf16[512,768]{1,0:T(8,128)(2,1)S(1)}, bf16[512,768]{1,0:T(8,128)(2,1)S(1)}, u32[]{:S(2)}, u32[]{:S(2)}) collective-permute-start(bf16[512,768]{1,0:T(8,128)(2,1)S(1)} %dynamic-slice_bitcast_fusion.4), channel_id=1, source_target_pairs={{0,1},{1,0},{2,3},{3,2},{4,5},{5,4},{6,7},{7,6},{8,9},{9,8},{10,11... | collective-permute-start | bytes 2359304 | tf_op jit(solution)/shard_map/ppermute | solution.py:743
  60.6 36.9 %collective-permute-start.10 = (bf16[24,3072]{1,0:T(8,128)(2,1)S(1)}, bf16[24,3072]{1,0:T(8,128)(2,1)S(1)}, u32[]{:S(2)}, u32[]{:S(2)}) collective-permute-start(bf16[24,3072]{1,0:T(8,128)(2,1)S(1)} %pad_maximum_fusion.6), channel_id=1, source_target_pairs={{0,24},{1,25},{2,26},{3,27},{4,28},{5,29},{6,30},{7,31},{8,0},{9,1... | collective-permute-start | bytes 442376 | tf_op jit(solution)/shard_map/ppermute | solution.py:743
  63.5 33.9 %collective-permute-start.9 = (bf16[24,3072]{1,0:T(8,128)(2,1)S(1)}, bf16[24,3072]{1,0:T(8,128)(2,1)S(1)}, u32[]{:S(2)}, u32[]{:S(2)}) collective-permute-start(bf16[24,3072]{1,0:T(8,128)(2,1)S(1)} %pad_maximum_fusion.6), channel_id=1, source_target_pairs={{0,16},{1,17},{2,18},{3,19},{4,20},{5,21},{6,22},{7,23},{8,24},{9,... | collective-permute-start | bytes 442376 | tf_op jit(solution)/shard_map/ppermute | solution.py:743
  63.9 33.5 %collective-permute-start.8 = (bf16[24,3072]{1,0:T(8,128)(2,1)S(1)}, bf16[24,3072]{1,0:T(8,128)(2,1)S(1)}, u32[]{:S(2)}, u32[]{:S(2)}) collective-permute-start(bf16[24,3072]{1,0:T(8,128)(2,1)S(1)} %pad_maximum_fusion.6), channel_id=1, source_target_pairs={{0,8},{1,9},{2,10},{3,11},{4,12},{5,13},{6,14},{7,15},{8,16},{9,17... | collective-permute-start | bytes 442376 | tf_op jit(solution)/shard_map/ppermute | solution.py:743
  97.5 17.2 %collective-permute-start.22 = (bf16[4,24,3072]{2,1,0:T(8,128)(2,1)S(1)}, bf16[4,24,3072]{2,1,0:T(8,128)(2,1)S(1)}, u32[]{:S(2)}, u32[]{:S(2)}) collective-permute-start(bf16[4,24,3072]{2,1,0:T(8,128)(2,1)S(1)} %bitcast_dynamic-update-slice_fusion.11), channel_id=1, source_target_pairs={{0,5},{1,4},{2,7},{3,6},{4,1},{5,0},{6,3},{7,2},{8,13},{9,12},{10,... | collective-permute-start | bytes 1769480 | tf_op jit(solution)/shard_map/ppermute | solution.py:743
  99.1 26.9 %collective-permute-start.20 = (bf16[4,24,3072]{2,1,0:T(8,128)(2,1)S(1)}, bf16[4,24,3072]{2,1,0:T(8,128)(2,1)S(1)}, u32[]{:S(2)}, u32[]{:S(2)}) collective-permute-start(bf16[4,24,3072]{2,1,0:T(8,128)(2,1)S(1)} %bitcast_dynamic-update-slice_fusion.11), channel_id=1, source_target_pairs={{0,4},{1,5},{2,6},{3,7},{4,0},{5,1},{6,2},{7,3},{8,12},{9,13},{10,... | collective-permute-start | bytes 1769480 | tf_op jit(solution)/shard_map/ppermute | solution.py:743
  100.0 26.1 %collective-permute-start.18 = (bf16[4,24,3072]{2,1,0:T(8,128)(2,1)S(1)}, bf16[4,24,3072]{2,1,0:T(8,128)(2,1)S(1)}, u32[]{:S(2)}, u32[]{:S(2)}) collective-permute-start(bf16[4,24,3072]{2,1,0:T(8,128)(2,1)S(1)} %bitcast_dynamic-update-slice_fusion.11), channel_id=1, source_target_pairs={{0,1},{1,0},{2,3},{3,2},{4,5},{5,4},{6,7},{7,6},{8,9},{9,8},{10,11... | collective-permute-start | bytes 1769480 | tf_op jit(solution)/shard_map/ppermute | solution.py:743
  101.1 25.5 %collective-permute-start.17 = (bf16[4,24,3072]{2,1,0:T(8,128)(2,1)S(1)}, bf16[4,24,3072]{2,1,0:T(8,128)(2,1)S(1)}, u32[]{:S(2)}, u32[]{:S(2)}) collective-permute-start(bf16[4,24,3072]{2,1,0:T(8,128)(2,1)S(1)} %bitcast_dynamic-update-slice_fusion.11), channel_id=1, source_target_pairs={{0,2},{1,3},{2,0},{3,1},{4,6},{5,7},{6,4},{7,5},{8,10},{9,11},{10,... | collective-permute-start | bytes 1769480 | tf_op jit(solution)/shard_map/ppermute | solution.py:743
  114.8 14.3 %collective-permute-start.23 = (bf16[4,24,3072]{2,1,0:T(8,128)(2,1)S(1)}, bf16[4,24,3072]{2,1,0:T(8,128)(2,1)S(1)}, u32[]{:S(2)}, u32[]{:S(2)}) collective-permute-start(bf16[4,24,3072]{2,1,0:T(8,128)(2,1)S(1)} %collective-permute-done.22), channel_id=1, source_target_pairs={{0,2},{1,3},{2,0},{3,1},{4,6},{5,7},{6,4},{7,5},{8,10},{9,11},{10,... | collective-permute-start | bytes 1769480 | tf_op jit(solution)/shard_map/ppermute | solution.py:743
  176.4 48.7 %collective-permute-start.30 = (bf16[512,768]{1,0:T(8,128)(2,1)S(1)}, bf16[512,768]{1,0:T(8,128)(2,1)S(1)}, u32[]{:S(2)}, u32[]{:S(2)}) collective-permute-start(bf16[512,768]{1,0:T(8,128)(2,1)S(1)} %dynamic-slice_bitcast_fusion.3), channel_id=1, source_target_pairs={{0,1},{1,0},{2,3},{3,2},{4,5},{5,4},{6,7},{7,6},{8,9},{9,8},{10,11... | collective-permute-start | bytes 2359304 | tf_op jit(solution)/shard_map/ppermute | solution.py:743
  181.9 42.1 %collective-permute-start.31 = (bf16[4,24,3072]{2,1,0:T(8,128)(2,1)S(1)}, bf16[4,24,3072]{2,1,0:T(8,128)(2,1)S(1)}, u32[]{:S(2)}, u32[]{:S(2)}) collective-permute-start(bf16[4,24,3072]{2,1,0:T(8,128)(2,1)S(1)} %get-tuple-element.104), channel_id=1, source_target_pairs={{0,1},{1,0},{2,3},{3,2},{4,5},{5,4},{6,7},{7,6},{8,9},{9,8},{10,11... | collective-permute-start | bytes 1769480 | tf_op jit(solution)/shard_map/ppermute | solution.py:743
  182.9 41.1 %collective-permute-start.33 = (bf16[4,24,3072]{2,1,0:T(8,128)(2,1)S(1)}, bf16[4,24,3072]{2,1,0:T(8,128)(2,1)S(1)}, u32[]{:S(2)}, u32[]{:S(2)}) collective-permute-start(bf16[4,24,3072]{2,1,0:T(8,128)(2,1)S(1)} %get-tuple-element.105), channel_id=1, source_target_pairs={{0,5},{1,4},{2,7},{3,6},{4,1},{5,0},{6,3},{7,2},{8,13},{9,12},{10,... | collective-permute-start | bytes 1769480 | tf_op jit(solution)/shard_map/ppermute | solution.py:743
  184.6 39.3 %collective-permute-start.32 = (bf16[4,24,3072]{2,1,0:T(8,128)(2,1)S(1)}, bf16[4,24,3072]{2,1,0:T(8,128)(2,1)S(1)}, u32[]{:S(2)}, u32[]{:S(2)}) collective-permute-start(bf16[4,24,3072]{2,1,0:T(8,128)(2,1)S(1)} %get-tuple-element.106), channel_id=1, source_target_pairs={{0,4},{1,5},{2,6},{3,7},{4,0},{5,1},{6,2},{7,3},{8,12},{9,13},{10,... | collective-permute-start | bytes 1769480 | tf_op jit(solution)/shard_map/ppermute | solution.py:743
  248.0 11.4 %collective-permute-start.35 = (bf16[4,24,1920]{2,1,0:T(8,128)(2,1)S(1)}, bf16[4,24,1920]{2,1,0:T(8,128)(2,1)S(1)}, u32[]{:S(2)}, u32[]{:S(2)}) collective-permute-start(bf16[4,24,1920]{2,1,0:T(8,128)(2,1)S(1)} %get-tuple-element.113), channel_id=1, source_target_pairs={{0,1},{1,0},{2,3},{3,2},{4,5},{5,4},{6,7},{7,6},{8,9},{9,8},{10,11... | collective-permute-start | bytes 1105928 | tf_op jit(solution)/shard_map/ppermute | solution.py:743
  249.0 18.7 %collective-permute-start.37 = (bf16[4,24,1920]{2,1,0:T(8,128)(2,1)S(1)}, bf16[4,24,1920]{2,1,0:T(8,128)(2,1)S(1)}, u32[]{:S(2)}, u32[]{:S(2)}) collective-permute-start(bf16[4,24,1920]{2,1,0:T(8,128)(2,1)S(1)} %get-tuple-element.114), channel_id=1, source_target_pairs={{0,5},{1,4},{2,7},{3,6},{4,1},{5,0},{6,3},{7,2},{8,13},{9,12},{10,... | collective-permute-start | bytes 1105928 | tf_op jit(solution)/shard_map/ppermute | solution.py:743
  250.8 18.4 %collective-permute-start.36 = (bf16[4,24,1920]{2,1,0:T(8,128)(2,1)S(1)}, bf16[4,24,1920]{2,1,0:T(8,128)(2,1)S(1)}, u32[]{:S(2)}, u32[]{:S(2)}) collective-permute-start(bf16[4,24,1920]{2,1,0:T(8,128)(2,1)S(1)} %get-tuple-element.115), channel_id=1, source_target_pairs={{0,4},{1,5},{2,6},{3,7},{4,0},{5,1},{6,2},{7,3},{8,12},{9,13},{10,... | collective-permute-start | bytes 1105928 | tf_op jit(solution)/shard_map/ppermute | solution.py:743
  282.3 24.6 %collective-permute-start.46 = (bf16[24,4992]{1,0:T(8,128)(2,1)S(1)}, bf16[24,4992]{1,0:T(8,128)(2,1)S(1)}, u32[]{:S(2)}, u32[]{:S(2)}) collective-permute-start(bf16[24,4992]{1,0:T(8,128)(2,1)S(1)} %get-tuple-element.116), channel_id=1, source_target_pairs={{0,8},{1,9},{2,10},{3,11},{4,12},{5,13},{6,14},{7,15},{8,16},{9,17... | collective-permute-start | bytes 718856 | tf_op jit(solution)/shard_map/ppermute | solution.py:743
  282.9 24.1 %collective-permute-start.47 = (bf16[24,4992]{1,0:T(8,128)(2,1)S(1)}, bf16[24,4992]{1,0:T(8,128)(2,1)S(1)}, u32[]{:S(2)}, u32[]{:S(2)}) collective-permute-start(bf16[24,4992]{1,0:T(8,128)(2,1)S(1)} %get-tuple-element.117), channel_id=1, source_target_pairs={{0,16},{1,17},{2,18},{3,19},{4,20},{5,21},{6,22},{7,23},{8,24},{9,... | collective-permute-start | bytes 718856 | tf_op jit(solution)/shard_map/ppermute | solution.py:743
  284.8 18.6 %collective-permute-start.43 = (f32[8,128]{1,0:T(8,128)S(1)}, f32[8,128]{1,0:T(8,128)S(1)}, u32[]{:S(2)}, u32[]{:S(2)}) collective-permute-start(f32[8,128]{1,0:T(8,128)S(1)} %get-tuple-element.126), channel_id=1, source_target_pairs={{0,8},{1,9},{2,10},{3,11},{4,12},{5,13},{6,14},{7,15},{8,16},{9,17... | collective-permute-start | bytes 12296 | tf_op jit(solution)/shard_map/ppermute | solution.py:743
  286.0 17.5 %collective-permute-start.45 = (f32[8,128]{1,0:T(8,128)S(1)}, f32[8,128]{1,0:T(8,128)S(1)}, u32[]{:S(2)}, u32[]{:S(2)}) collective-permute-start(f32[8,128]{1,0:T(8,128)S(1)} %get-tuple-element.127), channel_id=1, source_target_pairs={{0,24},{1,25},{2,26},{3,27},{4,28},{5,29},{6,30},{7,31},{8,0},{9,1... | collective-permute-start | bytes 12296 | tf_op jit(solution)/shard_map/ppermute | solution.py:743
  286.9 17.8 %collective-permute-start.44 = (f32[8,128]{1,0:T(8,128)S(1)}, f32[8,128]{1,0:T(8,128)S(1)}, u32[]{:S(2)}, u32[]{:S(2)}) collective-permute-start(f32[8,128]{1,0:T(8,128)S(1)} %get-tuple-element.128), channel_id=1, source_target_pairs={{0,16},{1,17},{2,18},{3,19},{4,20},{5,21},{6,22},{7,23},{8,24},{9,... | collective-permute-start | bytes 12296 | tf_op jit(solution)/shard_map/ppermute | solution.py:743
  303.5 18.1 %collective-permute-start.38 = (bf16[512,768]{1,0:T(8,128)(2,1)S(1)}, bf16[512,768]{1,0:T(8,128)(2,1)S(1)}, u32[]{:S(2)}, u32[]{:S(2)}) collective-permute-start(bf16[512,768]{1,0:T(8,128)(2,1)S(1)} %dynamic-slice_bitcast_fusion.2), channel_id=1, source_target_pairs={{0,1},{1,0},{2,3},{3,2},{4,5},{5,4},{6,7},{7,6},{8,9},{9,8},{10,11... | collective-permute-start | bytes 2359304 | tf_op jit(solution)/shard_map/ppermute | solution.py:743
  (41 other events, 579.3 us)

commit v3 on v2

--- a/solution.py
+++ b/solution.py
@@ -707,12 +707,11 @@
 
 def input_grad(xf, r_in, gain_in, dnormed, cot):
     scaled = gain_in.astype(jnp.float32) * dnormed
-    dx = (
+    return (
         r_in * scaled
         - xf * r_in**3 * jnp.mean(scaled * xf, -1, keepdims=True)
         + cot.astype(jnp.float32)
     ).astype(jnp.bfloat16)
-    return (dx, jnp.sum(dnormed * xf * r_in, 0))
 
 
 def low_dot(left, right):
@@ -780,18 +779,14 @@
     return found
 
 
-def reduce_plane(parts, kind=jnp.bfloat16):
-    return add_up(plane_parts(parts)).astype(kind)
-
-
-def reduce_line(parts):
+def line_parts(parts):
     high = lax.axis_size("dp") // 4
     z, _, _, _ = grid_place()
     found = [pick(parts, (0,), (z,))]
     for hop in range(1, high):
         piece = pick(parts, (0,), (lax.rem(z + hop, high),))
         found.append(grid_send(piece, (hop, 0, 0, 0)))
-    return add_up(found)
+    return found
 
 
 def place_in(array, axis, places, pieces):
@@ -846,10 +841,6 @@
     return jnp.dot(order, held, preferred_element_type=jnp.float32).reshape((-1,) + own.shape)
 
 
-def reduce_all(parts, kind=jnp.bfloat16):
-    return reduce_line(reduce_plane(reduce_core(parts, kind), kind))
-
-
 def after(value, *others):
     return lax.optimization_barrier((value,) + others)[0]
 
@@ -894,9 +885,9 @@
 
     line_first = gather_line(first)
     xb = swap_halves(x_in[:, 0])
-    small = gather_small(small)
+    small = gather_small(after(small, line_first))
     plane_first = gather_plane(line_first)
-    line_second = gather_line(after(second, xb))
+    line_second = gather_line(after(second, line_first))
     (w_xt,) = gather_core(plane_first, [[slice(0, XTAIL)]])
     plane_second = gather_plane(after(line_second, *plane_first))
 
@@ -934,32 +925,37 @@
     y_out = swap_join(y.reshape(micro, length, WIDE), y_got).reshape(x_in.shape)
     grad_wxt = tdot(normed, dxt).astype(jnp.bfloat16)
     late = reduce_core(grad_wxt)
-    dnormed = ndot(after(dz, late), w_z) + ndot(after(dxt, late), w_xt)
-    late = plane_parts(late)
-    dx, grad_gin = input_grad(xf, r_in, gain_in, dnormed, cot)
-    dx_in = swap_halves(after(dx.reshape(micro, length, WIDE), *late)).reshape(x_in.shape)
-    late_pieces = late
-    both = [add_up(parts).astype(jnp.bfloat16) for parts in (early, late)]
-    both = reduce_line(jnp.concatenate(both, -1))
-    early, late = both[:, : 2 * INNER], both[:, 2 * INNER :]
     head_terms = jnp.concatenate(
         [ghead[0, :HEADS], ghead[1, :HEADS], jnp.sum(gskip[0].reshape(HEADS, HEADDIM), -1)]
     )
-    grad_gin = after(grad_gin, *late_pieces)
     tiny = jax.vmap(pack_small)(
-        grad_gin.reshape(devices, -1),
+        jnp.zeros((devices, 8), jnp.float32),
         gconv[:KCONV].reshape(KCONV, devices, -1).transpose(1, 0, 2),
         gconv[KCONV].reshape(devices, -1),
         jnp.sum(ggain, 0).reshape(devices, -1),
         jnp.broadcast_to(head_terms, (devices, 3 * HEADS)),
-    )
-    own = reduce_all(tiny.reshape(devices * (KCONV + 4), PAIR), jnp.float32)
+    )[:, :, : XTAIL - SPARE]
+    tiny = reduce_core(tiny.reshape(devices * (KCONV + 4), -1), jnp.float32)
+    tiny = jnp.pad(tiny, ((0, 0),) * 3 + ((0, rows - KCONV - 4), (SPARE, 0)))
+    late = (late.astype(jnp.float32) + tiny).astype(jnp.bfloat16)
+    dnormed = ndot(after(dz, late), w_z) + ndot(after(dxt, late), w_xt)
+    late = plane_parts(late)
+    dx = input_grad(xf, r_in, gain_in, dnormed, cot)
+    dx_got = swap_send(after(dx.reshape(micro, length, WIDE), *late))
+    both = [add_up(parts).astype(jnp.bfloat16) for parts in (early, late)]
+    both = line_parts(jnp.concatenate(both, -1))
+    both = add_up(lax.optimization_barrier(tuple(both) + (dx_got,))[:-1])
+    dx_in = swap_join(dx.reshape(micro, length, WIDE), dx_got).reshape(x_in.shape)
+    early, late = both[:, : 2 * INNER], both[:, 2 * INNER :]
     own_in = jnp.concatenate([early[:, :INNER], late[:, :SPARE]], 1)
     own_out = jnp.concatenate([early[:, INNER : INNER + WIDE], early[:, INNER + WIDE :]], 0)
+    own = late[:, SPARE:]
     found = unpack_small(own, sizes)
     heads_sum = own[KCONV + 3]
+    weighted = jnp.sum(own_in * in_weight.astype(jnp.float32), -1)
+    grad_gain = weighted / norm_gain.astype(jnp.float32)
     return (
-        y_out, dx_in, found[3], own_in, found[0], found[1], found[2], own_out,
+        y_out, dx_in, grad_gain, own_in, found[0], found[1], found[2], own_out,
         heads_sum[:HEADS], heads_sum[HEADS : 2 * HEADS], heads_sum[2 * HEADS : 3 * HEADS],
     )
 

time: 329 us -> 279 us (0.85)
  waiting for transfers between devices: 98.7 us -> 47.4 us
  starting transfers between devices: 47.6 us -> 43.5 us
  local copies, waits for them, and re-layouts: 29 us -> 32.8 us
    ppermute x49 -> x43, waiting for transfers between devices: 98.7 us -> 47.4 us  [grid_send(): return lax.ppermute(array, ('dp', 'seq'), grid_moves(step))]
    dynamic_update_slice x32, local copies, waits for them, and re-layouts: 0.9 us -> 15.5 us  [gather_core(): found[k] = lax.dynamic_update_slice(found[k], part, start)]
    pad x10 -> x6, local copies, waits for them, and re-layouts: 6.57 us -> 0.04 us  [pack_small(): jnp.pad(line, ((0, 0), (0, PAIR - line.shape[1])))]
    unnamed x49 -> x63, local copies, waits for them, and re-layouts: 7.48 us -> 2.56 us
    ppermute x49 -> x43, starting transfers between devices: 47.6 us -> 43.5 us  [grid_send(): return lax.ppermute(array, ('dp', 'seq'), grid_moves(step))]
  transfers between devices with their start and end apart: 49 -> 43, of which waited for: 15 -> 12; matrix products, arithmetic and copies ran while one was open for 11% -> 19% of each run, Pallas kernels for 19% -> 23%
where the time goes in v3:
time: 279 us; the launch traced here: 274 us
  Pallas kernels  92.2 us (33%)
  waiting for transfers between devices  47.4 us (17%)
  starting transfers between devices  43.5 us (16%)
  matrix products  35.8 us (13%)
  local copies, waits for them, and re-layouts  32.8 us (12%)
  other arithmetic  19.6 us (7%)
    ppermute x43, waiting for transfers between devices, grid_send(): return lax.ppermute(array, ('dp', 'seq'), grid_moves(step))  47.4 us
    ppermute x43, starting transfers between devices, grid_send(): return lax.ppermute(array, ('dp', 'seq'), grid_moves(step))  43.5 us
    pallas_call x1, Pallas kernels, run_backward(): pl.pallas_call(backward_kernel, grid=(count,), in_specs=[tall_block(XTAIL...  38.9 us
    pallas_call x1, Pallas kernels, run_gate(): pl.pallas_call(gate_kernel, grid=(length // GROUP,), in_specs=[tall_block...  29.8 us
    pallas_call x1, Pallas kernels, run_scan(): pl.pallas_call(scan_kernel, grid=(count,), in_specs=[tall_block(XTAIL), f...  23.5 us
    dynamic_update_slice x32, local copies, waits for them, and re-layouts, gather_core(): found[k] = lax.dynamic_update_slice(found[k], part, start)  15.5 us
    dot_general x3, matrix products, tdot(): lax.dot_general(left, right, (((0,), (0,)), ((), ())), preferred_element_...  14.2 us
    dot_general x2, matrix products, low_dot(): jnp.dot(left, right, preferred_element_type=jnp.float32)  12.9 us
  transfers between devices with their start and end apart: 43, of which 12 were waited for; matrix products, arithmetic and copies ran while one was open for 19% of the time, Pallas kernels for 23%

profile of v3, /device:TPU:8, one launch (start us, length us, event | category | flops | bytes accessed | tf_op | source)
XLA Modules:
  0.0 273.6 jit_solution(10292926481787064623)
XLA Ops:
  1.7 1.6 collective-permute-start.1
  4.4 1.9 collective-permute-start.3
  6.4 2.1 dynamic-slice_bitcast_fusion.5
  13.1 3.4 %collective-permute-start.5 = (bf16[1,1024]{1,0:T(2,128)(2,1)S(1)}, bf16[1,1024]{1,0:T(2,128)(2,1)S(1)}, u32[]{:S(2)}, u32[]{:S(2)}) collective-permute-start(bf16[1,1024]{1,0:T(2,128)(2,1)S(1)} %bitcast.342), channel_id=1, source_target_pairs={{0,16},{1,17},{2,18},{3,19},{4,20},{5,21},{6,22},{7,23},{8,24},{9,... | collective-permute-start | bytes 6152 | tf_op jit(solution)/shard_map/ppermute | solution.py:742
  17.0 1.7 collective-permute-start.11
  23.7 3.6 %collective-permute-done.7 = bf16[4,1024]{1,0:T(4,128)(2,1)S(1)} collective-permute-done((bf16[4,1024]{1,0:T(4,128)(2,1)S(1)}, bf16[4,1024]{1,0:T(4,128)(2,1)S(1)}, u32[]{:S(2)}, u32[]{:S(2)}) %collective-permute-start.7) | collective-permute-done | bytes 8224 | tf_op jit(solution)/shard_map/ppermute | solution.py:742
  29.3 1.8 broadcast_in_dim.67
  35.9 1.9 collective-permute-start.16
  38.3 5.0 %collective-permute-done.14 = bf16[4,24,1920]{2,1,0:T(8,128)(2,1)S(1)} collective-permute-done((bf16[4,24,1920]{2,1,0:T(8,128)(2,1)S(1)}, bf16[4,24,1920]{2,1,0:T(8,128)(2,1)S(1)}, u32[]{:S(2)}, u32[]{:S(2)}) %collective-permute-start.14) | collective-permute-done | bytes 368672 | tf_op jit(solution)/shard_map/ppermute | solution.py:742
  43.3 9.6 %collective-permute-done.15 = bf16[4,24,1920]{2,1,0:T(8,128)(2,1)S(1)} collective-permute-done((bf16[4,24,1920]{2,1,0:T(8,128)(2,1)S(1)}, bf16[4,24,1920]{2,1,0:T(8,128)(2,1)S(1)}, u32[]{:S(2)}, u32[]{:S(2)}) %collective-permute-start.15) | collective-permute-done | bytes 368672 | tf_op jit(solution)/shard_map/ppermute | solution.py:742
  65.7 7.9 %convolution_convert_fusion.xt_ref = bf16[1024,1920]{1,0:T(8,128)(2,1)} fusion(bf16[768,1920]{1,0:T(8,128)(2,1)} %bitcast.45, f32[768]{0:T(1024)S(1)} %mul.70, f32[1024]{0:T(1024)S(1)} %get-tuple-element.127, bf16[512,768]{1,0:T(8,128)(2,1)S(1)} %get-tuple-element.109, bf16[512,768]{1,0:T(8,128)(2,1)S(1)} %get-tuple-element.108), kind=kOutput, calls=%fused_computation.7 | convolution fusion | flops 3027369984 | bytes 8461312 | tf_op jit(solution)/shard_map/dot_general | solution.py:718
  73.6 23.5 %scan_forward.1 = (bf16[1024,1792]{1,0:T(8,128)(2,1)}, f32[1024,1792]{1,0:T(8,128)}, f32[512,1536]{1,0:T(8,128)S(1)}, f32[1024,1536]{1,0:T(8,128)}) custom-call(bf16[1024,1920]{1,0:T(8,128)(2,1)} %convolution_convert_fusion.xt_ref, f32[8,1792]{1,0:T(8,128)S(1)} %select_maximum_fusion.taps_ref, f32[8,128]{1,0:T(8,128)S(1)} %maximum_maximum_fusion.1.heads_ref, ...), custom_call_target="tpu_custom_call" | custom-call | flops 24999999488 | bytes 30000000 | tf_op jit(solution)/shard_map/scan_forward/pallas_call | solution.py:603
  104.8 5.0 %convolution_convert_fusion.1.z_ref = bf16[1024,1536]{1,0:T(8,128)(2,1)} fusion(bf16[768,1536]{1,0:T(8,128)(2,1)S(1)} %bitcast.324, f32[768]{0:T(1024)S(1)} %mul.70, f32[1024]{0:T(1024)S(1)} %get-tuple-element.127, bf16[512,768]{1,0:T(8,128)(2,1)S(1)} %get-tuple-element.109, bf16[512,768]{1,0:T(8,128)(2,1)S(1)} %get-tuple-element.108), kind=kOutput, calls=%fused_computation.8 | convolution fusion | flops 2422996992 | bytes 7085056 | tf_op jit(solution)/shard_map/dot_general | solution.py:718
  115.0 29.8 %gate_both_ways.1 = (bf16[1024,768]{1,0:T(8,128)(2,1)S(1)}, bf16[1024,1536]{1,0:T(8,128)(2,1)}, bf16[1024,1536]{1,0:T(8,128)(2,1)}, bf16[1024,1536]{1,0:T(8,128)...) custom-call(bf16[1024,1536]{1,0:T(8,128)(2,1)} %convolution_convert_fusion.1.z_ref, ...), custom_call_target="tpu_custom_call" | custom-call | flops 20000000000 | bytes 30000000 | tf_op jit(solution)/shard_map/gate_both_ways/pallas_call | solution.py:630
  144.9 5.1 %convolution_convert_fusion.3 = bf16[768,1536]{1,0:T(8,128)(2,1)S(1)} fusion(bf16[1024,1536]{1,0:T(8,128)(2,1)} %get-tuple-element.62, f32[768]{0:T(1024)S(1)} %mul.70, f32[1024]{0:T(1024)S(1)} %get-tuple-element.127, bf16[512,768]{1,0:T(8,128)(2,1)S(1)} %get-tuple-element.109, bf16[512,768]{1,0:T(8,128)(2,1)S(1)} %get-tuple-element.108), kind=kOutput, calls=%fused_computation.10 | convolution fusion | flops 2422603776 | bytes 7085056 | tf_op jit(solution)/shard_map/dot_general | solution.py:50
  150.0 3.2 %convolution_convert_fusion.2 = bf16[1536,768]{1,0:T(8,128)(2,1)S(1)} fusion(bf16[1024,1536]{1,0:T(8,128)(2,1)S(1)} %copy-done.27, bf16[512,768]{1,0:T(8,128)(2,1)S(1)} %get-tuple-element.107, bf16[512,768]{1,0:T(8,128)(2,1)S(1)} %get-tuple-element.106), kind=kOutput, calls=%fused_computation.9 | convolution fusion | flops 2420244480 | bytes 7077888 | tf_op jit(solution)/shard_map/dot_general | solution.py:50
  153.9 1.9 dynamic-slice_bitcast_fusion
  159.9 1.9 collective-permute-done.29
  161.8 3.3 %fusion = bf16[4,2,2,24,3072]{4,3,2,1,0:T(8,128)(2,1)S(1)} fusion(bf16[4,2,2,24,3072]{4,3,2,1,0:T(8,128)(2,1)} %collective-permute-done.29, bf16[4,2,2,2,24,3072]{5,4,3,2,1,0:T(8,128)(2,1)} %copy-done.2, s32[]{:T(128)S(6)} %select_n.141), kind=kLoop, calls=%fused_computation.6 | loop fusion | flops 4718592 | bytes 7077892 | tf_op jit(solution)/shard_map/convert_element_type | solution.py:770
  169.9 38.9 %scan_backward.1 = (bf16[1024,1920]{1,0:T(8,128)(2,1)}, f32[8,1792]{1,0:T(8,128)S(1)}, f32[8,128]{1,0:T(8,128)S(1)}, f32[8,1536]{1,0:T(8,128)S(1)}) custom-call(bf16[1024,1920]{1,0:T(8,128)(2,1)} %convolution_convert_fusion.xt_ref, bf16[1024,1792]{1,0:T(8,128)(2,1)} %get-tuple-element.44.xh_ref.mixed_ref, f32[1024,1792]{1,0:T(8,128)} %get-tuple-element.48.slope_ref, ...), custom_call_target="tpu_custom_call" | custom-call | flops 30000001024 | bytes 30000000 | tf_op jit(solution)/shard_map/scan_backward/pallas_call | solution.py:659
  209.3 2.0 add_convert_fusion.1
  211.2 6.0 %convolution_convert_fusion.4 = bf16[768,1920]{1,0:T(8,128)(2,1)S(1)} fusion(bf16[1024,1920]{1,0:T(8,128)(2,1)} %get-tuple-element.63, f32[768]{0:T(1024)S(1)} %mul.70, f32[1024]{0:T(1024)S(1)} %get-tuple-element.127, bf16[512,768]{1,0:T(8,128)(2,1)} %copy-done.3, bf16[512,768]{1,0:T(8,128)(2,1)S(1)} %get-tuple-element.108), kind=kOutput, calls=%fused_computation.11 | convolution fusion | flops 3026878464 | bytes 8461312 | tf_op jit(solution)/shard_map/dot_general | solution.py:50
  218.2 2.5 collective-permute-done.35
  221.4 1.6 collective-permute-start.36
  224.9 5.5 %fusion.97 = f32[1024,768]{1,0:T(8,128)S(1)} fusion(bf16[1024,1920]{1,0:T(8,128)(2,1)S(1)} %copy-done.25, bf16[768,1920]{1,0:T(8,128)(2,1)} %bitcast.45), kind=kOutput, calls=%fused_computation.254 | convolution fusion | flops 3019898880 | bytes 10027008 | tf_op jit(solution)/shard_map/dot_general | solution.py:56
  230.5 3.0 %fusion.8 = (f32[1024]{0:T(1024)S(1)}, f32[1024,768]{1,0:T(8,128)S(1)}) fusion(bf16[512,768]{1,0:T(8,128)(2,1)S(1)} %copy-done.4, bf16[512,768]{1,0:T(8,128)(2,1)S(1)} %get-tuple-element.108, f32[1024,768]{1,0:T(8,128)S(1)} %fusion.97, bf16[1024,1536]{1,0:T(8,128)(2,1)S(1)} %copy-done.26, bf16[768,1536]{1,0:T(8,128)(2,1)S(1)} %bitcast.325, f32[768]{0:T(1024)S(1)} %mul.70), kind=kOutput, calls=%fused_computation.19 | convolution fusion | flops 2422209536 | bytes 13376512 | tf_op jit(solution)/shard_map/dot_general | solution.py:56
  233.5 2.1 fusion.7
  235.6 5.6 %collective-permute-done.37 = bf16[4,24,1920]{2,1,0:T(8,128)(2,1)S(1)} collective-permute-done((bf16[4,24,1920]{2,1,0:T(8,128)(2,1)S(1)}, bf16[4,24,1920]{2,1,0:T(8,128)(2,1)S(1)}, u32[]{:S(2)}, u32[]{:S(2)}) %collective-permute-start.37) | collective-permute-done | bytes 368672 | tf_op jit(solution)/shard_map/ppermute | solution.py:742
  243.9 3.9 %collective-permute-start.41 = (bf16[24,4992]{1,0:T(8,128)(2,1)S(1)}, bf16[24,4992]{1,0:T(8,128)(2,1)S(1)}, u32[]{:S(2)}, u32[]{:S(2)}) collective-permute-start(bf16[24,4992]{1,0:T(8,128)(2,1)S(1)} %get-tuple-element.116), channel_id=1, source_target_pairs={{0,16},{1,17},{2,18},{3,19},{4,20},{5,21},{6,22},{7,23},{8,24},{9,... | collective-permute-start | bytes 718856 | tf_op jit(solution)/shard_map/ppermute | solution.py:742
  250.3 1.9 collective-permute-done.40
  252.2 11.3 %collective-permute-done.41 = bf16[24,4992]{1,0:T(8,128)(2,1)S(1)} collective-permute-done((bf16[24,4992]{1,0:T(8,128)(2,1)S(1)}, bf16[24,4992]{1,0:T(8,128)(2,1)S(1)}, u32[]{:S(2)}, u32[]{:S(2)}) %collective-permute-start.41) | collective-permute-done | bytes 239648 | tf_op jit(solution)/shard_map/ppermute | solution.py:742
  263.5 3.6 %collective-permute-done.42 = bf16[24,4992]{1,0:T(8,128)(2,1)S(1)} collective-permute-done((bf16[24,4992]{1,0:T(8,128)(2,1)S(1)}, bf16[24,4992]{1,0:T(8,128)(2,1)S(1)}, u32[]{:S(2)}, u32[]{:S(2)}) %collective-permute-start.42) | collective-permute-done | bytes 239648 | tf_op jit(solution)/shard_map/ppermute | solution.py:742
  (271 shorter events, 69.2 us)
Async XLA Ops:
  1.7 10.9 %collective-permute-start.1 = (bf16[24,1920]{1,0:T(8,128)(2,1)S(1)}, bf16[24,1920]{1,0:T(8,128)(2,1)S(1)}, u32[]{:S(2)}, u32[]{:S(2)}) collective-permute-start(bf16[24,1920]{1,0:T(8,128)(2,1)S(1)} %pad.71), channel_id=1, source_target_pairs={{0,8},{1,9},{2,10},{3,11},{4,12},{5,13},{6,14},{7,15},{8,16},{9,17... | collective-permute-start | bytes 276488 | tf_op jit(solution)/shard_map/ppermute | solution.py:742
  3.3 9.3 %collective-permute-start.2 = (bf16[24,1920]{1,0:T(8,128)(2,1)S(1)}, bf16[24,1920]{1,0:T(8,128)(2,1)S(1)}, u32[]{:S(2)}, u32[]{:S(2)}) collective-permute-start(bf16[24,1920]{1,0:T(8,128)(2,1)S(1)} %pad.71), channel_id=1, source_target_pairs={{0,16},{1,17},{2,18},{3,19},{4,20},{5,21},{6,22},{7,23},{8,24},{9,... | collective-permute-start | bytes 276488 | tf_op jit(solution)/shard_map/ppermute | solution.py:742
  4.4 8.6 %collective-permute-start.3 = (bf16[24,1920]{1,0:T(8,128)(2,1)S(1)}, bf16[24,1920]{1,0:T(8,128)(2,1)S(1)}, u32[]{:S(2)}, u32[]{:S(2)}) collective-permute-start(bf16[24,1920]{1,0:T(8,128)(2,1)S(1)} %pad.71), channel_id=1, source_target_pairs={{0,24},{1,25},{2,26},{3,27},{4,28},{5,29},{6,30},{7,31},{8,0},{9,1... | collective-permute-start | bytes 276488 | tf_op jit(solution)/shard_map/ppermute | solution.py:742
  8.4 50.3 %collective-permute-start = (bf16[512,768]{1,0:T(8,128)(2,1)}, bf16[512,768]{1,0:T(8,128)(2,1)}, u32[]{:S(2)}, u32[]{:S(2)}) collective-permute-start(bf16[512,768]{1,0:T(8,128)(2,1)} %dynamic-slice_bitcast_fusion.5), channel_id=1, source_target_pairs={{0,1},{1,0},{2,3},{3,2},{4,5},{5,4},{6,7},{7,6},{8,9},{9,8},{10,11... | collective-permute-start | bytes 2359304 | tf_op jit(solution)/shard_map/ppermute | solution.py:742
  17.0 17.3 %collective-permute-start.11 = (bf16[24,3072]{1,0:T(8,128)(2,1)S(1)}, bf16[24,3072]{1,0:T(8,128)(2,1)S(1)}, u32[]{:S(2)}, u32[]{:S(2)}) collective-permute-start(bf16[24,3072]{1,0:T(8,128)(2,1)S(1)} %pad_maximum_fusion.6), channel_id=1, source_target_pairs={{0,8},{1,9},{2,10},{3,11},{4,12},{5,13},{6,14},{7,15},{8,16},{9,17... | collective-permute-start | bytes 442376 | tf_op jit(solution)/shard_map/ppermute | solution.py:742
  20.1 7.3 %collective-permute-start.7 = (bf16[4,1024]{1,0:T(4,128)(2,1)S(1)}, bf16[4,1024]{1,0:T(4,128)(2,1)S(1)}, u32[]{:S(2)}, u32[]{:S(2)}) collective-permute-start(bf16[4,1024]{1,0:T(4,128)(2,1)S(1)} %pad_maximum_fusion.8), channel_id=1, source_target_pairs={{0,1},{1,0},{2,3},{3,2},{4,5},{5,4},{6,7},{7,6},{8,9},{9,8},{10,11... | collective-permute-start | bytes 24584 | tf_op jit(solution)/shard_map/ppermute | solution.py:742
  20.7 7.0 %collective-permute-start.8 = (bf16[4,1024]{1,0:T(4,128)(2,1)S(1)}, bf16[4,1024]{1,0:T(4,128)(2,1)S(1)}, u32[]{:S(2)}, u32[]{:S(2)}) collective-permute-start(bf16[4,1024]{1,0:T(4,128)(2,1)S(1)} %pad_maximum_fusion.8), channel_id=1, source_target_pairs={{0,4},{1,5},{2,6},{3,7},{4,0},{5,1},{6,2},{7,3},{8,12},{9,13},{10,... | collective-permute-start | bytes 24584 | tf_op jit(solution)/shard_map/ppermute | solution.py:742
  22.2 7.0 %collective-permute-start.9 = (bf16[4,1024]{1,0:T(4,128)(2,1)S(1)}, bf16[4,1024]{1,0:T(4,128)(2,1)S(1)}, u32[]{:S(2)}, u32[]{:S(2)}) collective-permute-start(bf16[4,1024]{1,0:T(4,128)(2,1)S(1)} %pad_maximum_fusion.8), channel_id=1, source_target_pairs={{0,5},{1,4},{2,7},{3,6},{4,1},{5,0},{6,3},{7,2},{8,13},{9,12},{10,... | collective-permute-start | bytes 24584 | tf_op jit(solution)/shard_map/ppermute | solution.py:742
  27.4 8.5 %collective-permute-start.12 = (bf16[24,3072]{1,0:T(8,128)(2,1)S(1)}, bf16[24,3072]{1,0:T(8,128)(2,1)S(1)}, u32[]{:S(2)}, u32[]{:S(2)}) collective-permute-start(bf16[24,3072]{1,0:T(8,128)(2,1)S(1)} %pad_maximum_fusion.6), channel_id=1, source_target_pairs={{0,16},{1,17},{2,18},{3,19},{4,20},{5,21},{6,22},{7,23},{8,24},{9,... | collective-permute-start | bytes 442376 | tf_op jit(solution)/shard_map/ppermute | solution.py:742
  27.7 10.6 %collective-permute-start.13 = (bf16[24,3072]{1,0:T(8,128)(2,1)S(1)}, bf16[24,3072]{1,0:T(8,128)(2,1)S(1)}, u32[]{:S(2)}, u32[]{:S(2)}) collective-permute-start(bf16[24,3072]{1,0:T(8,128)(2,1)S(1)} %pad_maximum_fusion.6), channel_id=1, source_target_pairs={{0,24},{1,25},{2,26},{3,27},{4,28},{5,29},{6,30},{7,31},{8,0},{9,1... | collective-permute-start | bytes 442376 | tf_op jit(solution)/shard_map/ppermute | solution.py:742
  31.9 11.4 %collective-permute-start.14 = (bf16[4,24,1920]{2,1,0:T(8,128)(2,1)S(1)}, bf16[4,24,1920]{2,1,0:T(8,128)(2,1)S(1)}, u32[]{:S(2)}, u32[]{:S(2)}) collective-permute-start(bf16[4,24,1920]{2,1,0:T(8,128)(2,1)S(1)} %bitcast_dynamic-update-slice_fusion.15), channel_id=1, source_target_pairs={{0,1},{1,0},{2,3},{3,2},{4,5},{5,4},{6,7},{7,6},{8,9},{9,8},{10,11... | collective-permute-start | bytes 1105928 | tf_op jit(solution)/shard_map/ppermute | solution.py:742
  34.3 18.7 %collective-permute-start.15 = (bf16[4,24,1920]{2,1,0:T(8,128)(2,1)S(1)}, bf16[4,24,1920]{2,1,0:T(8,128)(2,1)S(1)}, u32[]{:S(2)}, u32[]{:S(2)}) collective-permute-start(bf16[4,24,1920]{2,1,0:T(8,128)(2,1)S(1)} %bitcast_dynamic-update-slice_fusion.15), channel_id=1, source_target_pairs={{0,4},{1,5},{2,6},{3,7},{4,0},{5,1},{6,2},{7,3},{8,12},{9,13},{10,... | collective-permute-start | bytes 1105928 | tf_op jit(solution)/shard_map/ppermute | solution.py:742
  35.9 17.1 %collective-permute-start.16 = (bf16[4,24,1920]{2,1,0:T(8,128)(2,1)S(1)}, bf16[4,24,1920]{2,1,0:T(8,128)(2,1)S(1)}, u32[]{:S(2)}, u32[]{:S(2)}) collective-permute-start(bf16[4,24,1920]{2,1,0:T(8,128)(2,1)S(1)} %bitcast_dynamic-update-slice_fusion.15), channel_id=1, source_target_pairs={{0,5},{1,4},{2,7},{3,6},{4,1},{5,0},{6,3},{7,2},{8,13},{9,12},{10,... | collective-permute-start | bytes 1105928 | tf_op jit(solution)/shard_map/ppermute | solution.py:742
  38.3 17.3 %collective-permute-start.24 = (bf16[4,24,1920]{2,1,0:T(8,128)(2,1)S(1)}, bf16[4,24,1920]{2,1,0:T(8,128)(2,1)S(1)}, u32[]{:S(2)}, u32[]{:S(2)}) collective-permute-start(bf16[4,24,1920]{2,1,0:T(8,128)(2,1)S(1)} %bitcast_dynamic-update-slice_fusion.15), channel_id=1, source_target_pairs={{0,2},{1,3},{2,0},{3,1},{4,6},{5,7},{6,4},{7,5},{8,10},{9,11},{10,... | collective-permute-start | bytes 1105928 | tf_op jit(solution)/shard_map/ppermute | solution.py:742
  52.9 44.8 %collective-permute-start.17 = (bf16[4,24,3072]{2,1,0:T(8,128)(2,1)S(1)}, bf16[4,24,3072]{2,1,0:T(8,128)(2,1)S(1)}, u32[]{:S(2)}, u32[]{:S(2)}) collective-permute-start(bf16[4,24,3072]{2,1,0:T(8,128)(2,1)S(1)} %bitcast_dynamic-update-slice_fusion.11), channel_id=1, source_target_pairs={{0,2},{1,3},{2,0},{3,1},{4,6},{5,7},{6,4},{7,5},{8,10},{9,11},{10,... | collective-permute-start | bytes 1769480 | tf_op jit(solution)/shard_map/ppermute | solution.py:742
  52.9 44.2 %collective-permute-start.18 = (bf16[4,24,3072]{2,1,0:T(8,128)(2,1)S(1)}, bf16[4,24,3072]{2,1,0:T(8,128)(2,1)}, u32[]{:S(2)}, u32[]{:S(2)}) collective-permute-start(bf16[4,24,3072]{2,1,0:T(8,128)(2,1)S(1)} %bitcast_dynamic-update-slice_fusion.11), channel_id=1, source_target_pairs={{0,1},{1,0},{2,3},{3,2},{4,5},{5,4},{6,7},{7,6},{8,9},{9,8},{10,11... | collective-permute-start | bytes 1769480 | tf_op jit(solution)/shard_map/ppermute | solution.py:742
  53.4 43.8 %collective-permute-start.20 = (bf16[4,24,3072]{2,1,0:T(8,128)(2,1)S(1)}, bf16[4,24,3072]{2,1,0:T(8,128)(2,1)}, u32[]{:S(2)}, u32[]{:S(2)}) collective-permute-start(bf16[4,24,3072]{2,1,0:T(8,128)(2,1)S(1)} %bitcast_dynamic-update-slice_fusion.11), channel_id=1, source_target_pairs={{0,4},{1,5},{2,6},{3,7},{4,0},{5,1},{6,2},{7,3},{8,12},{9,13},{10,... | collective-permute-start | bytes 1769480 | tf_op jit(solution)/shard_map/ppermute | solution.py:742
  55.6 43.3 %collective-permute-start.22 = (bf16[4,24,3072]{2,1,0:T(8,128)(2,1)S(1)}, bf16[4,24,3072]{2,1,0:T(8,128)(2,1)}, u32[]{:S(2)}, u32[]{:S(2)}) collective-permute-start(bf16[4,24,3072]{2,1,0:T(8,128)(2,1)S(1)} %bitcast_dynamic-update-slice_fusion.11), channel_id=1, source_target_pairs={{0,5},{1,4},{2,7},{3,6},{4,1},{5,0},{6,3},{7,2},{8,13},{9,12},{10,... | collective-permute-start | bytes 1769480 | tf_op jit(solution)/shard_map/ppermute | solution.py:742
  64.4 36.5 %collective-permute-start.28 = (bf16[512,768]{1,0:T(8,128)(2,1)S(1)}, bf16[512,768]{1,0:T(8,128)(2,1)}, u32[]{:S(2)}, u32[]{:S(2)}) collective-permute-start(bf16[512,768]{1,0:T(8,128)(2,1)S(1)} %dynamic-slice_bitcast_fusion.4), channel_id=1, source_target_pairs={{0,1},{1,0},{2,3},{3,2},{4,5},{5,4},{6,7},{7,6},{8,9},{9,8},{10,11... | collective-permute-start | bytes 2359304 | tf_op jit(solution)/shard_map/ppermute | solution.py:742
  97.3 6.4 %collective-permute-start.21 = (bf16[4,24,3072]{2,1,0:T(8,128)(2,1)}, bf16[4,24,3072]{2,1,0:T(8,128)(2,1)S(1)}, u32[]{:S(2)}, u32[]{:S(2)}) collective-permute-start(bf16[4,24,3072]{2,1,0:T(8,128)(2,1)} %collective-permute-done.20), channel_id=1, source_target_pairs={{0,2},{1,3},{2,0},{3,1},{4,6},{5,7},{6,4},{7,5},{8,10},{9,11},{10,... | collective-permute-start | bytes 1769480 | tf_op jit(solution)/shard_map/ppermute | solution.py:742
  98.9 5.8 %collective-permute-start.23 = (bf16[4,24,3072]{2,1,0:T(8,128)(2,1)}, bf16[4,24,3072]{2,1,0:T(8,128)(2,1)S(1)}, u32[]{:S(2)}, u32[]{:S(2)}) collective-permute-start(bf16[4,24,3072]{2,1,0:T(8,128)(2,1)} %collective-permute-done.22), channel_id=1, source_target_pairs={{0,2},{1,3},{2,0},{3,1},{4,6},{5,7},{6,4},{7,5},{8,10},{9,11},{10,... | collective-permute-start | bytes 1769480 | tf_op jit(solution)/shard_map/ppermute | solution.py:742
  158.2 53.0 %collective-permute-start.30 = (bf16[512,768]{1,0:T(8,128)(2,1)}, bf16[512,768]{1,0:T(8,128)(2,1)}, u32[]{:S(2)}, u32[]{:S(2)}) collective-permute-start(bf16[512,768]{1,0:T(8,128)(2,1)} %dynamic-slice_bitcast_fusion.3), channel_id=1, source_target_pairs={{0,1},{1,0},{2,3},{3,2},{4,5},{5,4},{6,7},{7,6},{8,9},{9,8},{10,11... | collective-permute-start | bytes 2359304 | tf_op jit(solution)/shard_map/ppermute | solution.py:742
  166.4 42.9 %collective-permute-start.31 = (bf16[4,24,3072]{2,1,0:T(8,128)(2,1)}, bf16[4,24,3072]{2,1,0:T(8,128)(2,1)}, u32[]{:S(2)}, u32[]{:S(2)}) collective-permute-start(bf16[4,24,3072]{2,1,0:T(8,128)(2,1)} %get-tuple-element.101), channel_id=1, source_target_pairs={{0,1},{1,0},{2,3},{3,2},{4,5},{5,4},{6,7},{7,6},{8,9},{9,8},{10,11... | collective-permute-start | bytes 1769480 | tf_op jit(solution)/shard_map/ppermute | solution.py:742
  167.9 41.3 %collective-permute-start.32 = (bf16[4,24,3072]{2,1,0:T(8,128)(2,1)}, bf16[4,24,3072]{2,1,0:T(8,128)(2,1)}, u32[]{:S(2)}, u32[]{:S(2)}) collective-permute-start(bf16[4,24,3072]{2,1,0:T(8,128)(2,1)} %get-tuple-element.103), channel_id=1, source_target_pairs={{0,4},{1,5},{2,6},{3,7},{4,0},{5,1},{6,2},{7,3},{8,12},{9,13},{10,... | collective-permute-start | bytes 1769480 | tf_op jit(solution)/shard_map/ppermute | solution.py:742
  169.4 39.9 %collective-permute-start.33 = (bf16[4,24,3072]{2,1,0:T(8,128)(2,1)}, bf16[4,24,3072]{2,1,0:T(8,128)(2,1)}, u32[]{:S(2)}, u32[]{:S(2)}) collective-permute-start(bf16[4,24,3072]{2,1,0:T(8,128)(2,1)} %get-tuple-element.102), channel_id=1, source_target_pairs={{0,5},{1,4},{2,7},{3,6},{4,1},{5,0},{6,3},{7,2},{8,13},{9,12},{10,... | collective-permute-start | bytes 1769480 | tf_op jit(solution)/shard_map/ppermute | solution.py:742
  221.4 14.2 %collective-permute-start.36 = (bf16[4,24,1920]{2,1,0:T(8,128)(2,1)S(1)}, bf16[4,24,1920]{2,1,0:T(8,128)(2,1)S(1)}, u32[]{:S(2)}, u32[]{:S(2)}) collective-permute-start(bf16[4,24,1920]{2,1,0:T(8,128)(2,1)S(1)} %get-tuple-element.110), channel_id=1, source_target_pairs={{0,1},{1,0},{2,3},{3,2},{4,5},{5,4},{6,7},{7,6},{8,9},{9,8},{10,11... | collective-permute-start | bytes 1105928 | tf_op jit(solution)/shard_map/ppermute | solution.py:742
  223.0 18.2 %collective-permute-start.37 = (bf16[4,24,1920]{2,1,0:T(8,128)(2,1)S(1)}, bf16[4,24,1920]{2,1,0:T(8,128)(2,1)S(1)}, u32[]{:S(2)}, u32[]{:S(2)}) collective-permute-start(bf16[4,24,1920]{2,1,0:T(8,128)(2,1)S(1)} %get-tuple-element.112), channel_id=1, source_target_pairs={{0,4},{1,5},{2,6},{3,7},{4,0},{5,1},{6,2},{7,3},{8,12},{9,13},{10,... | collective-permute-start | bytes 1105928 | tf_op jit(solution)/shard_map/ppermute | solution.py:742
  224.5 16.7 %collective-permute-start.38 = (bf16[4,24,1920]{2,1,0:T(8,128)(2,1)S(1)}, bf16[4,24,1920]{2,1,0:T(8,128)(2,1)S(1)}, u32[]{:S(2)}, u32[]{:S(2)}) collective-permute-start(bf16[4,24,1920]{2,1,0:T(8,128)(2,1)S(1)} %get-tuple-element.111), channel_id=1, source_target_pairs={{0,5},{1,4},{2,7},{3,6},{4,1},{5,0},{6,3},{7,2},{8,13},{9,12},{10,... | collective-permute-start | bytes 1105928 | tf_op jit(solution)/shard_map/ppermute | solution.py:742
  241.5 25.7 %collective-permute-start.39 = (bf16[512,768]{1,0:T(8,128)(2,1)S(1)}, bf16[512,768]{1,0:T(8,128)(2,1)S(1)}, u32[]{:S(2)}, u32[]{:S(2)}) collective-permute-start(bf16[512,768]{1,0:T(8,128)(2,1)S(1)} %dynamic-slice_bitcast_fusion.2), channel_id=1, source_target_pairs={{0,1},{1,0},{2,3},{3,2},{4,5},{5,4},{6,7},{7,6},{8,9},{9,8},{10,11... | collective-permute-start | bytes 2359304 | tf_op jit(solution)/shard_map/ppermute | solution.py:742
  242.8 9.4 %collective-permute-start.40 = (bf16[24,4992]{1,0:T(8,128)(2,1)S(1)}, bf16[24,4992]{1,0:T(8,128)(2,1)S(1)}, u32[]{:S(2)}, u32[]{:S(2)}) collective-permute-start(bf16[24,4992]{1,0:T(8,128)(2,1)S(1)} %get-tuple-element.115), channel_id=1, source_target_pairs={{0,8},{1,9},{2,10},{3,11},{4,12},{5,13},{6,14},{7,15},{8,16},{9,17... | collective-permute-start | bytes 718856 | tf_op jit(solution)/shard_map/ppermute | solution.py:742
  243.9 19.6 %collective-permute-start.41 = (bf16[24,4992]{1,0:T(8,128)(2,1)S(1)}, bf16[24,4992]{1,0:T(8,128)(2,1)S(1)}, u32[]{:S(2)}, u32[]{:S(2)}) collective-permute-start(bf16[24,4992]{1,0:T(8,128)(2,1)S(1)} %get-tuple-element.116), channel_id=1, source_target_pairs={{0,16},{1,17},{2,18},{3,19},{4,20},{5,21},{6,22},{7,23},{8,24},{9,... | collective-permute-start | bytes 718856 | tf_op jit(solution)/shard_map/ppermute | solution.py:742
  247.8 19.3 %collective-permute-start.42 = (bf16[24,4992]{1,0:T(8,128)(2,1)S(1)}, bf16[24,4992]{1,0:T(8,128)(2,1)S(1)}, u32[]{:S(2)}, u32[]{:S(2)}) collective-permute-start(bf16[24,4992]{1,0:T(8,128)(2,1)S(1)} %get-tuple-element.113), channel_id=1, source_target_pairs={{0,24},{1,25},{2,26},{3,27},{4,28},{5,29},{6,30},{7,31},{8,0},{9,1... | collective-permute-start | bytes 718856 | tf_op jit(solution)/shard_map/ppermute | solution.py:742
  (40 other events, 406.3 us)

commit v4 on v3

--- a/solution.py
+++ b/solution.py
@@ -1,3 +1,5 @@
+import functools
+
 import jax
 import jax.numpy as jnp
 from jax import lax
@@ -282,6 +284,7 @@
 PAIR = 2 * HEADDIM
 WIDE = 768
 XTAIL = 1920
+STRIP = 64
 LOW = -1e30
 
 
@@ -336,22 +339,22 @@
     @pl.when(pl.program_id(0) == 0)
     def _():
         run_ref[...] = jnp.zeros_like(run_ref)
-        cin_ref[0:8, :] = jnp.zeros((8, CONVW), jnp.float32)
-
-    cin_ref[8 : 8 + GROUP, :] = xt_ref[:, 0:CONVW].astype(jnp.float32)
+        cin_ref[:, 0:8, :] = jnp.zeros((CONVW // PAIR, 8, PAIR), jnp.float32)
 
     def conv_chunk(chunk, carry):
         at = pl.ds(pl.multiple_of(chunk * PAIR, PAIR), PAIR)
-        total = taps_ref[KCONV : KCONV + 1, at] + taps_ref[0:1, at] * cin_ref[5 : 5 + GROUP, at]
-        for tap in range(1, KCONV):
-            total = total + taps_ref[tap : tap + 1, at] * cin_ref[5 + tap : 5 + tap + GROUP, at]
-        sig, value = silu_parts(total)
-        mixed_ref[:, at] = value.astype(jnp.bfloat16)
-        slope_ref[:, at] = sig + value * (1.0 - sig)
+        cin_ref[chunk, 8 : 8 + GROUP, :] = xt_ref[:, at].astype(jnp.float32)
+        for row in range(0, GROUP, STRIP):
+            total = taps_ref[KCONV : KCONV + 1, at]
+            for tap in range(KCONV):
+                total = total + taps_ref[tap : tap + 1, at] * cin_ref[chunk, 5 + tap + row : 5 + tap + row + STRIP, :]
+            sig, value = silu_parts(total)
+            mixed_ref[row : row + STRIP, at] = value.astype(jnp.bfloat16)
+            slope_ref[row : row + STRIP, at] = sig + value * (1.0 - sig)
+        cin_ref[chunk, 0:8, :] = cin_ref[chunk, GROUP : GROUP + 8, :]
         return carry
 
     lax.fori_loop(0, CONVW // PAIR, conv_chunk, 0)
-    cin_ref[0:8, :] = cin_ref[GROUP : GROUP + 8, :]
 
     bm = mixed_ref[:, INNER : INNER + STATE]
     cm = mixed_ref[:, INNER + STATE : CONVW]
@@ -412,33 +415,42 @@
 
     dgn_ref[...] = ndot(go_ref[...], wout_ref[...])
 
-    def gate_rows(index, total):
+    def gate_rows(index, carry):
         rows = pl.ds(pl.multiple_of(index * 16, 16), 16)
-        ssd = ssd_ref[rows, :]
-        z = z_ref[rows, :].astype(jnp.float32)
-        sig, value = silu_parts(z)
-        gated = ssd * value
-        scale = lax.rsqrt(jnp.mean(gated * gated, -1, keepdims=True) + EPS)
-        unit = gated * scale
-        gain = lanes_ref[0:1, :]
-        gn_ref[rows, :] = (unit * gain).astype(jnp.bfloat16)
-        dgn = dgn_ref[rows, :]
-        total = total + dgn * unit
-        scaled = gain * dgn
-        mean = jnp.mean(scaled * unit, -1, keepdims=True)
-        dgated = scale * (scaled - unit * mean)
-        dssd = (dgated * value).astype(jnp.bfloat16)
-        dssd_ref[rows, :] = dssd
-        dz_ref[rows, :] = (dgated * ssd * (sig + value * (1.0 - sig))).astype(jnp.bfloat16)
-        xh = xh_ref[rows, :].astype(jnp.float32)
-        product = dssd.astype(jnp.float32) * (ssd - lanes_ref[1:2, :] * xh)
-        top = product.astype(jnp.bfloat16)
-        high_ref[rows, :] = top
-        rest_ref[rows, :] = (product - top.astype(jnp.float32)).astype(jnp.bfloat16)
-        return total
-
-    total = lax.fori_loop(0, GROUP // 16, gate_rows, jnp.zeros((16, INNER), jnp.float32))
-    ggain_ref[...] = ggain_ref[...] + total[0:8] + total[8:16]
+        kept = []
+        square = jnp.zeros((16, PAIR), jnp.float32)
+        cross = jnp.zeros((16, PAIR), jnp.float32)
+        for chunk in range(INNER // PAIR):
+            at = slice(chunk * PAIR, (chunk + 1) * PAIR)
+            sig, value = silu_parts(z_ref[rows, at].astype(jnp.float32))
+            gated = ssd_ref[rows, at] * value
+            square = square + gated * gated
+            cross = cross + lanes_ref[0:1, at] * dgn_ref[rows, at] * gated
+            kept.append((sig, value, gated))
+        scale = lax.rsqrt(jnp.sum(square, -1, keepdims=True) * (1.0 / INNER) + EPS)
+        pull = scale * scale * scale * (jnp.sum(cross, -1, keepdims=True) * (1.0 / INNER))
+        for chunk in range(INNER // PAIR):
+            at = slice(chunk * PAIR, (chunk + 1) * PAIR)
+            sig, value, gated = kept[chunk]
+            gain = lanes_ref[0:1, at]
+            ssd = ssd_ref[rows, at]
+            unit = gated * scale
+            gn_ref[rows, at] = (unit * gain).astype(jnp.bfloat16)
+            dgn = dgn_ref[rows, at]
+            term = dgn * unit
+            ggain_ref[:, at] += term[0:8] + term[8:16]
+            dgated = scale * (gain * dgn) - gated * pull
+            dssd = (dgated * value).astype(jnp.bfloat16)
+            dssd_ref[rows, at] = dssd
+            dz_ref[rows, at] = (dgated * ssd * (sig + value * (1.0 - sig))).astype(jnp.bfloat16)
+            xh = xh_ref[rows, at].astype(jnp.float32)
+            product = dssd.astype(jnp.float32) * (ssd - lanes_ref[1:2, at] * xh)
+            top = product.astype(jnp.bfloat16)
+            high_ref[rows, at] = top
+            rest_ref[rows, at] = (product - top.astype(jnp.float32)).astype(jnp.bfloat16)
+        return carry
+
+    lax.fori_loop(0, GROUP // 16, gate_rows, 0, unroll=4)
     seg = seg_ref[...]
     delta_ref[...] = jnp.dot(
         high_ref[...], seg, preferred_element_type=jnp.float32
@@ -460,7 +472,7 @@
     @pl.when(pl.program_id(0) == 0)
     def _():
         run_ref[...] = jnp.zeros_like(run_ref)
-        dext_ref[GROUP:, :] = jnp.zeros((8, CONVW), jnp.float32)
+        dext_ref[:, GROUP:, :] = jnp.zeros((CONVW // PAIR, 8, PAIR), jnp.float32)
         gconv_ref[...] = jnp.zeros_like(gconv_ref)
         ghead_ref[...] = jnp.zeros_like(ghead_ref)
         gskip_ref[...] = jnp.zeros_like(gskip_ref)
@@ -524,7 +536,7 @@
         high_ref[:, at] = top
         rest_ref[:, at] = (product - top.astype(jnp.float32)).astype(jnp.bfloat16)
         dmixed = (inner + lanes_ref[1:2, at] * df).astype(jnp.bfloat16).astype(jnp.float32)
-        dext_ref[0:GROUP, at] = dmixed * slope_ref[:, at]
+        dext_ref[pair, 0:GROUP, :] = dmixed * slope_ref[:, at]
         decay = jnp.exp(end)
         lane_ref[0:1, at] = jnp.sum(xf * dxs, 0, keepdims=True) + decay * jnp.sum(
             grad * state_ref[:, at], 0, keepdims=True
@@ -541,7 +553,7 @@
     )
     for place, part in enumerate((dbm, dcm)):
         at = slice(INNER + place * STATE, INNER + (place + 1) * STATE)
-        dext_ref[0:GROUP, at] = part.astype(jnp.bfloat16).astype(jnp.float32) * slope_ref[:, at]
+        dext_ref[INNER // PAIR + place, 0:GROUP, :] = part.astype(jnp.bfloat16).astype(jnp.float32) * slope_ref[:, at]
     seg = seg_ref[...]
     sums = jnp.dot(high_ref[...], seg, preferred_element_type=jnp.float32) + jnp.dot(
         rest_ref[...], seg, preferred_element_type=jnp.float32
@@ -560,20 +572,25 @@
 
     def conv_chunk(chunk, carry):
         at = pl.ds(pl.multiple_of(chunk * PAIR, PAIR), PAIR)
-        given = xt_ref[:, at].astype(jnp.float32)
-        total = None
-        for tap in range(KCONV):
-            moved = dext_ref[KCONV - 1 - tap : KCONV - 1 - tap + GROUP, at]
-            term = taps_ref[tap : tap + 1, at] * moved
-            total = term if total is None else total + term
-            gconv_ref[tap : tap + 1, at] += jnp.sum(given * moved, 0, keepdims=True)
-            if tap == KCONV - 1:
-                gconv_ref[KCONV : KCONV + 1, at] += jnp.sum(moved, 0, keepdims=True)
-        dxt_ref[:, at] = total.astype(jnp.bfloat16)
+        sums = [jnp.zeros((8, PAIR), jnp.float32)] * (KCONV + 1)
+        for row in range(0, GROUP, STRIP):
+            given = xt_ref[row : row + STRIP, at].astype(jnp.float32)
+            total = None
+            for tap in range(KCONV):
+                start = KCONV - 1 - tap + row
+                moved = dext_ref[chunk, start : start + STRIP, :]
+                term = taps_ref[tap : tap + 1, at] * moved
+                total = term if total is None else total + term
+                sums[tap] = sums[tap] + jnp.sum((given * moved).reshape(-1, 8, PAIR), 0)
+                if tap == KCONV - 1:
+                    sums[KCONV] = sums[KCONV] + jnp.sum(moved.reshape(-1, 8, PAIR), 0)
+            dxt_ref[row : row + STRIP, at] = total.astype(jnp.bfloat16)
+        for k in range(KCONV + 1):
+            gconv_ref[k : k + 1, at] += jnp.sum(sums[k], 0, keepdims=True)
         return carry
 
     lax.fori_loop(0, CONVW // PAIR, conv_chunk, 0)
-    dext_ref[GROUP:, :] = dext_ref[0:8, :]
+    dext_ref[:, GROUP:, :] = dext_ref[:, 0:8, :]
 
 
 def tall_block(width, count=None):
@@ -615,7 +632,7 @@
             shape_of(count * STATE, INNER, f32), shape_of(length, INNER, f32),
         ],
         scratch_shapes=[
-            pltpu.VMEM((STATE, INNER), f32), pltpu.VMEM((GROUP + 8, CONVW), f32),
+            pltpu.VMEM((STATE, INNER), f32), pltpu.VMEM((CONVW // PAIR, GROUP + 8, PAIR), f32),
             pltpu.VMEM((GROUP, GROUP), f32),
         ],
         compiler_params=kernel_options(),
@@ -674,7 +691,7 @@
             shape_of(8, INNER, f32),
         ],
         scratch_shapes=[
-            pltpu.VMEM((STATE, INNER), f32), pltpu.VMEM((GROUP + 8, CONVW), f32),
+            pltpu.VMEM((STATE, INNER), f32), pltpu.VMEM((CONVW // PAIR, GROUP + 8, PAIR), f32),
             pltpu.VMEM((GROUP, GROUP), f32), pltpu.VMEM((GROUP, GROUP), f32),
             pltpu.VMEM((GROUP, INNER), b16), pltpu.VMEM((GROUP, INNER), b16),
             pltpu.VMEM((GROUP, INNER), b16), pltpu.VMEM((GROUP, INNER), b16),
@@ -762,12 +779,13 @@
 FLIPS = ((0, 1), (1, 0), (1, 1))
 
 
-def reduce_core(parts, kind=jnp.bfloat16):
+def reduce_core(grads, kind=jnp.bfloat16):
     high = lax.axis_size("dp") // 4
     _, _, c, _ = grid_place()
-    parts = parts.reshape((high, 2, 2, 2, -1) + parts.shape[1:])
-    got = grid_send(pick(parts, (2,), (1 - c,)), (0, 0, 1, 0))
-    return add_up([pick(parts, (2,), (c,)), got]).astype(kind)
+    grads = [grad.reshape((high, 2, 2, 2) + grad.shape[1:]) for grad in grads]
+    sent = jnp.concatenate([pick(grad, (2,), (1 - c,)) for grad in grads], -1)
+    kept = jnp.concatenate([pick(grad, (2,), (c,)) for grad in grads], -1)
+    return add_up([kept, grid_send(sent, (0, 0, 1, 0))]).astype(kind)
 
 
 def plane_parts(parts):
@@ -789,65 +807,129 @@
     return found
 
 
-def place_in(array, axis, places, pieces):
-    for place, piece in zip(places, pieces):
-        array = lax.dynamic_update_slice_in_dim(array, jnp.expand_dims(piece, axis), place, axis)
-    return array
-
-
 def gather_line(own):
     high = lax.axis_size("dp") // 4
-    z, _, _, _ = grid_place()
-    places = [z] + [lax.rem(z + high - hop, high) for hop in range(1, high)]
-    pieces = [own] + [grid_send(own, (hop, 0, 0, 0)) for hop in range(1, high)]
-    return place_in(jnp.zeros((high,) + own.shape, own.dtype), 0, places, pieces)
+    return jnp.stack([own] + [grid_send(own, (hop, 0, 0, 0)) for hop in range(1, high)])
 
 
 def gather_plane(tall):
     return [tall] + [grid_send(tall, (0, fy, 0, fx)) for fy, fx in FLIPS]
 
 
+def join_kernel(cuts, place_ref, *refs):
+    pieces, outs = refs[:8], refs[8:]
+    high = pieces[0].shape[0]
+    for slot, piece in enumerate(pieces):
+        fy, fx = (((0, 0),) + FLIPS)[slot // 2]
+        y, c, x = place_ref[1] ^ fy, place_ref[2] ^ (slot % 2), place_ref[3] ^ fx
+        for hop in range(high):
+            z = lax.rem(place_ref[0] + high - hop, high)
+            for out, cut in zip(outs, cuts):
+                for j, (start, size) in enumerate(cut):
+                    out[z, y, c, x, j] = piece[hop, :, start : start + size]
+
+
+def core_pieces(pieces):
+    both = []
+    for piece in pieces:
+        both += [piece, grid_send(piece, (0, 0, 1, 0))]
+    return both
+
+
+def place_now():
+    return jnp.stack([jnp.asarray(p, jnp.int32) for p in grid_place()])
+
+
+def join_options():
+    return pltpu.CompilerParams(vmem_limit_bytes=24 * 1024 * 1024)
+
+
 def gather_core(pieces, cuts):
-    _, y, c, x = grid_place()
     high, rows, _ = pieces[0].shape
-    found = []
-    for cut in cuts:
-        shape = (high, 2, 2, 2, len(cut) * rows, cut[0].stop - cut[0].start)
-        found.append(jnp.zeros(shape, pieces[0].dtype))
-    for (fy, fx), piece in zip(((0, 0),) + FLIPS, pieces):
-        other = grid_send(piece, (0, 0, 1, 0))
-        for core, value in ((c, piece), (1 - c, other)):
-            for k, cut in enumerate(cuts):
-                for j, columns in enumerate(cut):
-                    part = value[:, :, columns].reshape(high, 1, 1, 1, rows, -1)
-                    start = (0, y ^ fy, core, x ^ fx, j * rows, 0)
-                    found[k] = lax.dynamic_update_slice(found[k], part, start)
-    return [full.reshape((-1, full.shape[-1])) for full in found]
-
-
-def gather_small(own):
-    high = lax.axis_size("dp") // 4
-    z, y, c, x = grid_place()
-    flat = own.reshape(1, -1)
-    held = jnp.concatenate([flat] + [grid_send(flat, (hop, 0, 0, 0)) for hop in range(1, high)], 0)
-    held = jnp.concatenate([held] + [grid_send(held, (0, fy, 0, fx)) for fy, fx in FLIPS], 0)
-    held = jnp.concatenate([held, grid_send(held, (0, 0, 1, 0))], 0)
-    owner = lax.broadcasted_iota(jnp.int32, (high * 8, high * 8), 0)
-    slot = lax.broadcasted_iota(jnp.int32, (high * 8, high * 8), 1)
-    hop, flip, core = slot % high, slot // high % 4, slot // (4 * high)
-    source = ((z + high - hop) % high * 2 + (y ^ (flip // 2))) * 2 + (c ^ core)
-    match = owner == source * 2 + (x ^ (flip % 2))
-    order = match.astype(own.dtype)
-    return jnp.dot(order, held, preferred_element_type=jnp.float32).reshape((-1,) + own.shape)
+    shapes = [(high, 2, 2, 2, len(cut), rows, cut[0][1]) for cut in cuts]
+    outs = pl.pallas_call(
+        functools.partial(join_kernel, cuts),
+        in_specs=[pl.BlockSpec(memory_space=pltpu.SMEM)] + [pl.BlockSpec(memory_space=pltpu.VMEM)] * 8,
+        out_specs=[pl.BlockSpec(memory_space=pltpu.VMEM)] * len(cuts),
+        out_shape=[jax.ShapeDtypeStruct(shape, pieces[0].dtype) for shape in shapes],
+        compiler_params=join_options(),
+        name="join_rows",
+    )(place_now(), *core_pieces(pieces))
+    return [full.reshape((-1, full.shape[-1])) for full in outs]
+
+
+def join_first_kernel(cuts, place_ref, *refs):
+    spots, masks, skip_ref = refs[8:11], refs[11:14], refs[14]
+    full_ref, taps_ref, lanes_ref, gain_ref, held_ref = refs[15:]
+    join_kernel(cuts, place_ref, *refs[:8], full_ref)
+    high = refs[0].shape[0]
+    for slot, piece in enumerate(refs[:8]):
+        fy, fx = (((0, 0),) + FLIPS)[slot // 2]
+        y, c, x = place_ref[1] ^ fy, place_ref[2] ^ (slot % 2), place_ref[3] ^ fx
+        for hop in range(high):
+            z = lax.rem(place_ref[0] + high - hop, high)
+            owner = ((z * 2 + y) * 2 + c) * 2 + x
+            block = piece[hop, 0:16, XTAIL - PAIR : XTAIL].astype(jnp.float32)
+            held_ref[owner] = block[0:8]
+
+    def line(row, which):
+        spread = jnp.dot(
+            held_ref[:, row, :].astype(jnp.bfloat16), spots[which][...], preferred_element_type=jnp.float32
+        )
+        return jnp.sum(spread * masks[which][...], 0, keepdims=True)
+
+    taps_ref[...] = jnp.zeros_like(taps_ref)
+    for row in range(KCONV + 1):
+        taps_ref[row : row + 1, :] = line(row, 0)
+    lanes_ref[...] = jnp.zeros_like(lanes_ref)
+    lanes_ref[0:1, :] = line(KCONV + 1, 1)
+    lanes_ref[1:2, :] = skip_ref[0:1, :]
+    gain_ref[...] = jnp.zeros_like(gain_ref)
+    gain_ref[0:1, :] = line(KCONV + 2, 2)
+
+
+def spread_tables(width, devices):
+    size = width // devices
+    lane = lax.broadcasted_iota(jnp.int32, (PAIR, width), 1)
+    spot = lax.broadcasted_iota(jnp.int32, (PAIR, width), 0) - (SPARE - XTAIL + PAIR) == lane % size
+    owner = lax.broadcasted_iota(jnp.int32, (devices, width), 0)
+    mask = owner == lax.broadcasted_iota(jnp.int32, (devices, width), 1) // size
+    return (spot.astype(jnp.bfloat16), mask.astype(jnp.float32))
+
+
+def gather_first(pieces, skip_lanes):
+    high, rows, width = pieces[0].shape
+    devices = 8 * high
+    tables = [spread_tables(w, devices) for w in (CONVW, INNER, WIDE)]
+    f32 = jnp.float32
+    full, taps, lanes, gain = pl.pallas_call(
+        functools.partial(join_first_kernel, (((0, width),),)),
+        in_specs=[pl.BlockSpec(memory_space=pltpu.SMEM)] + [pl.BlockSpec(memory_space=pltpu.VMEM)] * 15,
+        out_specs=[pl.BlockSpec(memory_space=pltpu.VMEM)] * 4,
+        out_shape=[
+            jax.ShapeDtypeStruct((high, 2, 2, 2, 1, rows, width), pieces[0].dtype),
+            shape_of(8, CONVW, f32), shape_of(8, INNER, f32), shape_of(8, WIDE, f32),
+        ],
+        scratch_shapes=[pltpu.VMEM((devices, 8, PAIR), f32)],
+        compiler_params=join_options(),
+        name="join_first",
+    )(
+        place_now(), *core_pieces(pieces), *[t[0] for t in tables], *[t[1] for t in tables],
+        jnp.broadcast_to(skip_lanes[None], (8, INNER)),
+    )
+    return (full.reshape(-1, width), taps, lanes, gain[0])
 
 
 def after(value, *others):
     return lax.optimization_barrier((value,) + others)[0]
 
 
+def swap_pick(parts):
+    return lax.dynamic_index_in_dim(parts, 1 - lax.axis_index("seq"), 0, False)
+
+
 def swap_send(parts):
-    place = lax.axis_index("seq")
-    return grid_send(lax.dynamic_index_in_dim(parts, 1 - place, 0, False), (0, 0, 0, 1))
+    return grid_send(swap_pick(parts), (0, 0, 0, 1))
 
 
 def swap_join(parts, got):
@@ -879,42 +961,36 @@
     micro, _, length, _ = x_in.shape
     rows = in_weight.shape[0]
     sizes = (conv_weight.shape[1], conv_bias.size, gate_gain.size, norm_gain.size)
-    first = jnp.pad(in_weight[:, INNER:], ((0, 0), (0, XTAIL - SPARE)))
+    x_sent = swap_pick(x_in[:, 0])
+    small = pack_small(norm_gain, conv_weight, conv_bias, gate_gain, jnp.zeros((8,), norm_gain.dtype))
+    small = jnp.pad(small[:, : XTAIL - SPARE], ((0, rows - KCONV - 4), (0, 0)))
+    first = jnp.concatenate([in_weight[:, INNER:], small], 1)
     second = jnp.concatenate([in_weight[:, :INNER], out_weight[:rows], out_weight[rows:]], 1)
-    small = pack_small(norm_gain, conv_weight, conv_bias, gate_gain, jnp.zeros((8,), norm_gain.dtype))
 
     line_first = gather_line(first)
-    xb = swap_halves(x_in[:, 0])
-    small = gather_small(after(small, line_first))
+    x_got = grid_send(x_sent, (0, 0, 0, 1))
+    xb = swap_join(x_in[:, 0], x_got)
     plane_first = gather_plane(line_first)
-    line_second = gather_line(after(second, line_first))
-    (w_xt,) = gather_core(plane_first, [[slice(0, XTAIL)]])
+    line_second = gather_line(after(second, plane_first[2]))
+    heads, skip_lanes = head_tables(dt_bias, rate, skip)
+    seg = head_segments()
+    w_xt, taps_bias, lanes, gain_in = gather_first(plane_first, skip_lanes)
     plane_second = gather_plane(after(line_second, *plane_first))
-
-    taps, bias, gate, gain_in = unpack_small(small, sizes)
-    gain_in = gain_in.reshape(-1)
-    gate = gate.reshape(-1).astype(jnp.float32)
-    taps = taps.transpose(1, 0, 2).reshape(KCONV, -1)
-    taps_bias = jnp.concatenate([taps, bias.reshape(1, -1)], 0).astype(jnp.float32)
-    taps_bias = jnp.pad(taps_bias, ((0, 7 - KCONV), (0, 0)))
     xf, r_in, normed = input_norm(xb, gain_in)
-    heads, skip_lanes = head_tables(dt_bias, rate, skip)
-    lanes = jnp.stack([gate, skip_lanes] + [jnp.zeros_like(skip_lanes)] * 6)
-    seg = head_segments()
     xt = low_dot(normed, w_xt)
     mixed, slope, states, ssd = run_scan(xt, taps_bias, heads, lanes)
     cot = swap_halves(after(grad_out[:, 0], *plane_first), ssd)
 
+    plane_second = [after(piece, ssd) for piece in plane_second]
     w_z, w_out = gather_core(
-        plane_second,
-        [[slice(0, INNER)], [slice(INNER, INNER + WIDE), slice(INNER + WIDE, 2 * INNER)]],
+        plane_second, (((0, INNER),), ((INNER, WIDE), (INNER + WIDE, WIDE)))
     )
     z = low_dot(normed, w_z)
     y, gnorm, dz, dssd, delta, ggain = run_gate(z, ssd, mixed, xb, cot, w_out, lanes, seg)
     grad_wout = tdot(gnorm, cot).astype(jnp.bfloat16).reshape(devices, 2, rows, WIDE)
     grad_wz = tdot(normed, dz).astype(jnp.bfloat16)
-    early = [grad_wz] + [grad_wout[:, k].reshape(WIDE, WIDE) for k in range(2)]
-    early = reduce_core(jnp.concatenate(early, 1))
+    early = [grad_wz] + [grad_wout[:, k] for k in range(2)]
+    early = reduce_core([part.reshape(devices, rows, -1) for part in early])
     dssd = after(dssd, early)
     y_got = swap_send(y.reshape(micro, length, WIDE))
     early = plane_parts(early)
@@ -924,7 +1000,7 @@
     dxt, y_got = lax.optimization_barrier((dxt, y_got) + tuple(early))[:2]
     y_out = swap_join(y.reshape(micro, length, WIDE), y_got).reshape(x_in.shape)
     grad_wxt = tdot(normed, dxt).astype(jnp.bfloat16)
-    late = reduce_core(grad_wxt)
+    late = reduce_core([grad_wxt.reshape(devices, rows, -1)])
     head_terms = jnp.concatenate(
         [ghead[0, :HEADS], ghead[1, :HEADS], jnp.sum(gskip[0].reshape(HEADS, HEADDIM), -1)]
     )
@@ -935,20 +1011,20 @@
         jnp.sum(ggain, 0).reshape(devices, -1),
         jnp.broadcast_to(head_terms, (devices, 3 * HEADS)),
     )[:, :, : XTAIL - SPARE]
-    tiny = reduce_core(tiny.reshape(devices * (KCONV + 4), -1), jnp.float32)
+    tiny = reduce_core([tiny], jnp.float32)
     tiny = jnp.pad(tiny, ((0, 0),) * 3 + ((0, rows - KCONV - 4), (SPARE, 0)))
     late = (late.astype(jnp.float32) + tiny).astype(jnp.bfloat16)
     dnormed = ndot(after(dz, late), w_z) + ndot(after(dxt, late), w_xt)
     late = plane_parts(late)
     dx = input_grad(xf, r_in, gain_in, dnormed, cot)
     dx_got = swap_send(after(dx.reshape(micro, length, WIDE), *late))
-    both = [add_up(parts).astype(jnp.bfloat16) for parts in (early, late)]
-    both = line_parts(jnp.concatenate(both, -1))
-    both = add_up(lax.optimization_barrier(tuple(both) + (dx_got,))[:-1])
+    early = add_up(line_parts(after(add_up(early).astype(jnp.bfloat16), late[2])))
+    late = tuple(line_parts(add_up(late).astype(jnp.bfloat16)))
+    late = add_up(lax.optimization_barrier(late + (dx_got,))[:-1])
     dx_in = swap_join(dx.reshape(micro, length, WIDE), dx_got).reshape(x_in.shape)
-    early, late = both[:, : 2 * INNER], both[:, 2 * INNER :]
     own_in = jnp.concatenate([early[:, :INNER], late[:, :SPARE]], 1)
-    own_out = jnp.concatenate([early[:, INNER : INNER + WIDE], early[:, INNER + WIDE :]], 0)
+    owned = early[:, INNER:]
+    own_out = jnp.concatenate([owned[:, :WIDE], owned[:, WIDE:]], 0)
     own = late[:, SPARE:]
     found = unpack_small(own, sizes)
     heads_sum = own[KCONV + 3]

time: 279 us -> 260 us (0.932); the launches traced: 274 us -> 258 us
  Pallas kernels: 92.2 us -> 78 us
  waiting for transfers between devices: 47.4 us -> 58.3 us
  local copies, waits for them, and re-layouts: 32.8 us -> 22 us
  other arithmetic: 19.6 us -> 27.6 us
  starting transfers between devices: 43.5 us -> 38.1 us
  matrix products: 35.8 us -> 32.1 us
    dynamic_update_slice x40 -> x0, local copies, waits for them, and re-layouts: 15.7 us -> none  [the longest x32 15.5 us: gather_core(): found[k] = lax.dynamic_update_slice(found[k], part, start)]
    ppermute x43 -> x39, waiting for transfers between devices: 47.4 us -> 58.3 us  [grid_send(): return lax.ppermute(array, ('dp', 'seq'), grid_moves(step))]
    pallas_call x1, Pallas kernels: 29.8 us -> 21.9 us  [run_gate(): pl.pallas_call(gate_kernel, grid=(length // GROUP,), in_specs=[tall_block...]
    pallas_call x1, Pallas kernels: 38.9 us -> 32.5 us  [run_backward(): pl.pallas_call(backward_kernel, grid=(count,), in_specs=[tall_block(XTAIL...]
    ppermute x43 -> x39, starting transfers between devices: 43.5 us -> 38.1 us  [grid_send(): return lax.ppermute(array, ('dp', 'seq'), grid_moves(step))]
    pallas_call x0 -> x2, Pallas kernels: none -> 4.15 us  [the longest x1 2.23 us: gather_core(): pl.pallas_call(functools.partial(join_kernel, cuts), in_specs=[pl.BlockSp...]
    pallas_call x1, Pallas kernels: 23.5 us -> 19.4 us  [run_scan(): pl.pallas_call(scan_kernel, grid=(count,), in_specs=[tall_block(XTAIL), f...]
    pad x6, local copies, waits for them, and re-layouts: 0.04 us -> 3.19 us  [pack_small(): jnp.pad(line, ((0, 0), (0, PAIR - line.shape[1])))]
  transfers between devices with their start and end apart: 43 -> 39, of which waited for: 12 -> 13; matrix products, arithmetic and copies ran while one was open for 19% -> 16% of each run, Pallas kernels for 23% -> 21%
where the time goes in v4:
time: 260 us; the launch traced here: 258 us
  Pallas kernels  78 us (30%)
  waiting for transfers between devices  58.3 us (22%)
  starting transfers between devices  38.1 us (15%)
  matrix products  32.1 us (12%)
  other arithmetic  27.6 us (11%)
  local copies, waits for them, and re-layouts  22 us (8%)
    ppermute x39, waiting for transfers between devices, grid_send(): return lax.ppermute(array, ('dp', 'seq'), grid_moves(step))  58.3 us
    ppermute x39, starting transfers between devices, grid_send(): return lax.ppermute(array, ('dp', 'seq'), grid_moves(step))  38.1 us
    pallas_call x1, Pallas kernels, run_backward(): pl.pallas_call(backward_kernel, grid=(count,), in_specs=[tall_block(XTAIL...  32.5 us
    pallas_call x1, Pallas kernels, run_gate(): pl.pallas_call(gate_kernel, grid=(length // GROUP,), in_specs=[tall_block...  21.9 us
    pallas_call x1, Pallas kernels, run_scan(): pl.pallas_call(scan_kernel, grid=(count,), in_specs=[tall_block(XTAIL), f...  19.4 us
    dot_general x3, matrix products, tdot(): lax.dot_general(left, right, (((0,), (0,)), ((), ())), preferred_element_...  14.5 us
    dot_general x2, matrix products, low_dot(): jnp.dot(left, right, preferred_element_type=jnp.float32)  11.1 us
    dot_general x2, matrix products, ndot(): lax.dot_general(left, right, (((1,), (1,)), ((), ())), preferred_element_...  6.44 us
  transfers between devices with their start and end apart: 39, of which 13 were waited for; matrix products, arithmetic and copies ran while one was open for 16% of the time, Pallas kernels for 21%

profile of v4, /device:TPU:8, one launch (start us, length us, event | category | flops | bytes accessed | tf_op | source)
XLA Modules:
  0.0 257.5 jit_solution(5709121616474772172)
XLA Ops:
  7.1 2.0 collective-permute-start.3
  9.0 2.1 dynamic-slice_bitcast_fusion.6
  20.1 6.3 %collective-permute-done.7.refs_4_ = bf16[4,24,1920]{2,1,0:T(8,128)(2,1)S(1)} collective-permute-done((bf16[4,24,1920]{2,1,0:T(8,128)(2,1)S(1)}, bf16[4,24,1920]{2,1,0:T(8,128)(2,1)S(1)}, u32[]{:S(2)}, u32[]{:S(2)}) %collective-permute-start.7) | collective-permute-done | bytes 368672 | tf_op jit(solution)/shard_map/ppermute | solution.py:759
  26.4 2.0 collective-permute-start.12
  28.4 12.3 %collective-permute-done.9.refs_6_ = bf16[4,24,1920]{2,1,0:T(8,128)(2,1)} collective-permute-done((bf16[4,24,1920]{2,1,0:T(8,128)(2,1)S(1)}, bf16[4,24,1920]{2,1,0:T(8,128)(2,1)}, u32[]{:S(2)}, u32[]{:S(2)}) %collective-permute-start.9) | collective-permute-done | bytes 368672 | tf_op jit(solution)/shard_map/ppermute | solution.py:759
  42.3 3.3 %collective-permute-done.5.refs_2_ = bf16[4,24,1920]{2,1,0:T(8,128)(2,1)} collective-permute-done((bf16[4,24,1920]{2,1,0:T(8,128)(2,1)S(1)}, bf16[4,24,1920]{2,1,0:T(8,128)(2,1)}, u32[]{:S(2)}, u32[]{:S(2)}) %collective-permute-start.5) | collective-permute-done | bytes 368672 | tf_op jit(solution)/shard_map/ppermute | solution.py:759
  45.6 2.1 dynamic-slice_bitcast_fusion.5
  56.0 1.9 join_first.1
  58.0 6.1 %convolution_convert_fusion.1.xt_ref = bf16[1024,1920]{1,0:T(8,128)(2,1)} fusion(bf16[768,1920]{1,0:T(8,128)(2,1)S(1)} %bitcast.158, f32[768]{0:T(1024)S(1)} %slice_reduce_fusion.2, f32[1024]{0:T(1024)S(1)} %get-tuple-element.156, bf16[512,768]{1,0:T(8,128)(2,1)S(1)} %get-tuple-element.131, bf16[512,768]{1,0:T(8,128)(2,1)S(1)} %get-tuple-element.130), kind=kOutput, calls=%fused_computation.6 | convolution fusion | flops 3027369984 | bytes 8461312 | tf_op jit(solution)/shard_map/dot_general | solution.py:735
  64.2 19.4 %scan_forward.1 = (bf16[1024,1792]{1,0:T(8,128)(2,1)}, f32[1024,1792]{1,0:T(8,128)}, f32[512,1536]{1,0:T(8,128)S(1)}, f32[1024,1536]{1,0:T(8,128)}) custom-call(bf16[1024,1920]{1,0:T(8,128)(2,1)} %convolution_convert_fusion.1.xt_ref, f32[8,1792]{1,0:T(8,128)S(1)} %get-tuple-element.54.taps_ref, f32[8,128]{1,0:T(8,128)S(1)} %maximum_maximum_fusion.heads_ref, ...), custom_call_target="tpu_custom_call" | custom-call | flops 24999999488 | bytes 30000000 | tf_op jit(solution)/shard_map/scan_forward/pallas_call | solution.py:620
  85.8 7.5 %collective-permute-done.15.refs_2_ = bf16[4,24,3072]{2,1,0:T(8,128)(2,1)} collective-permute-done((bf16[4,24,3072]{2,1,0:T(8,128)(2,1)S(1)}, bf16[4,24,3072]{2,1,0:T(8,128)(2,1)}, u32[]{:S(2)}, u32[]{:S(2)}) %collective-permute-start.15) | collective-permute-done | bytes 589856 | tf_op jit(solution)/shard_map/ppermute | solution.py:759
  98.0 2.2 join_rows.1
  100.3 5.0 %convolution_convert_fusion.z_ref = bf16[1024,1536]{1,0:T(8,128)(2,1)} fusion(bf16[768,1536]{1,0:T(8,128)(2,1)S(1)} %bitcast.160, f32[768]{0:T(1024)S(1)} %slice_reduce_fusion.2, f32[1024]{0:T(1024)S(1)} %copy-done.30, bf16[512,768]{1,0:T(8,128)(2,1)S(1)} %copy-done.13, bf16[512,768]{1,0:T(8,128)(2,1)S(1)} %copy-done.10), kind=kOutput, calls=%fused_computation.5 | convolution fusion | flops 2422996992 | bytes 7085056 | tf_op jit(solution)/shard_map/dot_general | solution.py:735
  105.3 21.9 %gate_both_ways.1 = (bf16[1024,768]{1,0:T(8,128)(2,1)S(1)}, bf16[1024,1536]{1,0:T(8,128)(2,1)}, bf16[1024,1536]{1,0:T(8,128)(2,1)}, bf16[1024,1536]{1,0:T(8,128)...) custom-call(bf16[1024,1536]{1,0:T(8,128)(2,1)} %convolution_convert_fusion.z_ref, ...), custom_call_target="tpu_custom_call" | custom-call | flops 20000000000 | bytes 30000000 | tf_op jit(solution)/shard_map/gate_both_ways/pallas_call | solution.py:647
  127.2 5.1 %convolution_convert_fusion.3 = bf16[768,1536]{1,0:T(8,128)(2,1)S(1)} fusion(bf16[1024,1536]{1,0:T(8,128)(2,1)} %get-tuple-element.81, f32[768]{0:T(1024)S(1)} %slice_reduce_fusion.2, f32[1024]{0:T(1024)S(1)} %copy-done.30, bf16[512,768]{1,0:T(8,128)(2,1)S(1)} %copy-done.13, bf16[512,768]{1,0:T(8,128)(2,1)S(1)} %copy-done.10), kind=kOutput, calls=%fused_computation.8 | convolution fusion | flops 2422603776 | bytes 7085056 | tf_op jit(solution)/shard_map/dot_general | solution.py:52
  132.3 3.2 %convolution_convert_fusion.2 = bf16[1536,768]{1,0:T(8,128)(2,1)S(1)} fusion(bf16[1024,1536]{1,0:T(8,128)(2,1)S(1)} %copy-done.41, bf16[512,768]{1,0:T(8,128)(2,1)S(1)} %get-tuple-element.129, bf16[512,768]{1,0:T(8,128)(2,1)S(1)} %get-tuple-element.128), kind=kOutput, calls=%fused_computation.7 | convolution fusion | flops 2420244480 | bytes 7077888 | tf_op jit(solution)/shard_map/dot_general | solution.py:52
  144.6 2.9 %add_convert_fusion = bf16[4,2,2,24,3072]{4,3,2,1,0:T(8,128)(2,1)S(1)} fusion(bf16[4,2,2,24,3072]{4,3,2,1,0:T(8,128)(2,1)} %collective-permute-done.22, bf16[4,2,2,24,768]{4,3,2,1,0:T(8,128)(2,1)} %get-tuple-element.137, bf16[4,2,2,24,768]{4,3,2,1,0:T(8,128)(2,1)S(1)} %get-tuple-element.135, bf16[4,2,2,24,1536]{4,3,2,1,0:T(8,128)(2,1)} %get-tuple-element.124), kind=kLoop, calls=%fused_computation.4 | loop fusion | flops 10616832 | bytes 7077888 | tf_op jit(solution)/shard_map/convert_element_type | solution.py:788
  152.3 32.5 %scan_backward.1 = (bf16[1024,1920]{1,0:T(8,128)(2,1)}, f32[8,1792]{1,0:T(8,128)S(1)}, f32[8,128]{1,0:T(8,128)S(1)}, f32[8,1536]{1,0:T(8,128)S(1)}) custom-call(bf16[1024,1920]{1,0:T(8,128)(2,1)} %convolution_convert_fusion.1.xt_ref, bf16[1024,1792]{1,0:T(8,128)(2,1)} %get-tuple-element.62.xh_ref.mixed_ref, f32[1024,1792]{1,0:T(8,128)} %get-tuple-element.67.slope_ref, ...), custom_call_target="tpu_custom_call" | custom-call | flops 30000001024 | bytes 30000000 | tf_op jit(solution)/shard_map/scan_backward/pallas_call | solution.py:676
  185.4 2.1 collective-permute-done.26
  187.5 2.8 %add_convert_fusion.2 = bf16[4,24,3072]{2,1,0:T(8,128)(2,1)} fusion(bf16[4,24,3072]{2,1,0:T(8,128)(2,1)} %collective-permute-done.26, bf16[4,24,3072]{2,1,0:T(8,128)(2,1)} %collective-permute-done.25, bf16[4,24,3072]{2,1,0:T(8,128)(2,1)} %collective-permute-done.24, bf16[4,2,2,24,3072]{4,3,2,1,0:T(8,128)(2,1)} %copy-done.15, s32[]{:T(128)S(6)} %select_n.173, ...), kind=kLoop, calls=%fused_computation.28 | loop fusion | flops 2359296 | bytes 2949128 | tf_op jit(solution)/shard_map/convert_element_type | solution.py:1021
  190.4 6.2 %convolution_convert_fusion.4 = bf16[768,1920]{1,0:T(8,128)(2,1)S(1)} fusion(bf16[1024,1920]{1,0:T(8,128)(2,1)} %get-tuple-element.82, f32[768]{0:T(1024)S(1)} %copy-done.34, f32[1024]{0:T(1024)S(1)} %copy-done.31, bf16[512,768]{1,0:T(8,128)(2,1)S(1)} %copy-done.14, bf16[512,768]{1,0:T(8,128)(2,1)S(1)} %copy-done.11), kind=kOutput, calls=%fused_computation.9 | convolution fusion | flops 3026878464 | bytes 8461312 | tf_op jit(solution)/shard_map/dot_general | solution.py:52
  200.2 2.6 %collective-permute-done.28 = f32[4,2,2,8,104]{4,3,2,1,0:T(8,128)S(1)} collective-permute-done((f32[4,2,2,8,104]{4,3,2,1,0:T(8,128)S(1)}, f32[4,2,2,8,104]{4,3,2,1,0:T(8,128)S(1)}, u32[]{:S(2)}, u32[]{:S(2)}) %collective-permute-start.28) | collective-permute-done | bytes 53280 | tf_op jit(solution)/shard_map/ppermute | solution.py:759
  205.5 1.9 add_convert_fusion.1
  211.1 2.6 %fusion.47 = f32[1024,768]{1,0:T(8,128)S(1)} fusion(bf16[1024,1536]{1,0:T(8,128)(2,1)S(1)} %copy-done.40, bf16[768,1536]{1,0:T(8,128)(2,1)S(1)} %bitcast.161), kind=kOutput, calls=%fused_computation.161 | convolution fusion | flops 2415919104 | bytes 8650752 | tf_op jit(solution)/shard_map/dot_general | solution.py:58
  213.8 3.8 %fusion.7 = (f32[1024]{0:T(1024)S(1)}, f32[1024,768]{1,0:T(8,128)S(1)}) fusion(bf16[512,768]{1,0:T(8,128)(2,1)S(1)} %copy-done.14, bf16[512,768]{1,0:T(8,128)(2,1)S(1)} %copy-done.11, f32[1024,768]{1,0:T(8,128)S(1)} %fusion.47, bf16[1024,1920]{1,0:T(8,128)(2,1)S(1)} %copy-done.39, bf16[768,1920]{1,0:T(8,128)(2,1)S(1)} %bitcast.159, f32[768]{0:T(1024)S(1)} %copy-done.34), kind=kOutput, calls=%fused_computation.17 | convolution fusion | flops 3026189312 | bytes 14752768 | tf_op jit(solution)/shard_map/dot_general | solution.py:58
  217.6 2.1 fusion.6
  220.2 3.4 %collective-permute-start.34 = (bf16[24,3072]{1,0:T(8,128)(2,1)S(1)}, bf16[24,3072]{1,0:T(8,128)(2,1)S(1)}, u32[]{:S(2)}, u32[]{:S(2)}) collective-permute-start(bf16[24,3072]{1,0:T(8,128)(2,1)S(1)} %get-tuple-element.141), channel_id=1, source_target_pairs={{0,16},{1,17},{2,18},{3,19},{4,20},{5,21},{6,22},{7,23},{8,24},{9,... | collective-permute-start | bytes 442376 | tf_op jit(solution)/shard_map/ppermute | solution.py:759
  223.6 3.7 %collective-permute-done.31 = bf16[4,24,1920]{2,1,0:T(8,128)(2,1)S(1)} collective-permute-done((bf16[4,24,1920]{2,1,0:T(8,128)(2,1)S(1)}, bf16[4,24,1920]{2,1,0:T(8,128)(2,1)S(1)}, u32[]{:S(2)}, u32[]{:S(2)}) %collective-permute-start.31) | collective-permute-done | bytes 368672 | tf_op jit(solution)/shard_map/ppermute | solution.py:759
  228.0 3.4 %collective-permute-start.37 = (bf16[24,1920]{1,0:T(8,128)(2,1)S(1)}, bf16[24,1920]{1,0:T(8,128)(2,1)S(1)}, u32[]{:S(2)}, u32[]{:S(2)}) collective-permute-start(bf16[24,1920]{1,0:T(8,128)(2,1)S(1)} %get-tuple-element.143), channel_id=1, source_target_pairs={{0,16},{1,17},{2,18},{3,19},{4,20},{5,21},{6,22},{7,23},{8,24},{9,... | collective-permute-start | bytes 276488 | tf_op jit(solution)/shard_map/ppermute | solution.py:759
  231.5 5.4 %collective-permute-done.34 = bf16[24,3072]{1,0:T(8,128)(2,1)S(1)} collective-permute-done((bf16[24,3072]{1,0:T(8,128)(2,1)S(1)}, bf16[24,3072]{1,0:T(8,128)(2,1)S(1)}, u32[]{:S(2)}, u32[]{:S(2)}) %collective-permute-start.34) | collective-permute-done | bytes 147488 | tf_op jit(solution)/shard_map/ppermute | solution.py:759
  241.0 2.5 collective-permute-done.38
  243.4 8.8 %collective-permute-done.32 = bf16[512,768]{1,0:T(8,128)(2,1)S(1)} collective-permute-done((bf16[512,768]{1,0:T(8,128)(2,1)S(1)}, bf16[512,768]{1,0:T(8,128)(2,1)S(1)}, u32[]{:S(2)}, u32[]{:S(2)}) %collective-permute-start.32) | collective-permute-done | bytes 786464 | tf_op jit(solution)/shard_map/ppermute | solution.py:759
  (251 shorter events, 66.6 us)
Async XLA Ops:
  4.4 11.0 %collective-permute-start.1 = (bf16[24,1920]{1,0:T(8,128)(2,1)S(1)}, bf16[24,1920]{1,0:T(8,128)(2,1)S(1)}, u32[]{:S(2)}, u32[]{:S(2)}) collective-permute-start(bf16[24,1920]{1,0:T(8,128)(2,1)S(1)} %fusion.19), channel_id=1, source_target_pairs={{0,8},{1,9},{2,10},{3,11},{4,12},{5,13},{6,14},{7,15},{8,16},{9,17... | collective-permute-start | bytes 276488 | tf_op jit(solution)/shard_map/ppermute | solution.py:759
  6.0 9.4 %collective-permute-start.2 = (bf16[24,1920]{1,0:T(8,128)(2,1)S(1)}, bf16[24,1920]{1,0:T(8,128)(2,1)S(1)}, u32[]{:S(2)}, u32[]{:S(2)}) collective-permute-start(bf16[24,1920]{1,0:T(8,128)(2,1)S(1)} %fusion.19), channel_id=1, source_target_pairs={{0,16},{1,17},{2,18},{3,19},{4,20},{5,21},{6,22},{7,23},{8,24},{9,... | collective-permute-start | bytes 276488 | tf_op jit(solution)/shard_map/ppermute | solution.py:759
  7.1 8.6 %collective-permute-start.3 = (bf16[24,1920]{1,0:T(8,128)(2,1)S(1)}, bf16[24,1920]{1,0:T(8,128)(2,1)S(1)}, u32[]{:S(2)}, u32[]{:S(2)}) collective-permute-start(bf16[24,1920]{1,0:T(8,128)(2,1)S(1)} %fusion.19), channel_id=1, source_target_pairs={{0,24},{1,25},{2,26},{3,27},{4,28},{5,29},{6,30},{7,31},{8,0},{9,1... | collective-permute-start | bytes 276488 | tf_op jit(solution)/shard_map/ppermute | solution.py:759
  11.1 38.7 %collective-permute-start = (bf16[512,768]{1,0:T(8,128)(2,1)}, bf16[512,768]{1,0:T(8,128)(2,1)}, u32[]{:S(2)}, u32[]{:S(2)}) collective-permute-start(bf16[512,768]{1,0:T(8,128)(2,1)} %dynamic-slice_bitcast_fusion.6), channel_id=1, source_target_pairs={{0,1},{1,0},{2,3},{3,2},{4,5},{5,4},{6,7},{7,6},{8,9},{9,8},{10,11... | collective-permute-start | bytes 2359304 | tf_op jit(solution)/shard_map/ppermute | solution.py:759
  15.7 10.7 %collective-permute-start.7 = (bf16[4,24,1920]{2,1,0:T(8,128)(2,1)S(1)}, bf16[4,24,1920]{2,1,0:T(8,128)(2,1)S(1)}, u32[]{:S(2)}, u32[]{:S(2)}) collective-permute-start(bf16[4,24,1920]{2,1,0:T(8,128)(2,1)S(1)} %pad_maximum_fusion.6.refs_0_), channel_id=1, source_target_pairs={{0,4},{1,5},{2,6},{3,7},{4,0},{5,1},{6,2},{7,3},{8,12},{9,13},{10,... | collective-permute-start | bytes 1105928 | tf_op jit(solution)/shard_map/ppermute | solution.py:759
  17.3 23.5 %collective-permute-start.9 = (bf16[4,24,1920]{2,1,0:T(8,128)(2,1)S(1)}, bf16[4,24,1920]{2,1,0:T(8,128)(2,1)}, u32[]{:S(2)}, u32[]{:S(2)}) collective-permute-start(bf16[4,24,1920]{2,1,0:T(8,128)(2,1)S(1)} %pad_maximum_fusion.6.refs_0_), channel_id=1, source_target_pairs={{0,5},{1,4},{2,7},{3,6},{4,1},{5,0},{6,3},{7,2},{8,13},{9,12},{10,... | collective-permute-start | bytes 1105928 | tf_op jit(solution)/shard_map/ppermute | solution.py:759
  19.3 26.4 %collective-permute-start.5 = (bf16[4,24,1920]{2,1,0:T(8,128)(2,1)S(1)}, bf16[4,24,1920]{2,1,0:T(8,128)(2,1)}, u32[]{:S(2)}, u32[]{:S(2)}) collective-permute-start(bf16[4,24,1920]{2,1,0:T(8,128)(2,1)S(1)} %pad_maximum_fusion.6.refs_0_), channel_id=1, source_target_pairs={{0,1},{1,0},{2,3},{3,2},{4,5},{5,4},{6,7},{7,6},{8,9},{9,8},{10,11... | collective-permute-start | bytes 1105928 | tf_op jit(solution)/shard_map/ppermute | solution.py:759
  26.4 21.4 %collective-permute-start.11 = (bf16[24,3072]{1,0:T(8,128)(2,1)S(1)}, bf16[24,3072]{1,0:T(8,128)(2,1)S(1)}, u32[]{:S(2)}, u32[]{:S(2)}) collective-permute-start(bf16[24,3072]{1,0:T(8,128)(2,1)S(1)} %pad_maximum_fusion.8), channel_id=1, source_target_pairs={{0,8},{1,9},{2,10},{3,11},{4,12},{5,13},{6,14},{7,15},{8,16},{9,17... | collective-permute-start | bytes 442376 | tf_op jit(solution)/shard_map/ppermute | solution.py:759
  26.4 22.9 %collective-permute-start.12 = (bf16[24,3072]{1,0:T(8,128)(2,1)S(1)}, bf16[24,3072]{1,0:T(8,128)(2,1)S(1)}, u32[]{:S(2)}, u32[]{:S(2)}) collective-permute-start(bf16[24,3072]{1,0:T(8,128)(2,1)S(1)} %pad_maximum_fusion.8), channel_id=1, source_target_pairs={{0,16},{1,17},{2,18},{3,19},{4,20},{5,21},{6,22},{7,23},{8,24},{9,... | collective-permute-start | bytes 442376 | tf_op jit(solution)/shard_map/ppermute | solution.py:759
  40.7 8.7 %collective-permute-start.13 = (bf16[24,3072]{1,0:T(8,128)(2,1)S(1)}, bf16[24,3072]{1,0:T(8,128)(2,1)S(1)}, u32[]{:S(2)}, u32[]{:S(2)}) collective-permute-start(bf16[24,3072]{1,0:T(8,128)(2,1)S(1)} %pad_maximum_fusion.8), channel_id=1, source_target_pairs={{0,24},{1,25},{2,26},{3,27},{4,28},{5,29},{6,30},{7,31},{8,0},{9,1... | collective-permute-start | bytes 442376 | tf_op jit(solution)/shard_map/ppermute | solution.py:759
  45.6 6.8 %collective-permute-start.4 = (bf16[4,24,1920]{2,1,0:T(8,128)(2,1)S(1)}, bf16[4,24,1920]{2,1,0:T(8,128)(2,1)S(1)}, u32[]{:S(2)}, u32[]{:S(2)}) collective-permute-start(bf16[4,24,1920]{2,1,0:T(8,128)(2,1)S(1)} %pad_maximum_fusion.6.refs_0_), channel_id=1, source_target_pairs={{0,2},{1,3},{2,0},{3,1},{4,6},{5,7},{6,4},{7,5},{8,10},{9,11},{10,... | collective-permute-start | bytes 1105928 | tf_op jit(solution)/shard_map/ppermute | solution.py:759
  47.7 48.5 %collective-permute-start.21 = (bf16[512,768]{1,0:T(8,128)(2,1)}, bf16[512,768]{1,0:T(8,128)(2,1)}, u32[]{:S(2)}, u32[]{:S(2)}) collective-permute-start(bf16[512,768]{1,0:T(8,128)(2,1)} %dynamic-slice_bitcast_fusion.5), channel_id=1, source_target_pairs={{0,1},{1,0},{2,3},{3,2},{4,5},{5,4},{6,7},{7,6},{8,9},{9,8},{10,11... | collective-permute-start | bytes 2359304 | tf_op jit(solution)/shard_map/ppermute | solution.py:759
  52.5 32.7 %collective-permute-start.19 = (bf16[4,24,3072]{2,1,0:T(8,128)(2,1)S(1)}, bf16[4,24,3072]{2,1,0:T(8,128)(2,1)S(1)}, u32[]{:S(2)}, u32[]{:S(2)}) collective-permute-start(bf16[4,24,3072]{2,1,0:T(8,128)(2,1)S(1)} %pad_maximum_fusion.5.refs_0_), channel_id=1, source_target_pairs={{0,5},{1,4},{2,7},{3,6},{4,1},{5,0},{6,3},{7,2},{8,13},{9,12},{10,... | collective-permute-start | bytes 1769480 | tf_op jit(solution)/shard_map/ppermute | solution.py:759
  54.0 31.8 %collective-permute-start.17 = (bf16[4,24,3072]{2,1,0:T(8,128)(2,1)S(1)}, bf16[4,24,3072]{2,1,0:T(8,128)(2,1)}, u32[]{:S(2)}, u32[]{:S(2)}) collective-permute-start(bf16[4,24,3072]{2,1,0:T(8,128)(2,1)S(1)} %pad_maximum_fusion.5.refs_0_), channel_id=1, source_target_pairs={{0,4},{1,5},{2,6},{3,7},{4,0},{5,1},{6,2},{7,3},{8,12},{9,13},{10,... | collective-permute-start | bytes 1769480 | tf_op jit(solution)/shard_map/ppermute | solution.py:759
  54.5 38.8 %collective-permute-start.15 = (bf16[4,24,3072]{2,1,0:T(8,128)(2,1)S(1)}, bf16[4,24,3072]{2,1,0:T(8,128)(2,1)}, u32[]{:S(2)}, u32[]{:S(2)}) collective-permute-start(bf16[4,24,3072]{2,1,0:T(8,128)(2,1)S(1)} %pad_maximum_fusion.5.refs_0_), channel_id=1, source_target_pairs={{0,1},{1,0},{2,3},{3,2},{4,5},{5,4},{6,7},{7,6},{8,9},{9,8},{10,11... | collective-permute-start | bytes 1769480 | tf_op jit(solution)/shard_map/ppermute | solution.py:759
  85.2 12.7 %collective-permute-start.14 = (bf16[4,24,3072]{2,1,0:T(8,128)(2,1)S(1)}, bf16[4,24,3072]{2,1,0:T(8,128)(2,1)S(1)}, u32[]{:S(2)}, u32[]{:S(2)}) collective-permute-start(bf16[4,24,3072]{2,1,0:T(8,128)(2,1)S(1)} %pad_maximum_fusion.5.refs_0_), channel_id=1, source_target_pairs={{0,2},{1,3},{2,0},{3,1},{4,6},{5,7},{6,4},{7,5},{8,10},{9,11},{10,... | collective-permute-start | bytes 1769480 | tf_op jit(solution)/shard_map/ppermute | solution.py:759
  85.2 12.7 %collective-permute-start.20 = (bf16[4,24,3072]{2,1,0:T(8,128)(2,1)S(1)}, bf16[4,24,3072]{2,1,0:T(8,128)(2,1)S(1)}, u32[]{:S(2)}, u32[]{:S(2)}) collective-permute-start(bf16[4,24,3072]{2,1,0:T(8,128)(2,1)S(1)} %collective-permute-done.19.refs_6_), channel_id=1, source_target_pairs={{0,2},{1,3},{2,0},{3,1},{4,6},{5,7},{6,4},{7,5},{8,10},{9,11},{10,... | collective-permute-start | bytes 1769480 | tf_op jit(solution)/shard_map/ppermute | solution.py:759
  85.7 12.2 %collective-permute-start.18 = (bf16[4,24,3072]{2,1,0:T(8,128)(2,1)}, bf16[4,24,3072]{2,1,0:T(8,128)(2,1)S(1)}, u32[]{:S(2)}, u32[]{:S(2)}) collective-permute-start(bf16[4,24,3072]{2,1,0:T(8,128)(2,1)} %collective-permute-done.17.refs_4_), channel_id=1, source_target_pairs={{0,2},{1,3},{2,0},{3,1},{4,6},{5,7},{6,4},{7,5},{8,10},{9,11},{10,... | collective-permute-start | bytes 1769480 | tf_op jit(solution)/shard_map/ppermute | solution.py:759
  141.5 48.8 %collective-permute-start.23 = (bf16[512,768]{1,0:T(8,128)(2,1)}, bf16[512,768]{1,0:T(8,128)(2,1)}, u32[]{:S(2)}, u32[]{:S(2)}) collective-permute-start(bf16[512,768]{1,0:T(8,128)(2,1)} %dynamic-slice_bitcast_fusion.4), channel_id=1, source_target_pairs={{0,1},{1,0},{2,3},{3,2},{4,5},{5,4},{6,7},{7,6},{8,9},{9,8},{10,11... | collective-permute-start | bytes 2359304 | tf_op jit(solution)/shard_map/ppermute | solution.py:759
  148.8 36.6 %collective-permute-start.24 = (bf16[4,24,3072]{2,1,0:T(8,128)(2,1)}, bf16[4,24,3072]{2,1,0:T(8,128)(2,1)}, u32[]{:S(2)}, u32[]{:S(2)}) collective-permute-start(bf16[4,24,3072]{2,1,0:T(8,128)(2,1)} %get-tuple-element.121), channel_id=1, source_target_pairs={{0,1},{1,0},{2,3},{3,2},{4,5},{5,4},{6,7},{7,6},{8,9},{9,8},{10,11... | collective-permute-start | bytes 1769480 | tf_op jit(solution)/shard_map/ppermute | solution.py:759
  150.3 35.1 %collective-permute-start.25 = (bf16[4,24,3072]{2,1,0:T(8,128)(2,1)}, bf16[4,24,3072]{2,1,0:T(8,128)(2,1)}, u32[]{:S(2)}, u32[]{:S(2)}) collective-permute-start(bf16[4,24,3072]{2,1,0:T(8,128)(2,1)} %get-tuple-element.123), channel_id=1, source_target_pairs={{0,4},{1,5},{2,6},{3,7},{4,0},{5,1},{6,2},{7,3},{8,12},{9,13},{10,... | collective-permute-start | bytes 1769480 | tf_op jit(solution)/shard_map/ppermute | solution.py:759
  151.9 35.7 %collective-permute-start.26 = (bf16[4,24,3072]{2,1,0:T(8,128)(2,1)}, bf16[4,24,3072]{2,1,0:T(8,128)(2,1)}, u32[]{:S(2)}, u32[]{:S(2)}) collective-permute-start(bf16[4,24,3072]{2,1,0:T(8,128)(2,1)} %get-tuple-element.122), channel_id=1, source_target_pairs={{0,5},{1,4},{2,7},{3,6},{4,1},{5,0},{6,3},{7,2},{8,13},{9,12},{10,... | collective-permute-start | bytes 1769480 | tf_op jit(solution)/shard_map/ppermute | solution.py:759
  207.5 12.2 %collective-permute-start.30 = (bf16[4,24,1920]{2,1,0:T(8,128)(2,1)S(1)}, bf16[4,24,1920]{2,1,0:T(8,128)(2,1)S(1)}, u32[]{:S(2)}, u32[]{:S(2)}) collective-permute-start(bf16[4,24,1920]{2,1,0:T(8,128)(2,1)S(1)} %get-tuple-element.134), channel_id=1, source_target_pairs={{0,4},{1,5},{2,6},{3,7},{4,0},{5,1},{6,2},{7,3},{8,12},{9,13},{10,... | collective-permute-start | bytes 1105928 | tf_op jit(solution)/shard_map/ppermute | solution.py:759
  208.1 15.5 %collective-permute-start.29 = (bf16[4,24,1920]{2,1,0:T(8,128)(2,1)S(1)}, bf16[4,24,1920]{2,1,0:T(8,128)(2,1)S(1)}, u32[]{:S(2)}, u32[]{:S(2)}) collective-permute-start(bf16[4,24,1920]{2,1,0:T(8,128)(2,1)S(1)} %get-tuple-element.132), channel_id=1, source_target_pairs={{0,1},{1,0},{2,3},{3,2},{4,5},{5,4},{6,7},{7,6},{8,9},{9,8},{10,11... | collective-permute-start | bytes 1105928 | tf_op jit(solution)/shard_map/ppermute | solution.py:759
  209.6 17.7 %collective-permute-start.31 = (bf16[4,24,1920]{2,1,0:T(8,128)(2,1)S(1)}, bf16[4,24,1920]{2,1,0:T(8,128)(2,1)S(1)}, u32[]{:S(2)}, u32[]{:S(2)}) collective-permute-start(bf16[4,24,1920]{2,1,0:T(8,128)(2,1)S(1)} %get-tuple-element.133), channel_id=1, source_target_pairs={{0,5},{1,4},{2,7},{3,6},{4,1},{5,0},{6,3},{7,2},{8,13},{9,12},{10,... | collective-permute-start | bytes 1105928 | tf_op jit(solution)/shard_map/ppermute | solution.py:759
  219.8 11.6 %collective-permute-start.33 = (bf16[24,3072]{1,0:T(8,128)(2,1)S(1)}, bf16[24,3072]{1,0:T(8,128)(2,1)S(1)}, u32[]{:S(2)}, u32[]{:S(2)}) collective-permute-start(bf16[24,3072]{1,0:T(8,128)(2,1)S(1)} %get-tuple-element.139), channel_id=1, source_target_pairs={{0,8},{1,9},{2,10},{3,11},{4,12},{5,13},{6,14},{7,15},{8,16},{9,17... | collective-permute-start | bytes 442376 | tf_op jit(solution)/shard_map/ppermute | solution.py:759
  220.2 16.7 %collective-permute-start.34 = (bf16[24,3072]{1,0:T(8,128)(2,1)S(1)}, bf16[24,3072]{1,0:T(8,128)(2,1)S(1)}, u32[]{:S(2)}, u32[]{:S(2)}) collective-permute-start(bf16[24,3072]{1,0:T(8,128)(2,1)S(1)} %get-tuple-element.141), channel_id=1, source_target_pairs={{0,16},{1,17},{2,18},{3,19},{4,20},{5,21},{6,22},{7,23},{8,24},{9,... | collective-permute-start | bytes 442376 | tf_op jit(solution)/shard_map/ppermute | solution.py:759
  223.6 16.6 %collective-permute-start.35 = (bf16[24,3072]{1,0:T(8,128)(2,1)S(1)}, bf16[24,3072]{1,0:T(8,128)(2,1)S(1)}, u32[]{:S(2)}, u32[]{:S(2)}) collective-permute-start(bf16[24,3072]{1,0:T(8,128)(2,1)S(1)} %get-tuple-element.140), channel_id=1, source_target_pairs={{0,24},{1,25},{2,26},{3,27},{4,28},{5,29},{6,30},{7,31},{8,0},{9,1... | collective-permute-start | bytes 442376 | tf_op jit(solution)/shard_map/ppermute | solution.py:759
  227.6 13.4 %collective-permute-start.36 = (bf16[24,1920]{1,0:T(8,128)(2,1)S(1)}, bf16[24,1920]{1,0:T(8,128)(2,1)S(1)}, u32[]{:S(2)}, u32[]{:S(2)}) collective-permute-start(bf16[24,1920]{1,0:T(8,128)(2,1)S(1)} %get-tuple-element.144), channel_id=1, source_target_pairs={{0,8},{1,9},{2,10},{3,11},{4,12},{5,13},{6,14},{7,15},{8,16},{9,17... | collective-permute-start | bytes 276488 | tf_op jit(solution)/shard_map/ppermute | solution.py:759
  228.0 13.0 %collective-permute-start.37 = (bf16[24,1920]{1,0:T(8,128)(2,1)S(1)}, bf16[24,1920]{1,0:T(8,128)(2,1)S(1)}, u32[]{:S(2)}, u32[]{:S(2)}) collective-permute-start(bf16[24,1920]{1,0:T(8,128)(2,1)S(1)} %get-tuple-element.143), channel_id=1, source_target_pairs={{0,16},{1,17},{2,18},{3,19},{4,20},{5,21},{6,22},{7,23},{8,24},{9,... | collective-permute-start | bytes 276488 | tf_op jit(solution)/shard_map/ppermute | solution.py:759
  231.4 12.0 %collective-permute-start.38 = (bf16[24,1920]{1,0:T(8,128)(2,1)S(1)}, bf16[24,1920]{1,0:T(8,128)(2,1)S(1)}, u32[]{:S(2)}, u32[]{:S(2)}) collective-permute-start(bf16[24,1920]{1,0:T(8,128)(2,1)S(1)} %get-tuple-element.142), channel_id=1, source_target_pairs={{0,24},{1,25},{2,26},{3,27},{4,28},{5,29},{6,30},{7,31},{8,0},{9,1... | collective-permute-start | bytes 276488 | tf_op jit(solution)/shard_map/ppermute | solution.py:759
  236.9 15.4 %collective-permute-start.32 = (bf16[512,768]{1,0:T(8,128)(2,1)S(1)}, bf16[512,768]{1,0:T(8,128)(2,1)S(1)}, u32[]{:S(2)}, u32[]{:S(2)}) collective-permute-start(bf16[512,768]{1,0:T(8,128)(2,1)S(1)} %dynamic-slice_bitcast_fusion.3), channel_id=1, source_target_pairs={{0,1},{1,0},{2,3},{3,2},{4,5},{5,4},{6,7},{7,6},{8,9},{9,8},{10,11... | collective-permute-start | bytes 2359304 | tf_op jit(solution)/shard_map/ppermute | solution.py:759
  (50 other events, 554.4 us)

commit v5 on v4

--- a/solution.py
+++ b/solution.py
@@ -325,6 +325,11 @@
     return (shifted_raw, dt, cum, cum - jnp.log(dt))
 
 
+def spread_pair(table, pair, first):
+    rows = table.shape[0]
+    return jnp.where(first, spread_lanes(table, 2 * pair, rows), spread_lanes(table, 2 * pair + 1, rows))
+
+
 def spread_lanes(table, head, rows):
     return jnp.broadcast_to(table[:, head : head + 1], (rows, PAIR))
 
@@ -362,6 +367,7 @@
     cb_ref[...] = ndot(cm, bm)
     _, _, cum, late = step_sizes(xt_ref[:, CONVW:], heads_ref)
     late_t = late.T
+    scale = jnp.exp(cum[GROUP - 1 : GROUP, :] - late)
     lower = lower_ones(half, False)
     first = lax.broadcasted_iota(jnp.int32, (1, PAIR), 1) < HEADDIM
     for pair in range(HEADS // 2):
@@ -384,22 +390,19 @@
             )
             inside.append(jnp.concatenate([above, below], 0))
             spread.append(here)
-        both = jnp.where(first, spread[0], spread[1])
-        end = both[GROUP - 1 : GROUP, :]
+        both = jnp.exp(jnp.where(first, spread[0], spread[1]))
+        decay = both[GROUP - 1 : GROUP, :]
         state = run_ref[:, at]
-        carried = jnp.exp(both) * jnp.dot(
+        carried = both * jnp.dot(
             cm, state.astype(jnp.bfloat16), preferred_element_type=jnp.float32
         )
         xf = xp.astype(jnp.float32)
         ssd_ref[:, at] = (
             jnp.where(first, inside[0], inside[1]) + carried + lanes_ref[1:2, at] * xf
         )
-        both_late = jnp.where(
-            first, spread_lanes(late, 2 * pair, GROUP), spread_lanes(late, 2 * pair + 1, GROUP)
-        )
-        xw = (xf * jnp.exp(end - both_late)).astype(jnp.bfloat16)
+        xw = (xf * spread_pair(scale, pair, first)).astype(jnp.bfloat16)
         state_ref[:, at] = state
-        run_ref[:, at] = jnp.exp(end) * state + jnp.dot(
+        run_ref[:, at] = decay * state + jnp.dot(
             bm_t, xw, preferred_element_type=jnp.float32
         )
 
@@ -485,6 +488,8 @@
     dcb_ref[...] = jnp.zeros_like(dcb_ref)
     raw, dt, cum, late = step_sizes(xt_ref[:, CONVW:], heads_ref)
     cum_t = cum.T
+    exp_cum = jnp.exp(cum)
+    late_scale = jnp.exp(cum[GROUP - 1 : GROUP, :] - late)
     upper = lower_ones(half, True)
     first = lax.broadcasted_iota(jnp.int32, (1, PAIR), 1) < HEADDIM
     masks = (first.astype(jnp.float32), 1.0 - first.astype(jnp.float32))
@@ -494,7 +499,6 @@
         dp = dssd_ref[:, at]
         xf = xp.astype(jnp.float32)
         df = dp.astype(jnp.float32)
-        spread = []
         inside = []
         for place, head in enumerate((2 * pair, 2 * pair + 1)):
             here = spread_lanes(late, head, GROUP)
@@ -516,14 +520,11 @@
             )
             below = jnp.dot(last, dp[half:], preferred_element_type=jnp.float32)
             inside.append(jnp.concatenate([above, below], 0))
-            spread.append(here)
-        both = jnp.where(
-            first, spread_lanes(cum, 2 * pair, GROUP), spread_lanes(cum, 2 * pair + 1, GROUP)
-        )
-        end = both[GROUP - 1 : GROUP, :]
-        scale = jnp.exp(end - jnp.where(first, spread[0], spread[1]))
+        both = spread_pair(exp_cum, pair, first)
+        decay = both[GROUP - 1 : GROUP, :]
+        scale = spread_pair(late_scale, pair, first)
         xw_ref[:, at] = (xf * scale).astype(jnp.bfloat16)
-        dcarry = (df * jnp.exp(both)).astype(jnp.bfloat16)
+        dcarry = (df * both).astype(jnp.bfloat16)
         dcarry_ref[:, at] = dcarry
         grad = run_ref[:, at]
         grad_low = grad.astype(jnp.bfloat16)
@@ -537,7 +538,6 @@
         rest_ref[:, at] = (product - top.astype(jnp.float32)).astype(jnp.bfloat16)
         dmixed = (inner + lanes_ref[1:2, at] * df).astype(jnp.bfloat16).astype(jnp.float32)
         dext_ref[pair, 0:GROUP, :] = dmixed * slope_ref[:, at]
-        decay = jnp.exp(end)
         lane_ref[0:1, at] = jnp.sum(xf * dxs, 0, keepdims=True) + decay * jnp.sum(
             grad * state_ref[:, at], 0, keepdims=True
         )
@@ -961,25 +961,35 @@
     micro, _, length, _ = x_in.shape
     rows = in_weight.shape[0]
     sizes = (conv_weight.shape[1], conv_bias.size, gate_gain.size, norm_gain.size)
-    x_sent = swap_pick(x_in[:, 0])
-    small = pack_small(norm_gain, conv_weight, conv_bias, gate_gain, jnp.zeros((8,), norm_gain.dtype))
-    small = jnp.pad(small[:, : XTAIL - SPARE], ((0, rows - KCONV - 4), (0, 0)))
-    first = jnp.concatenate([in_weight[:, INNER:], small], 1)
+    place = lambda a, row, column: jnp.pad(
+        a, ((row, rows - row - a.shape[0]), (column, XTAIL - column - a.shape[1]))
+    )
+    first = (
+        place(in_weight[:, INNER:], 0, 0)
+        + place(conv_weight, 0, SPARE)
+        + place(conv_bias[None], KCONV, SPARE)
+        + place(gate_gain[None], KCONV + 1, SPARE)
+        + place(norm_gain[None], KCONV + 2, SPARE)
+    )
     second = jnp.concatenate([in_weight[:, :INNER], out_weight[:rows], out_weight[rows:]], 1)
 
     line_first = gather_line(first)
-    x_got = grid_send(x_sent, (0, 0, 0, 1))
+    x_got = swap_send(x_in[:, 0])
     xb = swap_join(x_in[:, 0], x_got)
     plane_first = gather_plane(line_first)
     line_second = gather_line(after(second, plane_first[2]))
     heads, skip_lanes = head_tables(dt_bias, rate, skip)
     seg = head_segments()
     w_xt, taps_bias, lanes, gain_in = gather_first(plane_first, skip_lanes)
-    plane_second = gather_plane(after(line_second, *plane_first))
+    line_second = after(line_second, *plane_first)
+    second_y = grid_send(line_second, (0, 1, 0, 0))
+    second_x = grid_send(line_second, (0, 0, 0, 1))
+    plane_second = [line_second, second_x, second_y, grid_send(second_x, (0, 1, 0, 0))]
     xf, r_in, normed = input_norm(xb, gain_in)
-    xt = low_dot(normed, w_xt)
+    normed = after(normed)
+    xt = after(low_dot(normed, w_xt), second_x)
     mixed, slope, states, ssd = run_scan(xt, taps_bias, heads, lanes)
-    cot = swap_halves(after(grad_out[:, 0], *plane_first), ssd)
+    cot = swap_halves(after(grad_out[:, 0], second_x), ssd)
 
     plane_second = [after(piece, ssd) for piece in plane_second]
     w_z, w_out = gather_core(
@@ -998,7 +1008,6 @@
         xt, mixed, slope, dssd, states, delta, taps_bias, heads, lanes, seg
     )
     dxt, y_got = lax.optimization_barrier((dxt, y_got) + tuple(early))[:2]
-    y_out = swap_join(y.reshape(micro, length, WIDE), y_got).reshape(x_in.shape)
     grad_wxt = tdot(normed, dxt).astype(jnp.bfloat16)
     late = reduce_core([grad_wxt.reshape(devices, rows, -1)])
     head_terms = jnp.concatenate(
@@ -1014,12 +1023,16 @@
     tiny = reduce_core([tiny], jnp.float32)
     tiny = jnp.pad(tiny, ((0, 0),) * 3 + ((0, rows - KCONV - 4), (SPARE, 0)))
     late = (late.astype(jnp.float32) + tiny).astype(jnp.bfloat16)
-    dnormed = ndot(after(dz, late), w_z) + ndot(after(dxt, late), w_xt)
+    dn_z = ndot(after(dz, late), w_z)
     late = plane_parts(late)
+    early = lax.optimization_barrier(tuple(early) + (late[2],))[:-1]
+    dnormed = dn_z + ndot(after(dxt, late[2]), w_xt)
     dx = input_grad(xf, r_in, gain_in, dnormed, cot)
     dx_got = swap_send(after(dx.reshape(micro, length, WIDE), *late))
-    early = add_up(line_parts(after(add_up(early).astype(jnp.bfloat16), late[2])))
+    early = add_up(line_parts(add_up(early).astype(jnp.bfloat16)))
     late = tuple(line_parts(add_up(late).astype(jnp.bfloat16)))
+    y_got = after(y_got, late[1])
+    y_out = swap_join(y.reshape(micro, length, WIDE), y_got).reshape(x_in.shape)
     late = add_up(lax.optimization_barrier(late + (dx_got,))[:-1])
     dx_in = swap_join(dx.reshape(micro, length, WIDE), dx_got).reshape(x_in.shape)
     own_in = jnp.concatenate([early[:, :INNER], late[:, :SPARE]], 1)

time: 260 us -> 240 us (0.923)
  waiting for transfers between devices: 58.3 us -> 47.6 us
  local copies, waits for them, and re-layouts: 22 us -> 17.1 us
    ppermute x39, waiting for transfers between devices: 58.3 us -> 47.6 us  [grid_send(): return lax.ppermute(array, ('dp', 'seq'), grid_moves(step))]
    pad x6 -> x1, local copies, waits for them, and re-layouts: 3.19 us -> 0.01 us  [pack_small(): jnp.pad(line, ((0, 0), (0, PAIR - line.shape[1])))]
  transfers between devices with their start and end apart: 39 -> 39, of which waited for: 13 -> 13; matrix products, arithmetic and copies ran while one was open for 16% -> 16% of each run, Pallas kernels for 21% -> 22%
where the time goes in v5:
time: 240 us; the launch traced here: 238 us
  Pallas kernels  76.2 us (32%)
  waiting for transfers between devices  47.6 us (20%)
  starting transfers between devices  38.8 us (16%)
  matrix products  29.6 us (12%)
  other arithmetic  27.6 us (12%)
  local copies, waits for them, and re-layouts  17.1 us (7%)
    ppermute x39, waiting for transfers between devices, grid_send(): return lax.ppermute(array, ('dp', 'seq'), grid_moves(step))  47.6 us
    ppermute x39, starting transfers between devices, grid_send(): return lax.ppermute(array, ('dp', 'seq'), grid_moves(step))  38.8 us
    pallas_call x1, Pallas kernels, run_backward(): pl.pallas_call(backward_kernel, grid=(count,), in_specs=[tall_block(XTAIL...  31.2 us
    pallas_call x1, Pallas kernels, run_gate(): pl.pallas_call(gate_kernel, grid=(length // GROUP,), in_specs=[tall_block...  22 us
    pallas_call x1, Pallas kernels, run_scan(): pl.pallas_call(scan_kernel, grid=(count,), in_specs=[tall_block(XTAIL), f...  18.9 us
    dot_general x3, matrix products, tdot(): lax.dot_general(left, right, (((0,), (0,)), ((), ())), preferred_element_...  14.1 us
    dot_general x2, matrix products, low_dot(): jnp.dot(left, right, preferred_element_type=jnp.float32)  9.1 us
    dot_general x2, matrix products, ndot(): lax.dot_general(left, right, (((1,), (1,)), ((), ())), preferred_element_...  6.42 us
  transfers between devices with their start and end apart: 39, of which 13 were waited for; matrix products, arithmetic and copies ran while one was open for 16% of the time, Pallas kernels for 22%

profile of v5, /device:TPU:8, one launch (start us, length us, event | category | flops | bytes accessed | tf_op | source)
XLA Modules:
  0.0 238.5 jit_solution(221194424554327479)
XLA Ops:
  5.1 2.0 collective-permute-start.3
  7.1 2.1 dynamic-slice_bitcast_fusion.6
  18.1 6.3 %collective-permute-done.7.refs_4_ = bf16[4,24,1920]{2,1,0:T(8,128)(2,1)S(1)} collective-permute-done((bf16[4,24,1920]{2,1,0:T(8,128)(2,1)S(1)}, bf16[4,24,1920]{2,1,0:T(8,128)(2,1)S(1)}, u32[]{:S(2)}, u32[]{:S(2)}) %collective-permute-start.7) | collective-permute-done | bytes 368672 | tf_op jit(solution)/shard_map/ppermute | solution.py:759
  26.2 12.6 %collective-permute-done.9.refs_6_ = bf16[4,24,1920]{2,1,0:T(8,128)(2,1)} collective-permute-done((bf16[4,24,1920]{2,1,0:T(8,128)(2,1)S(1)}, bf16[4,24,1920]{2,1,0:T(8,128)(2,1)}, u32[]{:S(2)}, u32[]{:S(2)}) %collective-permute-start.9) | collective-permute-done | bytes 368672 | tf_op jit(solution)/shard_map/ppermute | solution.py:759
  40.3 3.3 %collective-permute-done.5.refs_2_ = bf16[4,24,1920]{2,1,0:T(8,128)(2,1)} collective-permute-done((bf16[4,24,1920]{2,1,0:T(8,128)(2,1)S(1)}, bf16[4,24,1920]{2,1,0:T(8,128)(2,1)}, u32[]{:S(2)}, u32[]{:S(2)}) %collective-permute-start.5) | collective-permute-done | bytes 368672 | tf_op jit(solution)/shard_map/ppermute | solution.py:759
  50.5 1.9 join_first.1
  52.9 5.1 %convolution_convert_fusion.1.xt_ref = bf16[1024,1920]{1,0:T(8,128)(2,1)} fusion(bf16[1024,768]{1,0:T(8,128)(2,1)S(1)} %fusion.2, bf16[768,1920]{1,0:T(8,128)(2,1)S(1)} %bitcast.158), kind=kOutput, calls=%fused_computation.6 | convolution fusion | flops 3021864960 | bytes 8454144 | tf_op jit(solution)/shard_map/dot_general | solution.py:735
  58.1 2.1 collective-permute-done.14.refs_2_
  64.1 18.9 %scan_forward.1 = (bf16[1024,1792]{1,0:T(8,128)(2,1)}, f32[1024,1792]{1,0:T(8,128)}, f32[512,1536]{1,0:T(8,128)S(1)}, f32[1024,1536]{1,0:T(8,128)}) custom-call(bf16[1024,1920]{1,0:T(8,128)(2,1)} %convolution_convert_fusion.1.xt_ref, f32[8,1792]{1,0:T(8,128)S(1)} %get-tuple-element.60.taps_ref, f32[8,128]{1,0:T(8,128)S(1)} %maximum_maximum_fusion.heads_ref, ...), custom_call_target="tpu_custom_call" | custom-call | flops 24999999488 | bytes 30000000 | tf_op jit(solution)/shard_map/scan_forward/pallas_call | solution.py:620
  90.3 2.2 join_rows.1
  92.7 4.0 %convolution_convert_fusion.z_ref = bf16[1024,1536]{1,0:T(8,128)(2,1)} fusion(bf16[1024,768]{1,0:T(8,128)(2,1)S(1)} %copy-done.19, bf16[768,1536]{1,0:T(8,128)(2,1)S(1)} %bitcast.160), kind=kOutput, calls=%fused_computation.5 | convolution fusion | flops 2417491968 | bytes 7077888 | tf_op jit(solution)/shard_map/dot_general | solution.py:735
  96.7 22.0 %gate_both_ways.1 = (bf16[1024,768]{1,0:T(8,128)(2,1)S(1)}, bf16[1024,1536]{1,0:T(8,128)(2,1)}, bf16[1024,1536]{1,0:T(8,128)(2,1)}, bf16[1024,1536]{1,0:T(8,128)...) custom-call(bf16[1024,1536]{1,0:T(8,128)(2,1)} %convolution_convert_fusion.z_ref, ...), custom_call_target="tpu_custom_call" | custom-call | flops 20000000000 | bytes 30000000 | tf_op jit(solution)/shard_map/gate_both_ways/pallas_call | solution.py:647
  118.6 4.9 %convolution_convert_fusion.3 = bf16[768,1536]{1,0:T(8,128)(2,1)S(1)} fusion(bf16[1024,768]{1,0:T(8,128)(2,1)S(1)} %copy-done.19, bf16[1024,1536]{1,0:T(8,128)(2,1)} %get-tuple-element.88), kind=kOutput, calls=%fused_computation.8 | convolution fusion | flops 2417098752 | bytes 7077888 | tf_op jit(solution)/shard_map/dot_general | solution.py:52
  123.6 3.2 %convolution_convert_fusion.2 = bf16[1536,768]{1,0:T(8,128)(2,1)S(1)} fusion(bf16[1024,1536]{1,0:T(8,128)(2,1)S(1)} %copy-done.33, bf16[512,768]{1,0:T(8,128)(2,1)S(1)} %get-tuple-element.138, bf16[512,768]{1,0:T(8,128)(2,1)S(1)} %get-tuple-element.137), kind=kOutput, calls=%fused_computation.7 | convolution fusion | flops 2420244480 | bytes 7077888 | tf_op jit(solution)/shard_map/dot_general | solution.py:52
  132.6 3.2 %collective-permute-done.22 = bf16[4,2,2,24,3072]{4,3,2,1,0:T(8,128)(2,1)} collective-permute-done((bf16[4,2,2,24,3072]{4,3,2,1,0:T(8,128)(2,1)}, bf16[4,2,2,24,3072]{4,3,2,1,0:T(8,128)(2,1)}, u32[]{:S(2)}, u32[]{:S(2)}) %collective-permute-start.22) | collective-permute-done | bytes 2359328 | tf_op jit(solution)/shard_map/ppermute | solution.py:759
  135.8 2.9 %add_convert_fusion = bf16[4,2,2,24,3072]{4,3,2,1,0:T(8,128)(2,1)S(1)} fusion(bf16[4,2,2,24,3072]{4,3,2,1,0:T(8,128)(2,1)} %collective-permute-done.22, bf16[4,2,2,24,768]{4,3,2,1,0:T(8,128)(2,1)} %get-tuple-element.146, bf16[4,2,2,24,768]{4,3,2,1,0:T(8,128)(2,1)S(1)} %get-tuple-element.144, bf16[4,2,2,24,1536]{4,3,2,1,0:T(8,128)(2,1)} %get-tuple-element.133), kind=kLoop, calls=%fused_computation.4 | loop fusion | flops 10616832 | bytes 7077888 | tf_op jit(solution)/shard_map/convert_element_type | solution.py:788
  141.1 2.4 %collective-permute-start.26 = (bf16[4,24,3072]{2,1,0:T(8,128)(2,1)}, bf16[4,24,3072]{2,1,0:T(8,128)(2,1)}, u32[]{:S(2)}, u32[]{:S(2)}) collective-permute-start(bf16[4,24,3072]{2,1,0:T(8,128)(2,1)} %get-tuple-element.129), channel_id=1, source_target_pairs={{0,5},{1,4},{2,7},{3,6},{4,1},{5,0},{6,3},{7,2},{8,13},{9,12},{10,... | collective-permute-start | bytes 1769480 | tf_op jit(solution)/shard_map/ppermute | solution.py:759
  143.5 31.2 %scan_backward.1 = (bf16[1024,1920]{1,0:T(8,128)(2,1)}, f32[8,1792]{1,0:T(8,128)S(1)}, f32[8,128]{1,0:T(8,128)S(1)}, f32[8,1536]{1,0:T(8,128)S(1)}) custom-call(bf16[1024,1920]{1,0:T(8,128)(2,1)} %convolution_convert_fusion.1.xt_ref, bf16[1024,1792]{1,0:T(8,128)(2,1)} %get-tuple-element.68.xh_ref.mixed_ref, f32[1024,1792]{1,0:T(8,128)} %get-tuple-element.73.slope_ref, ...), custom_call_target="tpu_custom_call" | custom-call | flops 30000001024 | bytes 30000000 | tf_op jit(solution)/shard_map/scan_backward/pallas_call | solution.py:676
  175.2 2.2 collective-permute-done.26
  177.4 6.0 %convolution_convert_fusion.4 = bf16[768,1920]{1,0:T(8,128)(2,1)S(1)} fusion(bf16[1024,768]{1,0:T(8,128)(2,1)} %copy-done.18, bf16[1024,1920]{1,0:T(8,128)(2,1)} %get-tuple-element.89), kind=kOutput, calls=%fused_computation.9 | convolution fusion | flops 3021373440 | bytes 8454144 | tf_op jit(solution)/shard_map/dot_general | solution.py:52
  185.9 2.3 collective-permute-done.28
  188.4 2.3 add_convert_fusion.1
  194.4 2.6 %fusion.41 = f32[1024,768]{1,0:T(8,128)S(1)} fusion(bf16[1024,1536]{1,0:T(8,128)(2,1)S(1)} %copy-done.31, bf16[768,1536]{1,0:T(8,128)(2,1)S(1)} %bitcast.161), kind=kOutput, calls=%fused_computation.158 | convolution fusion | flops 2415919104 | bytes 8650752 | tf_op jit(solution)/shard_map/dot_general | solution.py:58
  197.1 4.5 %collective-permute-done.30 = bf16[4,24,1920]{2,1,0:T(8,128)(2,1)S(1)} collective-permute-done((bf16[4,24,1920]{2,1,0:T(8,128)(2,1)S(1)}, bf16[4,24,1920]{2,1,0:T(8,128)(2,1)S(1)}, u32[]{:S(2)}, u32[]{:S(2)}) %collective-permute-start.30) | collective-permute-done | bytes 368672 | tf_op jit(solution)/shard_map/ppermute | solution.py:759
  203.8 3.4 %collective-permute-start.35 = (bf16[24,3072]{1,0:T(8,128)(2,1)S(1)}, bf16[24,3072]{1,0:T(8,128)(2,1)S(1)}, u32[]{:S(2)}, u32[]{:S(2)}) collective-permute-start(bf16[24,3072]{1,0:T(8,128)(2,1)S(1)} %get-tuple-element.150), channel_id=1, source_target_pairs={{0,16},{1,17},{2,18},{3,19},{4,20},{5,21},{6,22},{7,23},{8,24},{9,... | collective-permute-start | bytes 442376 | tf_op jit(solution)/shard_map/ppermute | solution.py:759
  207.3 3.8 %fusion.7 = (f32[1024]{0:T(1024)S(1)}, f32[1024,768]{1,0:T(8,128)S(1)}) fusion(bf16[512,768]{1,0:T(8,128)(2,1)S(1)} %copy-done.12, bf16[512,768]{1,0:T(8,128)(2,1)S(1)} %copy-done.10, f32[1024,768]{1,0:T(8,128)S(1)} %fusion.41, bf16[1024,1920]{1,0:T(8,128)(2,1)S(1)} %copy-done.32, bf16[768,1920]{1,0:T(8,128)(2,1)S(1)} %bitcast.159, ...), kind=kOutput, calls=%fused_computation.17 | convolution fusion | flops 3026189312 | bytes 14752768 | tf_op jit(solution)/shard_map/dot_general | solution.py:58
  211.1 2.1 fusion.6
  213.5 2.0 collective-permute-start.32
  216.2 2.0 collective-permute-done.32
  218.1 3.1 %collective-permute-start.37 = (bf16[24,1920]{1,0:T(8,128)(2,1)S(1)}, bf16[24,1920]{1,0:T(8,128)(2,1)S(1)}, u32[]{:S(2)}, u32[]{:S(2)}) collective-permute-start(bf16[24,1920]{1,0:T(8,128)(2,1)S(1)} %get-tuple-element.152), channel_id=1, source_target_pairs={{0,16},{1,17},{2,18},{3,19},{4,20},{5,21},{6,22},{7,23},{8,24},{9,... | collective-permute-start | bytes 276488 | tf_op jit(solution)/shard_map/ppermute | solution.py:759
  225.2 3.1 %collective-permute-done.38 = bf16[24,1920]{1,0:T(8,128)(2,1)S(1)} collective-permute-done((bf16[24,1920]{1,0:T(8,128)(2,1)S(1)}, bf16[24,1920]{1,0:T(8,128)(2,1)S(1)}, u32[]{:S(2)}, u32[]{:S(2)}) %collective-permute-start.38) | collective-permute-done | bytes 92192 | tf_op jit(solution)/shard_map/ppermute | solution.py:759
  228.3 4.9 %collective-permute-done.33 = bf16[512,768]{1,0:T(8,128)(2,1)S(1)} collective-permute-done((bf16[512,768]{1,0:T(8,128)(2,1)S(1)}, bf16[512,768]{1,0:T(8,128)(2,1)S(1)}, u32[]{:S(2)}, u32[]{:S(2)}) %collective-permute-start.33) | collective-permute-done | bytes 786464 | tf_op jit(solution)/shard_map/ppermute | solution.py:759
  (229 shorter events, 62.2 us)
Async XLA Ops:
  2.4 10.4 %collective-permute-start.1 = (bf16[24,1920]{1,0:T(8,128)(2,1)S(1)}, bf16[24,1920]{1,0:T(8,128)(2,1)S(1)}, u32[]{:S(2)}, u32[]{:S(2)}) collective-permute-start(bf16[24,1920]{1,0:T(8,128)(2,1)S(1)} %pad_add_fusion), channel_id=1, source_target_pairs={{0,8},{1,9},{2,10},{3,11},{4,12},{5,13},{6,14},{7,15},{8,16},{9,17... | collective-permute-start | bytes 276488 | tf_op jit(solution)/shard_map/ppermute | solution.py:759
  4.0 8.9 %collective-permute-start.2 = (bf16[24,1920]{1,0:T(8,128)(2,1)S(1)}, bf16[24,1920]{1,0:T(8,128)(2,1)S(1)}, u32[]{:S(2)}, u32[]{:S(2)}) collective-permute-start(bf16[24,1920]{1,0:T(8,128)(2,1)S(1)} %pad_add_fusion), channel_id=1, source_target_pairs={{0,16},{1,17},{2,18},{3,19},{4,20},{5,21},{6,22},{7,23},{8,24},{9,... | collective-permute-start | bytes 276488 | tf_op jit(solution)/shard_map/ppermute | solution.py:759
  5.1 8.6 %collective-permute-start.3 = (bf16[24,1920]{1,0:T(8,128)(2,1)S(1)}, bf16[24,1920]{1,0:T(8,128)(2,1)S(1)}, u32[]{:S(2)}, u32[]{:S(2)}) collective-permute-start(bf16[24,1920]{1,0:T(8,128)(2,1)S(1)} %pad_add_fusion), channel_id=1, source_target_pairs={{0,24},{1,25},{2,26},{3,27},{4,28},{5,29},{6,30},{7,31},{8,0},{9,1... | collective-permute-start | bytes 276488 | tf_op jit(solution)/shard_map/ppermute | solution.py:759
  9.1 35.7 %collective-permute-start = (bf16[512,768]{1,0:T(8,128)(2,1)}, bf16[512,768]{1,0:T(8,128)(2,1)}, u32[]{:S(2)}, u32[]{:S(2)}) collective-permute-start(bf16[512,768]{1,0:T(8,128)(2,1)} %dynamic-slice_bitcast_fusion.6), channel_id=1, source_target_pairs={{0,1},{1,0},{2,3},{3,2},{4,5},{5,4},{6,7},{7,6},{8,9},{9,8},{10,11... | collective-permute-start | bytes 2359304 | tf_op jit(solution)/shard_map/ppermute | solution.py:759
  13.7 10.7 %collective-permute-start.7 = (bf16[4,24,1920]{2,1,0:T(8,128)(2,1)S(1)}, bf16[4,24,1920]{2,1,0:T(8,128)(2,1)S(1)}, u32[]{:S(2)}, u32[]{:S(2)}) collective-permute-start(bf16[4,24,1920]{2,1,0:T(8,128)(2,1)S(1)} %pad_maximum_fusion.6.refs_0_), channel_id=1, source_target_pairs={{0,4},{1,5},{2,6},{3,7},{4,0},{5,1},{6,2},{7,3},{8,12},{9,13},{10,... | collective-permute-start | bytes 1105928 | tf_op jit(solution)/shard_map/ppermute | solution.py:759
  15.3 23.5 %collective-permute-start.9 = (bf16[4,24,1920]{2,1,0:T(8,128)(2,1)S(1)}, bf16[4,24,1920]{2,1,0:T(8,128)(2,1)}, u32[]{:S(2)}, u32[]{:S(2)}) collective-permute-start(bf16[4,24,1920]{2,1,0:T(8,128)(2,1)S(1)} %pad_maximum_fusion.6.refs_0_), channel_id=1, source_target_pairs={{0,5},{1,4},{2,7},{3,6},{4,1},{5,0},{6,3},{7,2},{8,13},{9,12},{10,... | collective-permute-start | bytes 1105928 | tf_op jit(solution)/shard_map/ppermute | solution.py:759
  16.9 26.8 %collective-permute-start.5 = (bf16[4,24,1920]{2,1,0:T(8,128)(2,1)S(1)}, bf16[4,24,1920]{2,1,0:T(8,128)(2,1)}, u32[]{:S(2)}, u32[]{:S(2)}) collective-permute-start(bf16[4,24,1920]{2,1,0:T(8,128)(2,1)S(1)} %pad_maximum_fusion.6.refs_0_), channel_id=1, source_target_pairs={{0,1},{1,0},{2,3},{3,2},{4,5},{5,4},{6,7},{7,6},{8,9},{9,8},{10,11... | collective-permute-start | bytes 1105928 | tf_op jit(solution)/shard_map/ppermute | solution.py:759
  24.4 19.3 %collective-permute-start.11 = (bf16[24,3072]{1,0:T(8,128)(2,1)S(1)}, bf16[24,3072]{1,0:T(8,128)(2,1)S(1)}, u32[]{:S(2)}, u32[]{:S(2)}) collective-permute-start(bf16[24,3072]{1,0:T(8,128)(2,1)S(1)} %pad_maximum_fusion.8), channel_id=1, source_target_pairs={{0,8},{1,9},{2,10},{3,11},{4,12},{5,13},{6,14},{7,15},{8,16},{9,17... | collective-permute-start | bytes 442376 | tf_op jit(solution)/shard_map/ppermute | solution.py:759
  24.4 19.8 %collective-permute-start.12 = (bf16[24,3072]{1,0:T(8,128)(2,1)S(1)}, bf16[24,3072]{1,0:T(8,128)(2,1)S(1)}, u32[]{:S(2)}, u32[]{:S(2)}) collective-permute-start(bf16[24,3072]{1,0:T(8,128)(2,1)S(1)} %pad_maximum_fusion.8), channel_id=1, source_target_pairs={{0,16},{1,17},{2,18},{3,19},{4,20},{5,21},{6,22},{7,23},{8,24},{9,... | collective-permute-start | bytes 442376 | tf_op jit(solution)/shard_map/ppermute | solution.py:759
  38.8 5.5 %collective-permute-start.13 = (bf16[24,3072]{1,0:T(8,128)(2,1)S(1)}, bf16[24,3072]{1,0:T(8,128)(2,1)S(1)}, u32[]{:S(2)}, u32[]{:S(2)}) collective-permute-start(bf16[24,3072]{1,0:T(8,128)(2,1)S(1)} %pad_maximum_fusion.8), channel_id=1, source_target_pairs={{0,24},{1,25},{2,26},{3,27},{4,28},{5,29},{6,30},{7,31},{8,0},{9,1... | collective-permute-start | bytes 442376 | tf_op jit(solution)/shard_map/ppermute | solution.py:759
  43.7 5.3 %collective-permute-start.4 = (bf16[4,24,1920]{2,1,0:T(8,128)(2,1)S(1)}, bf16[4,24,1920]{2,1,0:T(8,128)(2,1)S(1)}, u32[]{:S(2)}, u32[]{:S(2)}) collective-permute-start(bf16[4,24,1920]{2,1,0:T(8,128)(2,1)S(1)} %pad_maximum_fusion.6.refs_0_), channel_id=1, source_target_pairs={{0,2},{1,3},{2,0},{3,1},{4,6},{5,7},{6,4},{7,5},{8,10},{9,11},{10,... | collective-permute-start | bytes 1105928 | tf_op jit(solution)/shard_map/ppermute | solution.py:759
  43.7 6.8 %collective-permute-start.8 = (bf16[4,24,1920]{2,1,0:T(8,128)(2,1)S(1)}, bf16[4,24,1920]{2,1,0:T(8,128)(2,1)S(1)}, u32[]{:S(2)}, u32[]{:S(2)}) collective-permute-start(bf16[4,24,1920]{2,1,0:T(8,128)(2,1)S(1)} %collective-permute-done.7.refs_4_), channel_id=1, source_target_pairs={{0,2},{1,3},{2,0},{3,1},{4,6},{5,7},{6,4},{7,5},{8,10},{9,11},{10,... | collective-permute-start | bytes 1105928 | tf_op jit(solution)/shard_map/ppermute | solution.py:759
  44.2 6.3 %collective-permute-start.10 = (bf16[4,24,1920]{2,1,0:T(8,128)(2,1)}, bf16[4,24,1920]{2,1,0:T(8,128)(2,1)S(1)}, u32[]{:S(2)}, u32[]{:S(2)}) collective-permute-start(bf16[4,24,1920]{2,1,0:T(8,128)(2,1)} %collective-permute-done.9.refs_6_), channel_id=1, source_target_pairs={{0,2},{1,3},{2,0},{3,1},{4,6},{5,7},{6,4},{7,5},{8,10},{9,11},{10,... | collective-permute-start | bytes 1105928 | tf_op jit(solution)/shard_map/ppermute | solution.py:759
  44.3 6.2 %collective-permute-start.6 = (bf16[4,24,1920]{2,1,0:T(8,128)(2,1)}, bf16[4,24,1920]{2,1,0:T(8,128)(2,1)S(1)}, u32[]{:S(2)}, u32[]{:S(2)}) collective-permute-start(bf16[4,24,1920]{2,1,0:T(8,128)(2,1)} %collective-permute-done.5.refs_2_), channel_id=1, source_target_pairs={{0,2},{1,3},{2,0},{3,1},{4,6},{5,7},{6,4},{7,5},{8,10},{9,11},{10,... | collective-permute-start | bytes 1105928 | tf_op jit(solution)/shard_map/ppermute | solution.py:759
  44.8 15.4 %collective-permute-start.14 = (bf16[4,24,3072]{2,1,0:T(8,128)(2,1)S(1)}, bf16[4,24,3072]{2,1,0:T(8,128)(2,1)S(1)}, u32[]{:S(2)}, u32[]{:S(2)}) collective-permute-start(bf16[4,24,3072]{2,1,0:T(8,128)(2,1)S(1)} %pad_maximum_fusion.5.refs_0_), channel_id=1, source_target_pairs={{0,1},{1,0},{2,3},{3,2},{4,5},{5,4},{6,7},{7,6},{8,9},{9,8},{10,11... | collective-permute-start | bytes 1769480 | tf_op jit(solution)/shard_map/ppermute | solution.py:759
  48.9 35.8 %collective-permute-start.17 = (bf16[4,24,3072]{2,1,0:T(8,128)(2,1)S(1)}, bf16[4,24,3072]{2,1,0:T(8,128)(2,1)}, u32[]{:S(2)}, u32[]{:S(2)}) collective-permute-start(bf16[4,24,3072]{2,1,0:T(8,128)(2,1)S(1)} %pad_maximum_fusion.5.refs_0_), channel_id=1, source_target_pairs={{0,4},{1,5},{2,6},{3,7},{4,0},{5,1},{6,2},{7,3},{8,12},{9,13},{10,... | collective-permute-start | bytes 1769480 | tf_op jit(solution)/shard_map/ppermute | solution.py:759
  61.1 27.5 %collective-permute-start.21 = (bf16[512,768]{1,0:T(8,128)(2,1)}, bf16[512,768]{1,0:T(8,128)(2,1)}, u32[]{:S(2)}, u32[]{:S(2)}) collective-permute-start(bf16[512,768]{1,0:T(8,128)(2,1)} %dynamic-slice_bitcast_fusion.5), channel_id=1, source_target_pairs={{0,1},{1,0},{2,3},{3,2},{4,5},{5,4},{6,7},{7,6},{8,9},{9,8},{10,11... | collective-permute-start | bytes 2359304 | tf_op jit(solution)/shard_map/ppermute | solution.py:759
  62.6 22.7 %collective-permute-start.19 = (bf16[4,24,3072]{2,1,0:T(8,128)(2,1)S(1)}, bf16[4,24,3072]{2,1,0:T(8,128)(2,1)S(1)}, u32[]{:S(2)}, u32[]{:S(2)}) collective-permute-start(bf16[4,24,3072]{2,1,0:T(8,128)(2,1)S(1)} %collective-permute-done.14.refs_2_), channel_id=1, source_target_pairs={{0,4},{1,5},{2,6},{3,7},{4,0},{5,1},{6,2},{7,3},{8,12},{9,13},{10,... | collective-permute-start | bytes 1769480 | tf_op jit(solution)/shard_map/ppermute | solution.py:759
  84.7 5.6 %collective-permute-start.18 = (bf16[4,24,3072]{2,1,0:T(8,128)(2,1)}, bf16[4,24,3072]{2,1,0:T(8,128)(2,1)S(1)}, u32[]{:S(2)}, u32[]{:S(2)}) collective-permute-start(bf16[4,24,3072]{2,1,0:T(8,128)(2,1)} %collective-permute-done.17.refs_4_), channel_id=1, source_target_pairs={{0,2},{1,3},{2,0},{3,1},{4,6},{5,7},{6,4},{7,5},{8,10},{9,11},{10,... | collective-permute-start | bytes 1769480 | tf_op jit(solution)/shard_map/ppermute | solution.py:759
  84.7 5.6 %collective-permute-start.16 = (bf16[4,24,3072]{2,1,0:T(8,128)(2,1)S(1)}, bf16[4,24,3072]{2,1,0:T(8,128)(2,1)S(1)}, u32[]{:S(2)}, u32[]{:S(2)}) collective-permute-start(bf16[4,24,3072]{2,1,0:T(8,128)(2,1)S(1)} %collective-permute-done.14.refs_2_), channel_id=1, source_target_pairs={{0,2},{1,3},{2,0},{3,1},{4,6},{5,7},{6,4},{7,5},{8,10},{9,11},{10,... | collective-permute-start | bytes 1769480 | tf_op jit(solution)/shard_map/ppermute | solution.py:759
  131.9 43.3 %collective-permute-start.23 = (bf16[512,768]{1,0:T(8,128)(2,1)}, bf16[512,768]{1,0:T(8,128)(2,1)}, u32[]{:S(2)}, u32[]{:S(2)}) collective-permute-start(bf16[512,768]{1,0:T(8,128)(2,1)} %dynamic-slice_bitcast_fusion.4), channel_id=1, source_target_pairs={{0,1},{1,0},{2,3},{3,2},{4,5},{5,4},{6,7},{7,6},{8,9},{9,8},{10,11... | collective-permute-start | bytes 2359304 | tf_op jit(solution)/shard_map/ppermute | solution.py:759
  140.0 35.2 %collective-permute-start.24 = (bf16[4,24,3072]{2,1,0:T(8,128)(2,1)}, bf16[4,24,3072]{2,1,0:T(8,128)(2,1)}, u32[]{:S(2)}, u32[]{:S(2)}) collective-permute-start(bf16[4,24,3072]{2,1,0:T(8,128)(2,1)} %get-tuple-element.131), channel_id=1, source_target_pairs={{0,1},{1,0},{2,3},{3,2},{4,5},{5,4},{6,7},{7,6},{8,9},{9,8},{10,11... | collective-permute-start | bytes 1769480 | tf_op jit(solution)/shard_map/ppermute | solution.py:759
  140.6 34.6 %collective-permute-start.25 = (bf16[4,24,3072]{2,1,0:T(8,128)(2,1)}, bf16[4,24,3072]{2,1,0:T(8,128)(2,1)}, u32[]{:S(2)}, u32[]{:S(2)}) collective-permute-start(bf16[4,24,3072]{2,1,0:T(8,128)(2,1)} %get-tuple-element.130), channel_id=1, source_target_pairs={{0,4},{1,5},{2,6},{3,7},{4,0},{5,1},{6,2},{7,3},{8,12},{9,13},{10,... | collective-permute-start | bytes 1769480 | tf_op jit(solution)/shard_map/ppermute | solution.py:759
  141.1 36.3 %collective-permute-start.26 = (bf16[4,24,3072]{2,1,0:T(8,128)(2,1)}, bf16[4,24,3072]{2,1,0:T(8,128)(2,1)}, u32[]{:S(2)}, u32[]{:S(2)}) collective-permute-start(bf16[4,24,3072]{2,1,0:T(8,128)(2,1)} %get-tuple-element.129), channel_id=1, source_target_pairs={{0,5},{1,4},{2,7},{3,6},{4,1},{5,0},{6,3},{7,2},{8,13},{9,12},{10,... | collective-permute-start | bytes 1769480 | tf_op jit(solution)/shard_map/ppermute | solution.py:759
  190.8 10.7 %collective-permute-start.30 = (bf16[4,24,1920]{2,1,0:T(8,128)(2,1)S(1)}, bf16[4,24,1920]{2,1,0:T(8,128)(2,1)S(1)}, u32[]{:S(2)}, u32[]{:S(2)}) collective-permute-start(bf16[4,24,1920]{2,1,0:T(8,128)(2,1)S(1)} %get-tuple-element.143), channel_id=1, source_target_pairs={{0,4},{1,5},{2,6},{3,7},{4,0},{5,1},{6,2},{7,3},{8,12},{9,13},{10,... | collective-permute-start | bytes 1105928 | tf_op jit(solution)/shard_map/ppermute | solution.py:759
  192.4 20.8 %collective-permute-start.29 = (bf16[4,24,1920]{2,1,0:T(8,128)(2,1)S(1)}, bf16[4,24,1920]{2,1,0:T(8,128)(2,1)S(1)}, u32[]{:S(2)}, u32[]{:S(2)}) collective-permute-start(bf16[4,24,1920]{2,1,0:T(8,128)(2,1)S(1)} %get-tuple-element.141), channel_id=1, source_target_pairs={{0,1},{1,0},{2,3},{3,2},{4,5},{5,4},{6,7},{7,6},{8,9},{9,8},{10,11... | collective-permute-start | bytes 1105928 | tf_op jit(solution)/shard_map/ppermute | solution.py:759
  193.0 20.3 %collective-permute-start.31 = (bf16[4,24,1920]{2,1,0:T(8,128)(2,1)S(1)}, bf16[4,24,1920]{2,1,0:T(8,128)(2,1)S(1)}, u32[]{:S(2)}, u32[]{:S(2)}) collective-permute-start(bf16[4,24,1920]{2,1,0:T(8,128)(2,1)S(1)} %get-tuple-element.142), channel_id=1, source_target_pairs={{0,5},{1,4},{2,7},{3,6},{4,1},{5,0},{6,3},{7,2},{8,13},{9,12},{10,... | collective-permute-start | bytes 1105928 | tf_op jit(solution)/shard_map/ppermute | solution.py:759
  203.4 20.4 %collective-permute-start.34 = (bf16[24,3072]{1,0:T(8,128)(2,1)S(1)}, bf16[24,3072]{1,0:T(8,128)(2,1)S(1)}, u32[]{:S(2)}, u32[]{:S(2)}) collective-permute-start(bf16[24,3072]{1,0:T(8,128)(2,1)S(1)} %get-tuple-element.148), channel_id=1, source_target_pairs={{0,8},{1,9},{2,10},{3,11},{4,12},{5,13},{6,14},{7,15},{8,16},{9,17... | collective-permute-start | bytes 442376 | tf_op jit(solution)/shard_map/ppermute | solution.py:759
  203.8 20.6 %collective-permute-start.35 = (bf16[24,3072]{1,0:T(8,128)(2,1)S(1)}, bf16[24,3072]{1,0:T(8,128)(2,1)S(1)}, u32[]{:S(2)}, u32[]{:S(2)}) collective-permute-start(bf16[24,3072]{1,0:T(8,128)(2,1)S(1)} %get-tuple-element.150), channel_id=1, source_target_pairs={{0,16},{1,17},{2,18},{3,19},{4,20},{5,21},{6,22},{7,23},{8,24},{9,... | collective-permute-start | bytes 442376 | tf_op jit(solution)/shard_map/ppermute | solution.py:759
  207.1 17.3 %collective-permute-start.36 = (bf16[24,3072]{1,0:T(8,128)(2,1)S(1)}, bf16[24,3072]{1,0:T(8,128)(2,1)S(1)}, u32[]{:S(2)}, u32[]{:S(2)}) collective-permute-start(bf16[24,3072]{1,0:T(8,128)(2,1)S(1)} %get-tuple-element.149), channel_id=1, source_target_pairs={{0,24},{1,25},{2,26},{3,27},{4,28},{5,29},{6,30},{7,31},{8,0},{9,1... | collective-permute-start | bytes 442376 | tf_op jit(solution)/shard_map/ppermute | solution.py:759
  215.6 17.7 %collective-permute-start.33 = (bf16[512,768]{1,0:T(8,128)(2,1)S(1)}, bf16[512,768]{1,0:T(8,128)(2,1)S(1)}, u32[]{:S(2)}, u32[]{:S(2)}) collective-permute-start(bf16[512,768]{1,0:T(8,128)(2,1)S(1)} %dynamic-slice_bitcast_fusion.3), channel_id=1, source_target_pairs={{0,1},{1,0},{2,3},{3,2},{4,5},{5,4},{6,7},{7,6},{8,9},{9,8},{10,11... | collective-permute-start | bytes 2359304 | tf_op jit(solution)/shard_map/ppermute | solution.py:759
  218.1 7.1 %collective-permute-start.37 = (bf16[24,1920]{1,0:T(8,128)(2,1)S(1)}, bf16[24,1920]{1,0:T(8,128)(2,1)S(1)}, u32[]{:S(2)}, u32[]{:S(2)}) collective-permute-start(bf16[24,1920]{1,0:T(8,128)(2,1)S(1)} %get-tuple-element.152), channel_id=1, source_target_pairs={{0,16},{1,17},{2,18},{3,19},{4,20},{5,21},{6,22},{7,23},{8,24},{9,... | collective-permute-start | bytes 276488 | tf_op jit(solution)/shard_map/ppermute | solution.py:759
  (42 other events, 384.7 us)

commit v6 on v5

--- a/solution.py
+++ b/solution.py
@@ -453,7 +453,7 @@
             rest_ref[rows, at] = (product - top.astype(jnp.float32)).astype(jnp.bfloat16)
         return carry
 
-    lax.fori_loop(0, GROUP // 16, gate_rows, 0, unroll=4)
+    lax.fori_loop(0, GROUP // 16, gate_rows, 0, unroll=8)
     seg = seg_ref[...]
     delta_ref[...] = jnp.dot(
         high_ref[...], seg, preferred_element_type=jnp.float32
@@ -980,6 +980,7 @@
     line_second = gather_line(after(second, plane_first[2]))
     heads, skip_lanes = head_tables(dt_bias, rate, skip)
     seg = head_segments()
+    seg, skip_lanes = lax.optimization_barrier((seg, skip_lanes))
     w_xt, taps_bias, lanes, gain_in = gather_first(plane_first, skip_lanes)
     line_second = after(line_second, *plane_first)
     second_y = grid_send(line_second, (0, 1, 0, 0))

time: 240 us -> 239 us (level)
  no operation moved by 1% of the time
where the time goes in v6:
time: 239 us; the launch traced here: 237 us
  Pallas kernels  75.7 us (32%)
  waiting for transfers between devices  46.5 us (19%)
  starting transfers between devices  40 us (17%)
  matrix products  29.7 us (12%)
  other arithmetic  26.4 us (11%)
  local copies, waits for them, and re-layouts  17 us (7%)
    ppermute x39, waiting for transfers between devices, grid_send(): return lax.ppermute(array, ('dp', 'seq'), grid_moves(step))  46.5 us
    ppermute x39, starting transfers between devices, grid_send(): return lax.ppermute(array, ('dp', 'seq'), grid_moves(step))  40 us
    pallas_call x1, Pallas kernels, run_backward(): pl.pallas_call(backward_kernel, grid=(count,), in_specs=[tall_block(XTAIL...  31.2 us
    pallas_call x1, Pallas kernels, run_gate(): pl.pallas_call(gate_kernel, grid=(length // GROUP,), in_specs=[tall_block...  21.2 us
    pallas_call x1, Pallas kernels, run_scan(): pl.pallas_call(scan_kernel, grid=(count,), in_specs=[tall_block(XTAIL), f...  19 us
    dot_general x3, matrix products, tdot(): lax.dot_general(left, right, (((0,), (0,)), ((), ())), preferred_element_...  14.1 us
    dot_general x2, matrix products, low_dot(): jnp.dot(left, right, preferred_element_type=jnp.float32)  9.22 us
    dot_general x2, matrix products, ndot(): lax.dot_general(left, right, (((1,), (1,)), ((), ())), preferred_element_...  6.38 us
  transfers between devices with their start and end apart: 39, of which 13 were waited for; matrix products, arithmetic and copies ran while one was open for 16% of the time, Pallas kernels for 22%

profile of v6, /device:TPU:8, one launch (start us, length us, event | category | flops | bytes accessed | tf_op | source)
XLA Modules:
  0.0 236.9 jit_solution(1099889603252361731)
XLA Ops:
  7.1 2.1 dynamic-slice_bitcast_fusion.6
  18.1 6.4 %collective-permute-done.7.refs_4_ = bf16[4,24,1920]{2,1,0:T(8,128)(2,1)} collective-permute-done((bf16[4,24,1920]{2,1,0:T(8,128)(2,1)S(1)}, bf16[4,24,1920]{2,1,0:T(8,128)(2,1)}, u32[]{:S(2)}, u32[]{:S(2)}) %collective-permute-start.7) | collective-permute-done | bytes 368672 | tf_op jit(solution)/shard_map/ppermute | solution.py:759
  24.5 2.8 %collective-permute-start.12 = (bf16[24,3072]{1,0:T(8,128)(2,1)S(1)}, bf16[24,3072]{1,0:T(8,128)(2,1)S(1)}, u32[]{:S(2)}, u32[]{:S(2)}) collective-permute-start(bf16[24,3072]{1,0:T(8,128)(2,1)S(1)} %pad_maximum_fusion.8), channel_id=1, source_target_pairs={{0,16},{1,17},{2,18},{3,19},{4,20},{5,21},{6,22},{7,23},{8,24},{9,... | collective-permute-start | bytes 442376 | tf_op jit(solution)/shard_map/ppermute | solution.py:759
  27.3 11.5 %collective-permute-done.9.refs_6_ = bf16[4,24,1920]{2,1,0:T(8,128)(2,1)} collective-permute-done((bf16[4,24,1920]{2,1,0:T(8,128)(2,1)S(1)}, bf16[4,24,1920]{2,1,0:T(8,128)(2,1)}, u32[]{:S(2)}, u32[]{:S(2)}) %collective-permute-start.9) | collective-permute-done | bytes 368672 | tf_op jit(solution)/shard_map/ppermute | solution.py:759
  40.4 3.3 %collective-permute-done.5.refs_2_ = bf16[4,24,1920]{2,1,0:T(8,128)(2,1)} collective-permute-done((bf16[4,24,1920]{2,1,0:T(8,128)(2,1)S(1)}, bf16[4,24,1920]{2,1,0:T(8,128)(2,1)}, u32[]{:S(2)}, u32[]{:S(2)}) %collective-permute-start.5) | collective-permute-done | bytes 368672 | tf_op jit(solution)/shard_map/ppermute | solution.py:759
  49.9 2.0 join_first.1
  52.4 5.1 %convolution_convert_fusion.1.xt_ref = bf16[1024,1920]{1,0:T(8,128)(2,1)} fusion(bf16[1024,768]{1,0:T(8,128)(2,1)S(1)} %fusion.2, bf16[768,1920]{1,0:T(8,128)(2,1)S(1)} %bitcast.158), kind=kOutput, calls=%fused_computation.6 | convolution fusion | flops 3021864960 | bytes 8454144 | tf_op jit(solution)/shard_map/dot_general | solution.py:735
  57.5 2.6 %collective-permute-done.14.refs_2_ = bf16[4,24,3072]{2,1,0:T(8,128)(2,1)S(1)} collective-permute-done((bf16[4,24,3072]{2,1,0:T(8,128)(2,1)S(1)}, bf16[4,24,3072]{2,1,0:T(8,128)(2,1)S(1)}, u32[]{:S(2)}, u32[]{:S(2)}) %collective-permute-start.14) | collective-permute-done | bytes 589856 | tf_op jit(solution)/shard_map/ppermute | solution.py:759
  64.1 19.0 %scan_forward.1 = (bf16[1024,1792]{1,0:T(8,128)(2,1)}, f32[1024,1792]{1,0:T(8,128)}, f32[512,1536]{1,0:T(8,128)S(1)}, f32[1024,1536]{1,0:T(8,128)}) custom-call(bf16[1024,1920]{1,0:T(8,128)(2,1)} %convolution_convert_fusion.1.xt_ref, f32[8,1792]{1,0:T(8,128)S(1)} %get-tuple-element.63.taps_ref, f32[8,128]{1,0:T(8,128)S(1)} %maximum_maximum_fusion.heads_ref, ...), custom_call_target="tpu_custom_call" | custom-call | flops 24999999488 | bytes 30000000 | tf_op jit(solution)/shard_map/scan_forward/pallas_call | solution.py:620
  89.5 2.3 join_rows.1
  91.9 4.1 %convolution_convert_fusion.z_ref = bf16[1024,1536]{1,0:T(8,128)(2,1)} fusion(bf16[1024,768]{1,0:T(8,128)(2,1)S(1)} %copy-done.21, bf16[768,1536]{1,0:T(8,128)(2,1)S(1)} %bitcast.160), kind=kOutput, calls=%fused_computation.5 | convolution fusion | flops 2417491968 | bytes 7077888 | tf_op jit(solution)/shard_map/dot_general | solution.py:735
  96.0 21.2 %gate_both_ways.1 = (bf16[1024,768]{1,0:T(8,128)(2,1)S(1)}, bf16[1024,1536]{1,0:T(8,128)(2,1)}, bf16[1024,1536]{1,0:T(8,128)(2,1)}, bf16[1024,1536]{1,0:T(8,128)...) custom-call(bf16[1024,1536]{1,0:T(8,128)(2,1)} %convolution_convert_fusion.z_ref, ...), custom_call_target="tpu_custom_call" | custom-call | flops 20000000000 | bytes 30000000 | tf_op jit(solution)/shard_map/gate_both_ways/pallas_call | solution.py:647
  117.2 4.9 %convolution_convert_fusion.3 = bf16[768,1536]{1,0:T(8,128)(2,1)S(1)} fusion(bf16[1024,768]{1,0:T(8,128)(2,1)S(1)} %copy-done.21, bf16[1024,1536]{1,0:T(8,128)(2,1)} %get-tuple-element.92), kind=kOutput, calls=%fused_computation.8 | convolution fusion | flops 2417098752 | bytes 7077888 | tf_op jit(solution)/shard_map/dot_general | solution.py:52
  122.1 3.2 %convolution_convert_fusion.2 = bf16[1536,768]{1,0:T(8,128)(2,1)S(1)} fusion(bf16[1024,1536]{1,0:T(8,128)(2,1)S(1)} %copy-done.31, bf16[512,768]{1,0:T(8,128)(2,1)S(1)} %get-tuple-element.142, bf16[512,768]{1,0:T(8,128)(2,1)S(1)} %get-tuple-element.141), kind=kOutput, calls=%fused_computation.7 | convolution fusion | flops 2420244480 | bytes 7077888 | tf_op jit(solution)/shard_map/dot_general | solution.py:52
  131.1 3.3 %collective-permute-done.22 = bf16[4,2,2,24,3072]{4,3,2,1,0:T(8,128)(2,1)} collective-permute-done((bf16[4,2,2,24,3072]{4,3,2,1,0:T(8,128)(2,1)}, bf16[4,2,2,24,3072]{4,3,2,1,0:T(8,128)(2,1)}, u32[]{:S(2)}, u32[]{:S(2)}) %collective-permute-start.22) | collective-permute-done | bytes 2359328 | tf_op jit(solution)/shard_map/ppermute | solution.py:759
  134.3 2.9 %add_convert_fusion = bf16[4,2,2,24,3072]{4,3,2,1,0:T(8,128)(2,1)S(1)} fusion(bf16[4,2,2,24,3072]{4,3,2,1,0:T(8,128)(2,1)} %collective-permute-done.22, bf16[4,2,2,24,768]{4,3,2,1,0:T(8,128)(2,1)} %get-tuple-element.150, bf16[4,2,2,24,768]{4,3,2,1,0:T(8,128)(2,1)S(1)} %get-tuple-element.148, bf16[4,2,2,24,1536]{4,3,2,1,0:T(8,128)(2,1)} %get-tuple-element.137), kind=kLoop, calls=%fused_computation.4 | loop fusion | flops 10616832 | bytes 7077888 | tf_op jit(solution)/shard_map/convert_element_type | solution.py:788
  139.6 2.5 %collective-permute-start.26 = (bf16[4,24,3072]{2,1,0:T(8,128)(2,1)}, bf16[4,24,3072]{2,1,0:T(8,128)(2,1)}, u32[]{:S(2)}, u32[]{:S(2)}) collective-permute-start(bf16[4,24,3072]{2,1,0:T(8,128)(2,1)} %get-tuple-element.133), channel_id=1, source_target_pairs={{0,5},{1,4},{2,7},{3,6},{4,1},{5,0},{6,3},{7,2},{8,13},{9,12},{10,... | collective-permute-start | bytes 1769480 | tf_op jit(solution)/shard_map/ppermute | solution.py:759
  142.1 31.2 %scan_backward.1 = (bf16[1024,1920]{1,0:T(8,128)(2,1)}, f32[8,1792]{1,0:T(8,128)S(1)}, f32[8,128]{1,0:T(8,128)S(1)}, f32[8,1536]{1,0:T(8,128)S(1)}) custom-call(bf16[1024,1920]{1,0:T(8,128)(2,1)} %convolution_convert_fusion.1.xt_ref, bf16[1024,1792]{1,0:T(8,128)(2,1)} %get-tuple-element.71.xh_ref.mixed_ref, f32[1024,1792]{1,0:T(8,128)} %get-tuple-element.77.slope_ref, ...), custom_call_target="tpu_custom_call" | custom-call | flops 30000001024 | bytes 30000000 | tf_op jit(solution)/shard_map/scan_backward/pallas_call | solution.py:676
  173.7 2.2 collective-permute-done.26
  175.9 6.0 %convolution_convert_fusion.4 = bf16[768,1920]{1,0:T(8,128)(2,1)S(1)} fusion(bf16[1024,768]{1,0:T(8,128)(2,1)} %copy-done.20, bf16[1024,1920]{1,0:T(8,128)(2,1)} %get-tuple-element.93), kind=kOutput, calls=%fused_computation.9 | convolution fusion | flops 3021373440 | bytes 8454144 | tf_op jit(solution)/shard_map/dot_general | solution.py:52
  184.4 2.3 collective-permute-done.28
  186.9 2.3 add_convert_fusion.1
  192.9 2.6 %fusion.41 = f32[1024,768]{1,0:T(8,128)S(1)} fusion(bf16[1024,1536]{1,0:T(8,128)(2,1)S(1)} %copy-done.29, bf16[768,1536]{1,0:T(8,128)(2,1)S(1)} %bitcast.161), kind=kOutput, calls=%fused_computation.158 | convolution fusion | flops 2415919104 | bytes 8650752 | tf_op jit(solution)/shard_map/dot_general | solution.py:58
  195.6 4.5 %collective-permute-done.30 = bf16[4,24,1920]{2,1,0:T(8,128)(2,1)S(1)} collective-permute-done((bf16[4,24,1920]{2,1,0:T(8,128)(2,1)S(1)}, bf16[4,24,1920]{2,1,0:T(8,128)(2,1)S(1)}, u32[]{:S(2)}, u32[]{:S(2)}) %collective-permute-start.30) | collective-permute-done | bytes 368672 | tf_op jit(solution)/shard_map/ppermute | solution.py:759
  202.3 3.4 %collective-permute-start.35 = (bf16[24,3072]{1,0:T(8,128)(2,1)S(1)}, bf16[24,3072]{1,0:T(8,128)(2,1)S(1)}, u32[]{:S(2)}, u32[]{:S(2)}) collective-permute-start(bf16[24,3072]{1,0:T(8,128)(2,1)S(1)} %get-tuple-element.154), channel_id=1, source_target_pairs={{0,16},{1,17},{2,18},{3,19},{4,20},{5,21},{6,22},{7,23},{8,24},{9,... | collective-permute-start | bytes 442376 | tf_op jit(solution)/shard_map/ppermute | solution.py:759
  205.8 3.8 %fusion.7 = (f32[1024]{0:T(1024)S(1)}, f32[1024,768]{1,0:T(8,128)S(1)}) fusion(bf16[512,768]{1,0:T(8,128)(2,1)S(1)} %copy-done.14, bf16[512,768]{1,0:T(8,128)(2,1)S(1)} %copy-done.12, f32[1024,768]{1,0:T(8,128)S(1)} %fusion.41, bf16[1024,1920]{1,0:T(8,128)(2,1)S(1)} %copy-done.30, bf16[768,1920]{1,0:T(8,128)(2,1)S(1)} %bitcast.159, ...), kind=kOutput, calls=%fused_computation.17 | convolution fusion | flops 3026189312 | bytes 14752768 | tf_op jit(solution)/shard_map/dot_general | solution.py:58
  209.6 2.1 fusion.6
  211.9 2.0 collective-permute-start.32
  214.6 2.0 collective-permute-done.32
  216.5 3.3 %collective-permute-start.37 = (bf16[24,1920]{1,0:T(8,128)(2,1)S(1)}, bf16[24,1920]{1,0:T(8,128)(2,1)S(1)}, u32[]{:S(2)}, u32[]{:S(2)}) collective-permute-start(bf16[24,1920]{1,0:T(8,128)(2,1)S(1)} %get-tuple-element.156), channel_id=1, source_target_pairs={{0,16},{1,17},{2,18},{3,19},{4,20},{5,21},{6,22},{7,23},{8,24},{9,... | collective-permute-start | bytes 276488 | tf_op jit(solution)/shard_map/ppermute | solution.py:759
  223.7 3.1 %collective-permute-done.38 = bf16[24,1920]{1,0:T(8,128)(2,1)S(1)} collective-permute-done((bf16[24,1920]{1,0:T(8,128)(2,1)S(1)}, bf16[24,1920]{1,0:T(8,128)(2,1)S(1)}, u32[]{:S(2)}, u32[]{:S(2)}) %collective-permute-start.38) | collective-permute-done | bytes 92192 | tf_op jit(solution)/shard_map/ppermute | solution.py:759
  226.9 4.8 %collective-permute-done.33 = bf16[512,768]{1,0:T(8,128)(2,1)S(1)} collective-permute-done((bf16[512,768]{1,0:T(8,128)(2,1)S(1)}, bf16[512,768]{1,0:T(8,128)(2,1)S(1)}, u32[]{:S(2)}, u32[]{:S(2)}) %collective-permute-start.33) | collective-permute-done | bytes 786464 | tf_op jit(solution)/shard_map/ppermute | solution.py:759
  (225 shorter events, 60.7 us)
Async XLA Ops:
  2.4 11.6 %collective-permute-start.1 = (bf16[24,1920]{1,0:T(8,128)(2,1)S(1)}, bf16[24,1920]{1,0:T(8,128)(2,1)S(1)}, u32[]{:S(2)}, u32[]{:S(2)}) collective-permute-start(bf16[24,1920]{1,0:T(8,128)(2,1)S(1)} %pad_add_fusion), channel_id=1, source_target_pairs={{0,8},{1,9},{2,10},{3,11},{4,12},{5,13},{6,14},{7,15},{8,16},{9,17... | collective-permute-start | bytes 276488 | tf_op jit(solution)/shard_map/ppermute | solution.py:759
  4.0 10.1 %collective-permute-start.2 = (bf16[24,1920]{1,0:T(8,128)(2,1)S(1)}, bf16[24,1920]{1,0:T(8,128)(2,1)S(1)}, u32[]{:S(2)}, u32[]{:S(2)}) collective-permute-start(bf16[24,1920]{1,0:T(8,128)(2,1)S(1)} %pad_add_fusion), channel_id=1, source_target_pairs={{0,16},{1,17},{2,18},{3,19},{4,20},{5,21},{6,22},{7,23},{8,24},{9,... | collective-permute-start | bytes 276488 | tf_op jit(solution)/shard_map/ppermute | solution.py:759
  5.1 9.0 %collective-permute-start.3 = (bf16[24,1920]{1,0:T(8,128)(2,1)S(1)}, bf16[24,1920]{1,0:T(8,128)(2,1)S(1)}, u32[]{:S(2)}, u32[]{:S(2)}) collective-permute-start(bf16[24,1920]{1,0:T(8,128)(2,1)S(1)} %pad_add_fusion), channel_id=1, source_target_pairs={{0,24},{1,25},{2,26},{3,27},{4,28},{5,29},{6,30},{7,31},{8,0},{9,1... | collective-permute-start | bytes 276488 | tf_op jit(solution)/shard_map/ppermute | solution.py:759
  9.1 35.7 %collective-permute-start = (bf16[512,768]{1,0:T(8,128)(2,1)}, bf16[512,768]{1,0:T(8,128)(2,1)}, u32[]{:S(2)}, u32[]{:S(2)}) collective-permute-start(bf16[512,768]{1,0:T(8,128)(2,1)} %dynamic-slice_bitcast_fusion.6), channel_id=1, source_target_pairs={{0,1},{1,0},{2,3},{3,2},{4,5},{5,4},{6,7},{7,6},{8,9},{9,8},{10,11... | collective-permute-start | bytes 2359304 | tf_op jit(solution)/shard_map/ppermute | solution.py:759
  14.2 10.3 %collective-permute-start.7 = (bf16[4,24,1920]{2,1,0:T(8,128)(2,1)S(1)}, bf16[4,24,1920]{2,1,0:T(8,128)(2,1)}, u32[]{:S(2)}, u32[]{:S(2)}) collective-permute-start(bf16[4,24,1920]{2,1,0:T(8,128)(2,1)S(1)} %pad_maximum_fusion.6.refs_0_), channel_id=1, source_target_pairs={{0,4},{1,5},{2,6},{3,7},{4,0},{5,1},{6,2},{7,3},{8,12},{9,13},{10,... | collective-permute-start | bytes 1105928 | tf_op jit(solution)/shard_map/ppermute | solution.py:759
  15.8 23.0 %collective-permute-start.9 = (bf16[4,24,1920]{2,1,0:T(8,128)(2,1)S(1)}, bf16[4,24,1920]{2,1,0:T(8,128)(2,1)}, u32[]{:S(2)}, u32[]{:S(2)}) collective-permute-start(bf16[4,24,1920]{2,1,0:T(8,128)(2,1)S(1)} %pad_maximum_fusion.6.refs_0_), channel_id=1, source_target_pairs={{0,5},{1,4},{2,7},{3,6},{4,1},{5,0},{6,3},{7,2},{8,13},{9,12},{10,... | collective-permute-start | bytes 1105928 | tf_op jit(solution)/shard_map/ppermute | solution.py:759
  16.9 26.8 %collective-permute-start.5 = (bf16[4,24,1920]{2,1,0:T(8,128)(2,1)S(1)}, bf16[4,24,1920]{2,1,0:T(8,128)(2,1)}, u32[]{:S(2)}, u32[]{:S(2)}) collective-permute-start(bf16[4,24,1920]{2,1,0:T(8,128)(2,1)S(1)} %pad_maximum_fusion.6.refs_0_), channel_id=1, source_target_pairs={{0,1},{1,0},{2,3},{3,2},{4,5},{5,4},{6,7},{7,6},{8,9},{9,8},{10,11... | collective-permute-start | bytes 1105928 | tf_op jit(solution)/shard_map/ppermute | solution.py:759
  24.5 19.2 %collective-permute-start.11 = (bf16[24,3072]{1,0:T(8,128)(2,1)S(1)}, bf16[24,3072]{1,0:T(8,128)(2,1)S(1)}, u32[]{:S(2)}, u32[]{:S(2)}) collective-permute-start(bf16[24,3072]{1,0:T(8,128)(2,1)S(1)} %pad_maximum_fusion.8), channel_id=1, source_target_pairs={{0,8},{1,9},{2,10},{3,11},{4,12},{5,13},{6,14},{7,15},{8,16},{9,17... | collective-permute-start | bytes 442376 | tf_op jit(solution)/shard_map/ppermute | solution.py:759
  24.5 19.7 %collective-permute-start.12 = (bf16[24,3072]{1,0:T(8,128)(2,1)S(1)}, bf16[24,3072]{1,0:T(8,128)(2,1)S(1)}, u32[]{:S(2)}, u32[]{:S(2)}) collective-permute-start(bf16[24,3072]{1,0:T(8,128)(2,1)S(1)} %pad_maximum_fusion.8), channel_id=1, source_target_pairs={{0,16},{1,17},{2,18},{3,19},{4,20},{5,21},{6,22},{7,23},{8,24},{9,... | collective-permute-start | bytes 442376 | tf_op jit(solution)/shard_map/ppermute | solution.py:759
  38.8 5.5 %collective-permute-start.13 = (bf16[24,3072]{1,0:T(8,128)(2,1)S(1)}, bf16[24,3072]{1,0:T(8,128)(2,1)S(1)}, u32[]{:S(2)}, u32[]{:S(2)}) collective-permute-start(bf16[24,3072]{1,0:T(8,128)(2,1)S(1)} %pad_maximum_fusion.8), channel_id=1, source_target_pairs={{0,24},{1,25},{2,26},{3,27},{4,28},{5,29},{6,30},{7,31},{8,0},{9,1... | collective-permute-start | bytes 442376 | tf_op jit(solution)/shard_map/ppermute | solution.py:759
  43.7 4.6 %collective-permute-start.4 = (bf16[4,24,1920]{2,1,0:T(8,128)(2,1)S(1)}, bf16[4,24,1920]{2,1,0:T(8,128)(2,1)S(1)}, u32[]{:S(2)}, u32[]{:S(2)}) collective-permute-start(bf16[4,24,1920]{2,1,0:T(8,128)(2,1)S(1)} %pad_maximum_fusion.6.refs_0_), channel_id=1, source_target_pairs={{0,2},{1,3},{2,0},{3,1},{4,6},{5,7},{6,4},{7,5},{8,10},{9,11},{10,... | collective-permute-start | bytes 1105928 | tf_op jit(solution)/shard_map/ppermute | solution.py:759
  43.7 6.2 %collective-permute-start.8 = (bf16[4,24,1920]{2,1,0:T(8,128)(2,1)}, bf16[4,24,1920]{2,1,0:T(8,128)(2,1)S(1)}, u32[]{:S(2)}, u32[]{:S(2)}) collective-permute-start(bf16[4,24,1920]{2,1,0:T(8,128)(2,1)} %collective-permute-done.7.refs_4_), channel_id=1, source_target_pairs={{0,2},{1,3},{2,0},{3,1},{4,6},{5,7},{6,4},{7,5},{8,10},{9,11},{10,... | collective-permute-start | bytes 1105928 | tf_op jit(solution)/shard_map/ppermute | solution.py:759
  44.2 5.7 %collective-permute-start.10 = (bf16[4,24,1920]{2,1,0:T(8,128)(2,1)}, bf16[4,24,1920]{2,1,0:T(8,128)(2,1)S(1)}, u32[]{:S(2)}, u32[]{:S(2)}) collective-permute-start(bf16[4,24,1920]{2,1,0:T(8,128)(2,1)} %collective-permute-done.9.refs_6_), channel_id=1, source_target_pairs={{0,2},{1,3},{2,0},{3,1},{4,6},{5,7},{6,4},{7,5},{8,10},{9,11},{10,... | collective-permute-start | bytes 1105928 | tf_op jit(solution)/shard_map/ppermute | solution.py:759
  44.3 5.6 %collective-permute-start.6 = (bf16[4,24,1920]{2,1,0:T(8,128)(2,1)}, bf16[4,24,1920]{2,1,0:T(8,128)(2,1)S(1)}, u32[]{:S(2)}, u32[]{:S(2)}) collective-permute-start(bf16[4,24,1920]{2,1,0:T(8,128)(2,1)} %collective-permute-done.5.refs_2_), channel_id=1, source_target_pairs={{0,2},{1,3},{2,0},{3,1},{4,6},{5,7},{6,4},{7,5},{8,10},{9,11},{10,... | collective-permute-start | bytes 1105928 | tf_op jit(solution)/shard_map/ppermute | solution.py:759
  44.8 15.4 %collective-permute-start.14 = (bf16[4,24,3072]{2,1,0:T(8,128)(2,1)S(1)}, bf16[4,24,3072]{2,1,0:T(8,128)(2,1)S(1)}, u32[]{:S(2)}, u32[]{:S(2)}) collective-permute-start(bf16[4,24,3072]{2,1,0:T(8,128)(2,1)S(1)} %pad_maximum_fusion.5.refs_0_), channel_id=1, source_target_pairs={{0,1},{1,0},{2,3},{3,2},{4,5},{5,4},{6,7},{7,6},{8,9},{9,8},{10,11... | collective-permute-start | bytes 1769480 | tf_op jit(solution)/shard_map/ppermute | solution.py:759
  48.3 36.6 %collective-permute-start.17 = (bf16[4,24,3072]{2,1,0:T(8,128)(2,1)S(1)}, bf16[4,24,3072]{2,1,0:T(8,128)(2,1)}, u32[]{:S(2)}, u32[]{:S(2)}) collective-permute-start(bf16[4,24,3072]{2,1,0:T(8,128)(2,1)S(1)} %pad_maximum_fusion.5.refs_0_), channel_id=1, source_target_pairs={{0,4},{1,5},{2,6},{3,7},{4,0},{5,1},{6,2},{7,3},{8,12},{9,13},{10,... | collective-permute-start | bytes 1769480 | tf_op jit(solution)/shard_map/ppermute | solution.py:759
  61.1 26.4 %collective-permute-start.21 = (bf16[512,768]{1,0:T(8,128)(2,1)}, bf16[512,768]{1,0:T(8,128)(2,1)}, u32[]{:S(2)}, u32[]{:S(2)}) collective-permute-start(bf16[512,768]{1,0:T(8,128)(2,1)} %dynamic-slice_bitcast_fusion.5), channel_id=1, source_target_pairs={{0,1},{1,0},{2,3},{3,2},{4,5},{5,4},{6,7},{7,6},{8,9},{9,8},{10,11... | collective-permute-start | bytes 2359304 | tf_op jit(solution)/shard_map/ppermute | solution.py:759
  62.6 22.8 %collective-permute-start.19 = (bf16[4,24,3072]{2,1,0:T(8,128)(2,1)S(1)}, bf16[4,24,3072]{2,1,0:T(8,128)(2,1)S(1)}, u32[]{:S(2)}, u32[]{:S(2)}) collective-permute-start(bf16[4,24,3072]{2,1,0:T(8,128)(2,1)S(1)} %collective-permute-done.14.refs_2_), channel_id=1, source_target_pairs={{0,4},{1,5},{2,6},{3,7},{4,0},{5,1},{6,2},{7,3},{8,12},{9,13},{10,... | collective-permute-start | bytes 1769480 | tf_op jit(solution)/shard_map/ppermute | solution.py:759
  129.5 4.9 %collective-permute-start.22 = (bf16[4,2,2,24,3072]{4,3,2,1,0:T(8,128)(2,1)}, bf16[4,2,2,24,3072]{4,3,2,1,0:T(8,128)(2,1)}, u32[]{:S(2)}, u32[]{:S(2)}) collective-permute-start(bf16[4,2,2,24,3072]{4,3,2,1,0:T(8,128)(2,1)} %pad_maximum_fusion), channel_id=1, source_target_pairs={{0,2},{1,3},{2,0},{3,1},{4,6},{5,7},{6,4},{7,5},{8,10},{9,11},{10,... | collective-permute-start | bytes 7077896 | tf_op jit(solution)/shard_map/ppermute | solution.py:759
  130.5 43.2 %collective-permute-start.23 = (bf16[512,768]{1,0:T(8,128)(2,1)}, bf16[512,768]{1,0:T(8,128)(2,1)}, u32[]{:S(2)}, u32[]{:S(2)}) collective-permute-start(bf16[512,768]{1,0:T(8,128)(2,1)} %dynamic-slice_bitcast_fusion.4), channel_id=1, source_target_pairs={{0,1},{1,0},{2,3},{3,2},{4,5},{5,4},{6,7},{7,6},{8,9},{9,8},{10,11... | collective-permute-start | bytes 2359304 | tf_op jit(solution)/shard_map/ppermute | solution.py:759
  138.6 35.1 %collective-permute-start.24 = (bf16[4,24,3072]{2,1,0:T(8,128)(2,1)}, bf16[4,24,3072]{2,1,0:T(8,128)(2,1)}, u32[]{:S(2)}, u32[]{:S(2)}) collective-permute-start(bf16[4,24,3072]{2,1,0:T(8,128)(2,1)} %get-tuple-element.135), channel_id=1, source_target_pairs={{0,1},{1,0},{2,3},{3,2},{4,5},{5,4},{6,7},{7,6},{8,9},{9,8},{10,11... | collective-permute-start | bytes 1769480 | tf_op jit(solution)/shard_map/ppermute | solution.py:759
  139.1 34.6 %collective-permute-start.25 = (bf16[4,24,3072]{2,1,0:T(8,128)(2,1)}, bf16[4,24,3072]{2,1,0:T(8,128)(2,1)}, u32[]{:S(2)}, u32[]{:S(2)}) collective-permute-start(bf16[4,24,3072]{2,1,0:T(8,128)(2,1)} %get-tuple-element.134), channel_id=1, source_target_pairs={{0,4},{1,5},{2,6},{3,7},{4,0},{5,1},{6,2},{7,3},{8,12},{9,13},{10,... | collective-permute-start | bytes 1769480 | tf_op jit(solution)/shard_map/ppermute | solution.py:759
  139.6 36.3 %collective-permute-start.26 = (bf16[4,24,3072]{2,1,0:T(8,128)(2,1)}, bf16[4,24,3072]{2,1,0:T(8,128)(2,1)}, u32[]{:S(2)}, u32[]{:S(2)}) collective-permute-start(bf16[4,24,3072]{2,1,0:T(8,128)(2,1)} %get-tuple-element.133), channel_id=1, source_target_pairs={{0,5},{1,4},{2,7},{3,6},{4,1},{5,0},{6,3},{7,2},{8,13},{9,12},{10,... | collective-permute-start | bytes 1769480 | tf_op jit(solution)/shard_map/ppermute | solution.py:759
  189.4 10.7 %collective-permute-start.30 = (bf16[4,24,1920]{2,1,0:T(8,128)(2,1)S(1)}, bf16[4,24,1920]{2,1,0:T(8,128)(2,1)S(1)}, u32[]{:S(2)}, u32[]{:S(2)}) collective-permute-start(bf16[4,24,1920]{2,1,0:T(8,128)(2,1)S(1)} %get-tuple-element.147), channel_id=1, source_target_pairs={{0,4},{1,5},{2,6},{3,7},{4,0},{5,1},{6,2},{7,3},{8,12},{9,13},{10,... | collective-permute-start | bytes 1105928 | tf_op jit(solution)/shard_map/ppermute | solution.py:759
  191.0 20.7 %collective-permute-start.29 = (bf16[4,24,1920]{2,1,0:T(8,128)(2,1)S(1)}, bf16[4,24,1920]{2,1,0:T(8,128)(2,1)S(1)}, u32[]{:S(2)}, u32[]{:S(2)}) collective-permute-start(bf16[4,24,1920]{2,1,0:T(8,128)(2,1)S(1)} %get-tuple-element.145), channel_id=1, source_target_pairs={{0,1},{1,0},{2,3},{3,2},{4,5},{5,4},{6,7},{7,6},{8,9},{9,8},{10,11... | collective-permute-start | bytes 1105928 | tf_op jit(solution)/shard_map/ppermute | solution.py:759
  191.5 20.2 %collective-permute-start.31 = (bf16[4,24,1920]{2,1,0:T(8,128)(2,1)S(1)}, bf16[4,24,1920]{2,1,0:T(8,128)(2,1)S(1)}, u32[]{:S(2)}, u32[]{:S(2)}) collective-permute-start(bf16[4,24,1920]{2,1,0:T(8,128)(2,1)S(1)} %get-tuple-element.146), channel_id=1, source_target_pairs={{0,5},{1,4},{2,7},{3,6},{4,1},{5,0},{6,3},{7,2},{8,13},{9,12},{10,... | collective-permute-start | bytes 1105928 | tf_op jit(solution)/shard_map/ppermute | solution.py:759
  201.9 20.4 %collective-permute-start.34 = (bf16[24,3072]{1,0:T(8,128)(2,1)S(1)}, bf16[24,3072]{1,0:T(8,128)(2,1)S(1)}, u32[]{:S(2)}, u32[]{:S(2)}) collective-permute-start(bf16[24,3072]{1,0:T(8,128)(2,1)S(1)} %get-tuple-element.152), channel_id=1, source_target_pairs={{0,8},{1,9},{2,10},{3,11},{4,12},{5,13},{6,14},{7,15},{8,16},{9,17... | collective-permute-start | bytes 442376 | tf_op jit(solution)/shard_map/ppermute | solution.py:759
  202.3 20.6 %collective-permute-start.35 = (bf16[24,3072]{1,0:T(8,128)(2,1)S(1)}, bf16[24,3072]{1,0:T(8,128)(2,1)S(1)}, u32[]{:S(2)}, u32[]{:S(2)}) collective-permute-start(bf16[24,3072]{1,0:T(8,128)(2,1)S(1)} %get-tuple-element.154), channel_id=1, source_target_pairs={{0,16},{1,17},{2,18},{3,19},{4,20},{5,21},{6,22},{7,23},{8,24},{9,... | collective-permute-start | bytes 442376 | tf_op jit(solution)/shard_map/ppermute | solution.py:759
  205.7 17.3 %collective-permute-start.36 = (bf16[24,3072]{1,0:T(8,128)(2,1)S(1)}, bf16[24,3072]{1,0:T(8,128)(2,1)S(1)}, u32[]{:S(2)}, u32[]{:S(2)}) collective-permute-start(bf16[24,3072]{1,0:T(8,128)(2,1)S(1)} %get-tuple-element.153), channel_id=1, source_target_pairs={{0,24},{1,25},{2,26},{3,27},{4,28},{5,29},{6,30},{7,31},{8,0},{9,1... | collective-permute-start | bytes 442376 | tf_op jit(solution)/shard_map/ppermute | solution.py:759
  211.9 4.6 %collective-permute-start.32 = (bf16[24,1920]{1,0:T(8,128)(2,1)S(1)}, bf16[24,1920]{1,0:T(8,128)(2,1)S(1)}, u32[]{:S(2)}, u32[]{:S(2)}) collective-permute-start(bf16[24,1920]{1,0:T(8,128)(2,1)S(1)} %get-tuple-element.158), channel_id=1, source_target_pairs={{0,8},{1,9},{2,10},{3,11},{4,12},{5,13},{6,14},{7,15},{8,16},{9,17... | collective-permute-start | bytes 276488 | tf_op jit(solution)/shard_map/ppermute | solution.py:759
  214.0 17.7 %collective-permute-start.33 = (bf16[512,768]{1,0:T(8,128)(2,1)S(1)}, bf16[512,768]{1,0:T(8,128)(2,1)S(1)}, u32[]{:S(2)}, u32[]{:S(2)}) collective-permute-start(bf16[512,768]{1,0:T(8,128)(2,1)S(1)} %dynamic-slice_bitcast_fusion.3), channel_id=1, source_target_pairs={{0,1},{1,0},{2,3},{3,2},{4,5},{5,4},{6,7},{7,6},{8,9},{9,8},{10,11... | collective-permute-start | bytes 2359304 | tf_op jit(solution)/shard_map/ppermute | solution.py:759
  216.5 7.2 %collective-permute-start.37 = (bf16[24,1920]{1,0:T(8,128)(2,1)S(1)}, bf16[24,1920]{1,0:T(8,128)(2,1)S(1)}, u32[]{:S(2)}, u32[]{:S(2)}) collective-permute-start(bf16[24,1920]{1,0:T(8,128)(2,1)S(1)} %get-tuple-element.156), channel_id=1, source_target_pairs={{0,16},{1,17},{2,18},{3,19},{4,20},{5,21},{6,22},{7,23},{8,24},{9,... | collective-permute-start | bytes 276488 | tf_op jit(solution)/shard_map/ppermute | solution.py:759
  (40 other events, 356.6 us)
